TPU v7x, 32 devices: a whole 2x2x4 slice. The times are simulated.
32 devices in a mesh: seq: 4 (over y, core), exp: 8 (over z, x).
Axes of the slice: x: 2, y: 2, z: 4, core: 2. Of those that a mesh axis runs over, the one named last changes fastest.
Arguments:
- tokens: bfloat16 [4096, 1280], P(('seq', 'exp')), may hold values from -64 to 64
- slot_keys: bfloat16 [1280, 8], P(None, 'exp'), may hold values from -3 to 3
- w_in: bfloat16 [8, 5120, 1280], P('exp', 'seq'), may hold values from -0.15625 to 0.15625
- w_out: bfloat16 [8, 5120, 1280], P('exp', 'seq'), may hold values from -0.078125 to 0.078125
- cotangent: bfloat16 [4096, 1280], P(('seq', 'exp')), may hold values from -6 to 6
Outputs:
- layer_out: bfloat16 [4096, 1280], P(('seq', 'exp'))
- tokens_grad: bfloat16 [4096, 1280], P(('seq', 'exp'))
- keys_grad: float32 [1280, 8], P(None, 'exp')
- w_in_grad: bfloat16 [8, 5120, 1280], P('exp', 'seq')
- w_out_grad: bfloat16 [8, 5120, 1280], P('exp', 'seq')
All inputs are finite; a program needn't handle non-finite values.
Results may differ from a plain program's by a relative error of at most 0.03.
Values may be sent and summed in bfloat16 or wider, within the bound.
No kernel may reach another device: no remote copies, remote signals or barrier semaphores. Data moves between devices by JAX's collectives and lax.ppermute only.
A program may use at most 64 MiB of HBM per device.

v0:
```python
import jax
import jax.numpy as jnp
from jax import lax
from jax.sharding import PartitionSpec as P

tanh_coeff = 0.7978845608028654
cubic_coeff = 0.044715


def merged(part, axis, combine):
    gathered = jax.tree.map(lambda a: lax.all_gather(a, axis), part)

    def take(source):
        return jax.tree.map(lambda a: lax.dynamic_index_in_dim(a, source, 0, False), gathered)

    return lax.fori_loop(
        1, lax.axis_size(axis), lambda source, state: combine(state, take(source)), take(0)
    )


def gelu_value(values):
    return (
        0.5
        * values
        * (1.0 + jnp.tanh(tanh_coeff * (values + cubic_coeff * values * values * values)))
    )


def gelu_slope(values):
    tanh_part = jnp.tanh(tanh_coeff * (values + cubic_coeff * values * values * values))
    return 0.5 * (1.0 + tanh_part) + 0.5 * values * (1.0 - tanh_part * tanh_part) * tanh_coeff * (
        1.0 + 3.0 * cubic_coeff * values * values
    )


def join_stats(earlier, later):
    top_score = jnp.maximum(earlier[0], later[0])
    summed = earlier[1] * jnp.exp(earlier[0] - top_score) + later[1] * jnp.exp(later[0] - top_score)
    return (top_score, summed)


def rows_of(weights, row_data):

    def make_rows(first_row, row_count):
        return jnp.dot(weights, row_data, preferred_element_type=jnp.float32)

    return make_rows


def to_owners(make_rows, local_experts, total_rows):
    summed_all = lax.psum(make_rows(0, total_rows), ("seq", "exp"))
    result = lax.dynamic_slice_in_dim(
        summed_all, lax.axis_index("exp") * local_experts, local_experts, 0
    )
    return result


def to_tokens(partial_value):
    summed = lax.psum(partial_value, "seq")
    return lax.all_gather(summed.astype(jnp.bfloat16), "exp", axis=0, tiled=True)


def local(tokens, slot_keys, w_in, w_out, cotangent):
    local_experts = w_in.shape[0]
    keys_all = lax.all_gather(slot_keys, "exp", axis=1, tiled=True)
    total_rows = keys_all.shape[1]
    logits = lax.dot_general(
        keys_all, tokens, (((0,), (1,)), ((), ())), preferred_element_type=jnp.float32
    )
    local_peak = jnp.max(logits, axis=1)
    local_total = jnp.sum(jnp.exp(logits - local_peak[:, None]), axis=1)
    slot_peak, slot_total = merged((local_peak, local_total), ("seq", "exp"), join_stats)
    exp_terms = jnp.exp(logits - slot_peak[:, None])
    disp_prob = exp_terms / slot_total[:, None]
    dispatch = disp_prob.astype(jnp.bfloat16)
    row_peak = jnp.max(logits, axis=0, keepdims=True)
    row_terms = jnp.exp(logits - row_peak)
    comb_prob = row_terms / jnp.sum(row_terms, axis=0, keepdims=True)
    combine = comb_prob.astype(jnp.bfloat16)
    slot_in = to_owners(rows_of(dispatch, tokens), local_experts, total_rows).astype(jnp.bfloat16)
    pre_act = jnp.einsum("efd,ed->ef", w_in, slot_in, preferred_element_type=jnp.float32)
    activation = gelu_value(pre_act).astype(jnp.bfloat16)
    slot_out = to_tokens(
        jnp.einsum("ef,efd->ed", activation, w_out, preferred_element_type=jnp.float32)
    )
    layer_out = lax.dot_general(
        combine, slot_out, (((0,), (0,)), ((), ())), preferred_element_type=jnp.float32
    ).astype(jnp.bfloat16)
    comb_grad = lax.dot_general(
        slot_out, cotangent, (((1,), (1,)), ((), ())), preferred_element_type=jnp.float32
    )
    slot_out_grad = to_owners(rows_of(combine, cotangent), local_experts, total_rows).astype(
        jnp.bfloat16
    )
    act_grad = jnp.einsum("efd,ed->ef", w_out, slot_out_grad, preferred_element_type=jnp.float32)
    w_out_grad = (
        activation.astype(jnp.float32)[:, :, None] * slot_out_grad.astype(jnp.float32)[:, None, :]
    ).astype(jnp.bfloat16)
    pre_grad = (act_grad * gelu_slope(pre_act)).astype(jnp.bfloat16)
    w_in_grad = (
        pre_grad.astype(jnp.float32)[:, :, None] * slot_in.astype(jnp.float32)[:, None, :]
    ).astype(jnp.bfloat16)
    slot_in_grad = to_tokens(
        jnp.einsum("ef,efd->ed", pre_grad, w_in, preferred_element_type=jnp.float32)
    )
    disp_grad = lax.dot_general(
        slot_in_grad, tokens, (((1,), (1,)), ((), ())), preferred_element_type=jnp.float32
    )
    correction = lax.psum(jnp.sum(disp_prob * disp_grad, axis=1), ("seq", "exp"))
    comb_mean = jnp.sum(comb_prob * comb_grad, axis=0, keepdims=True)
    logit_grad = (
        comb_prob * (comb_grad - comb_mean) + disp_prob * (disp_grad - correction[:, None])
    ).astype(jnp.bfloat16)
    tokens_grad = (
        lax.dot_general(
            dispatch, slot_in_grad, (((0,), (0,)), ((), ())), preferred_element_type=jnp.float32
        )
        + lax.dot_general(
            logit_grad, keys_all, (((0,), (1,)), ((), ())), preferred_element_type=jnp.float32
        )
    ).astype(jnp.bfloat16)
    keys_rows = to_owners(rows_of(logit_grad, tokens), local_experts, total_rows)
    keys_grad = keys_rows.T
    return (layer_out, tokens_grad, keys_grad, w_in_grad, w_out_grad)


def solution(mesh):
    return jax.shard_map(
        local,
        mesh=mesh,
        in_specs=(
            P(("seq", "exp"), None),
            P(None, "exp"),
            P("exp", "seq", None),
            P("exp", "seq", None),
            P(("seq", "exp"), None),
        ),
        out_specs=(
            P(("seq", "exp"), None),
            P(("seq", "exp"), None),
            P(None, "exp"),
            P("exp", "seq", None),
            P("exp", "seq", None),
        ),
        check_vma=False,
    )
```

profile of v0, /device:TPU:0, one launch (start us, length us, event | category | flops | bytes accessed | tf_op | source)
XLA Modules:
  0.0 287.9 jit_solution(15633100063959277876)
XLA Ops:
  0.6 0.0 copy-start
  0.7 32.7 %all-gather.2 = bf16[8,1,1280]{2,1,0:T(2,128)(2,1)S(1)} all-gather(bf16[1,1,1280]{2,1,0:T(2,128)(2,1)} %bitcast.70), channel_id=1, replica_groups=mesh['seq'=4,'exp'=8] {'exp'}, dimensions={0}, use_global_device_ids=true | all-gather | bytes 23040 | tf_op jit(solution)/shard_map/all_gather | solution.py:65
  33.4 1.3 fusion.58
  34.7 0.2 dynamic-update-slice
  34.9 0.2 fusion.45
  35.1 0.2 dynamic-update-slice.1
  35.4 39.4 %all-reduce.3 = (f32[256]{0:T(256)S(1)}, f32[256]{0:T(256)S(1)}) all-reduce(f32[256]{0:T(256)S(1)} %dynamic-update-slice, f32[256]{0:T(256)S(1)} %dynamic-update-slice.1), channel_id=2, replica_groups=mesh['seq'=4,'exp'=8] {'seq','exp'}, use_global_device_ids=true, to_apply=%add | all-reduce | flops 512 | bytes 4096
  74.7 0.1 reshape.182
  74.8 0.1 reshape.181
  74.9 1.4 while.17
  76.3 1.2 fusion.49
  77.5 1.1 fusion.51
  78.6 41.8 %all-reduce.2 = (bf16[8,1280]{1,0:T(8,128)(2,1)S(1)}, bf16[8,1280]{1,0:T(8,128)(2,1)S(1)}) all-reduce(f32[8,1280]{1,0:T(8,128)S(1)} %fusion.49, f32[8,1280]{1,0:T(8,128)S(1)} %fusion.51), channel_id=1, replica_groups=mesh['seq'=4,'exp'=8] {'seq','exp'}, use_global_device_ids=true, to_apply=%region_6.7 | all-reduce | flops 20480 | bytes 122880 | tf_op jit(solution)/shard_map/psum | solution.py:51
  120.4 0.0 copy-start.1
  120.4 0.0 copy-done
  120.5 1.0 fusion.11
  121.5 0.1 convert_reduce_fusion
  121.5 0.9 copy-done.1
  122.4 1.0 fusion.14
  123.4 0.5 fusion.6
  124.0 0.6 fusion.4
  124.5 11.7 %all-reduce.4 = (bf16[1,1280]{1,0:T(2,128)(2,1)S(1)}, bf16[1,1280]{1,0:T(2,128)(2,1)S(1)}) all-reduce(f32[1,1280]{1,0:T(1,128)S(1)} %fusion.4, f32[1,1280]{1,0:T(1,128)S(1)} %fusion.6), channel_id=1, replica_groups=mesh['seq'=4,'exp'=8] {'seq'}, use_global_device_ids=true, to_apply=%region_7.8 | all-reduce | flops 2560 | bytes 15360 | tf_op jit(solution)/shard_map/psum | solution.py:59
  136.2 30.6 %all-gather.4 = bf16[8,1,1280]{2,1,0:T(2,128)(2,1)S(1)} all-gather(bf16[1,1,1280]{2,1,0:T(2,128)(2,1)S(1)} %bitcast.72), channel_id=1, replica_groups=mesh['seq'=4,'exp'=8] {'exp'}, dimensions={0}, use_global_device_ids=true | all-gather | bytes 23040 | tf_op jit(solution)/shard_map/all_gather | solution.py:60
  166.8 1.1 fusion.17
  167.9 30.6 %all-gather.3 = bf16[8,1,1280]{2,1,0:T(2,128)(2,1)S(1)} all-gather(bf16[1,1,1280]{2,1,0:T(2,128)(2,1)S(1)} %bitcast.71), channel_id=1, replica_groups=mesh['seq'=4,'exp'=8] {'exp'}, dimensions={0}, use_global_device_ids=true | all-gather | bytes 23040 | tf_op jit(solution)/shard_map/all_gather | solution.py:60
  198.5 1.3 multiply_reduce_fusion.1
  199.8 38.5 %psum.46 = f32[8]{0:T(128)S(1)} all-reduce(f32[8]{0:T(128)S(1)} %get-tuple-element.141), channel_id=1, replica_groups=mesh['seq'=4,'exp'=8] {'seq','exp'}, use_global_device_ids=true, to_apply=%region_12.13 | all-reduce | flops 8 | bytes 64 | tf_op jit(solution)/shard_map/psum | solution.py:109
  238.4 1.2 fusion.62
  239.6 41.0 %psum.47 = f32[8,1280]{1,0:T(8,128)S(1)} all-reduce(f32[8,1280]{1,0:T(8,128)S(1)} %fusion.62), channel_id=1, replica_groups=mesh['seq'=4,'exp'=8] {'seq','exp'}, use_global_device_ids=true, to_apply=%region_13.14 | all-reduce | flops 10240 | bytes 81920 | tf_op jit(solution)/shard_map/psum | solution.py:51
  280.6 0.6 dynamic-slice_bitcast_fusion
  281.2 1.0 convolution_convert_fusion
  282.2 0.4 fusion.19
  282.6 1.1 fusion.10
  283.7 2.1 multiply_convert_fusion.1
  285.8 2.1 multiply_convert_fusion
  (40 shorter events, 0.9 us)
Async XLA Ops:
  0.6 119.8 %copy-start = (bf16[1,1280,1280]{2,1,0:T(8,128)(2,1)S(1)}, bf16[1,1280,1280]{2,1,0:T(8,128)(2,1)}, u32[]{:S(2)}) copy-start(bf16[1,1280,1280]{2,1,0:T(8,128)(2,1)} %param.9) | copy-start | bytes 9830404
  120.4 1.9 copy-start.1
where the time goes:
time: 289 us; the launch traced here: 288 us
  blocking collectives  266 us (92%)
  matrix products  12.7 us (4%)
  other arithmetic  5.31 us (2%)
    psum x2, blocking collectives, to_owners(): summed_all = lax.psum(make_rows(0, total_rows), ('seq', 'exp'))  82.8 us
    all_gather x2, blocking collectives, to_tokens(): lax.all_gather(summed.astype(jnp.bfloat16), 'exp', axis=0, tiled=True)  61.2 us
    unnamed x1, blocking collectives  39.4 us
    psum x1, blocking collectives, local(): lax.psum(jnp.sum(disp_prob * disp_grad, axis=1), ('seq', 'exp'))  38.5 us
    all_gather x1, blocking collectives, local(): keys_all = lax.all_gather(slot_keys, 'exp', axis=1, tiled=True)  32.7 us
    psum x1, blocking collectives, to_tokens(): summed = lax.psum(partial_value, 'seq')  11.7 us

commit v1 on v0

v1 whole, which is shorter than its diff:
```python
import jax
import jax.numpy as jnp
from jax import lax
from jax.sharding import PartitionSpec as P

tanh_coeff = 0.7978845608028654
cubic_coeff = 0.044715
LANES = 128


def gelu_parts(values):
    tanh_part = jnp.tanh(tanh_coeff * (values + cubic_coeff * values * values * values))
    value = 0.5 * values * (1.0 + tanh_part)
    slope = 0.5 * (1.0 + tanh_part) + 0.5 * values * (1.0 - tanh_part * tanh_part) * tanh_coeff * (
        1.0 + 3.0 * cubic_coeff * values * values
    )
    return value, slope


def rounded(values):
    return lax.reduce_precision(values, 8, 7)


def three_terms(values):
    first = rounded(values)
    second = rounded(values - first)
    third = rounded(values - first - second)
    return [term.astype(jnp.bfloat16) for term in (first, second, third)]


def dot(left, right, left_dim, right_dim):
    return lax.dot_general(
        left, right, (((left_dim,), (right_dim,)), ((), ())), preferred_element_type=jnp.float32
    )


def local(tokens, slot_keys, w_in, w_out, cotangent):
    both = ("seq", "exp")
    seq_size, exp_size = lax.axis_size("seq"), lax.axis_size("exp")
    devices = seq_size * exp_size
    experts, hidden, width = w_in.shape
    half = width // 2
    own_tokens = tokens.shape[0]
    side = lax.rem(lax.axis_index("seq"), 2)
    swap = [(i, i ^ 1) for i in range(seq_size)]

    tokens_pair = jnp.concatenate([tokens, lax.ppermute(tokens, "seq", swap)], axis=0)
    cotangent_pair = jnp.concatenate([cotangent, lax.ppermute(cotangent, "seq", swap)], axis=0)
    tokens_half = lax.dynamic_slice_in_dim(tokens_pair, side * half, half, 1)
    cotangent_half = lax.dynamic_slice_in_dim(cotangent_pair, side * half, half, 1)

    keys_all = lax.all_to_all(
        jnp.broadcast_to(slot_keys.T[None], (exp_size, experts, width)), "exp", 0, 0, tiled=True
    ).reshape(exp_size * experts, width)
    slots = exp_size * experts

    logits = dot(keys_all, tokens_pair, 1, 1)
    peak = jnp.max(logits, axis=1, keepdims=True)
    terms = jnp.exp(logits - peak)
    total = jnp.sum(terms, axis=1, keepdims=True)
    terms_high = rounded(terms)
    terms_low = terms - terms_high
    row_terms = jnp.exp(logits - jnp.max(logits, axis=0, keepdims=True))
    comb_prob = row_terms / jnp.sum(row_terms, axis=0, keepdims=True)
    combine = comb_prob.astype(jnp.bfloat16)
    sums = dot(
        jnp.concatenate([terms_high, terms_low], axis=0).astype(jnp.bfloat16), tokens_half, 1, 0
    )
    slot_sums = sums[:slots] + sums[slots:]
    grad_sums = dot(combine, cotangent_half, 1, 0)

    message = jnp.concatenate(
        [
            slot_sums,
            grad_sums,
            jnp.broadcast_to(peak, (slots, LANES // 2)),
            jnp.broadcast_to(total, (slots, LANES // 2)),
        ],
        axis=1,
    )
    parts = lax.all_to_all(
        jnp.broadcast_to(
            message.reshape(1, exp_size, experts, -1), (seq_size, exp_size, experts, message.shape[1])
        ).reshape(devices, experts, -1),
        both,
        0,
        0,
        tiled=True,
    ).reshape(seq_size // 2, 2, exp_size, experts, -1)
    peaks = parts[..., 2 * half]
    totals = parts[..., 2 * half + LANES // 2]
    slot_peak = jnp.max(peaks, axis=(0, 1, 2))
    scale = jnp.exp(peaks - slot_peak)
    slot_total = jnp.sum(totals[:, 0] * scale[:, 0], axis=(0, 1))
    slot_rows = jnp.sum(parts[..., :half] * scale[..., None], axis=(0, 2)) / slot_total[:, None]
    slot_rows = jnp.moveaxis(slot_rows, 0, 1).reshape(experts, width)
    slot_in = slot_rows.astype(jnp.bfloat16)
    slot_out_grad = jnp.sum(parts[..., half : 2 * half], axis=(0, 2))
    slot_out_grad = jnp.moveaxis(slot_out_grad, 0, 1).reshape(experts, width).astype(jnp.bfloat16)

    pre_act = jnp.einsum("efd,ed->ef", w_in, slot_in, preferred_element_type=jnp.float32)
    act_grad = jnp.einsum("efd,ed->ef", w_out, slot_out_grad, preferred_element_type=jnp.float32)
    value, slope = gelu_parts(pre_act)
    activation = value.astype(jnp.bfloat16)
    pre_grad = (act_grad * slope).astype(jnp.bfloat16)
    out_part = jnp.einsum("ef,efd->ed", activation, w_out, preferred_element_type=jnp.float32)
    grad_part = rounded(
        jnp.einsum("ef,efd->ed", pre_grad, w_in, preferred_element_type=jnp.float32)
    )
    corr_part = jnp.sum(slot_rows * grad_part, axis=1)

    scalars = three_terms(slot_peak) + three_terms(slot_total) + three_terms(corr_part)
    scalars = jnp.stack(scalars, axis=1)
    scalars = jnp.pad(scalars, ((0, 0), (0, LANES - scalars.shape[1])))
    rows = jnp.stack(
        [
            jnp.concatenate([out_part.astype(jnp.bfloat16), scalars], axis=1),
            jnp.concatenate([grad_part.astype(jnp.bfloat16), scalars], axis=1),
        ],
        axis=1,
    )
    gathered = lax.all_to_all(
        jnp.broadcast_to(rows[None], (devices,) + rows.shape), both, 0, 0, tiled=True
    )
    gathered = gathered.reshape((seq_size, slots) + rows.shape[1:])
    out_rows = gathered[:, :, 0, :width].reshape(seq_size * slots, width)
    grad_rows = gathered[:, :, 1, :width].reshape(seq_size * slots, width)
    extra = gathered[:, :, 0, width : width + 9].astype(jnp.float32).reshape(seq_size, slots, 3, 3)
    extra = jnp.sum(extra, axis=3)
    peak_all, total_all = extra[0, :, 0, None], extra[0, :, 1, None]
    correction = jnp.sum(extra[:, :, 2], axis=0)[:, None]

    comb_grad = jnp.sum(
        dot(out_rows, cotangent_pair, 1, 1).reshape(seq_size, slots, -1), axis=0
    )
    disp_grad = jnp.sum(dot(grad_rows, tokens_pair, 1, 1).reshape(seq_size, slots, -1), axis=0)
    disp_prob = jnp.exp(logits - peak_all) / total_all
    comb_mean = jnp.sum(comb_prob * comb_grad, axis=0, keepdims=True)
    logit_grad = (
        comb_prob * (comb_grad - comb_mean) + disp_prob * (disp_grad - correction)
    ).astype(jnp.bfloat16)

    keys_part = dot(logit_grad, tokens_half, 1, 0)
    keys_parts = lax.all_to_all(
        jnp.broadcast_to(
            keys_part.reshape(1, exp_size, experts, half), (seq_size, exp_size, experts, half)
        ).reshape(devices, experts, half),
        both,
        0,
        0,
        tiled=True,
    ).reshape(seq_size // 2, 2, exp_size, experts, half)
    keys_rows = jnp.moveaxis(jnp.sum(keys_parts, axis=(0, 2)), 0, 1).reshape(experts, width)
    keys_grad = keys_rows.T

    def tiled_rows(values):
        return jnp.tile(values, (seq_size, 1))

    layer_out = dot(tiled_rows(combine[:, :own_tokens]), out_rows, 0, 0).astype(jnp.bfloat16)
    dispatch = disp_prob[:, :own_tokens].astype(jnp.bfloat16)
    tokens_grad = (
        dot(tiled_rows(dispatch), grad_rows, 0, 0) + dot(logit_grad[:, :own_tokens], keys_all, 0, 0)
    ).astype(jnp.bfloat16)
    w_out_grad = (
        activation.astype(jnp.float32)[:, :, None] * slot_out_grad.astype(jnp.float32)[:, None, :]
    ).astype(jnp.bfloat16)
    w_in_grad = (
        pre_grad.astype(jnp.float32)[:, :, None] * slot_in.astype(jnp.float32)[:, None, :]
    ).astype(jnp.bfloat16)
    return (layer_out, tokens_grad, keys_grad, w_in_grad, w_out_grad)


def solution(mesh):
    return jax.shard_map(
        local,
        mesh=mesh,
        in_specs=(
            P(("seq", "exp"), None),
            P(None, "exp"),
            P("exp", "seq", None),
            P("exp", "seq", None),
            P(("seq", "exp"), None),
        ),
        out_specs=(
            P(("seq", "exp"), None),
            P(("seq", "exp"), None),
            P(None, "exp"),
            P("exp", "seq", None),
            P("exp", "seq", None),
        ),
        check_vma=False,
    )
```

time: 289 us -> 93.9 us (0.32)
  blocking collectives: 266 us -> 0 us
  waiting for transfers between devices: 0 us -> 19.8 us
  starting transfers between devices: 0 us -> 17.6 us
  between operations: 0.82 us -> 17.4 us
  local copies, waits for them, and re-layouts: 2.19 us -> 15.4 us
  other arithmetic: 5.31 us -> 8.81 us
    psum x4 -> x0, blocking collectives: 133 us -> none  [the longest x2 82.8 us: to_owners(): summed_all = lax.psum(make_rows(0, total_rows), ('seq', 'exp'))]
    all_gather x3 -> x0, blocking collectives: 94 us -> none  [the longest x2 61.2 us: to_tokens(): lax.all_gather(summed.astype(jnp.bfloat16), 'exp', axis=0, tiled=True)]
    unnamed x1 -> x0, blocking collectives: 39.4 us -> none
    all_to_all x0 -> x4, waiting for transfers between devices: none -> 19.8 us  [the longest x1 8.05 us: local(): lax.all_to_all(jnp.broadcast_to(message.reshape(1, exp_size, experts, -1)...]
    all_to_all x0 -> x4, starting transfers between devices: none -> 17.1 us  [the longest x1 7.25 us: local(): lax.all_to_all(jnp.broadcast_to(slot_keys.T[None], (exp_size, experts, wi...]
    unnamed x8 -> x17, local copies, waits for them, and re-layouts: 1.36 us -> 5.63 us
    concatenate x0 -> x3, local copies, waits for them, and re-layouts: none -> 3.54 us  [the longest x1 1.74 us: local(): jnp.concatenate([tokens, lax.ppermute(tokens, 'seq', swap)], axis=0)]
    broadcast_in_dim x0 -> x9, local copies, waits for them, and re-layouts: none -> 3.05 us  [the longest x2 0.88 us: local(): jnp.broadcast_to(message.reshape(1, exp_size, experts, -1), (seq_size, ex...]
  transfers between devices with their start and end apart: 0 -> 6, of which waited for: 0 -> 4; matrix products, arithmetic and copies ran while one was open for 0% -> 16% of each run, Pallas kernels for 0% -> 0%
where the time goes in v1:
time: 93.9 us; the launch traced here: 92.9 us
  waiting for transfers between devices  19.8 us (21%)
  starting transfers between devices  17.6 us (19%)
  between operations  17.4 us (19%)
  local copies, waits for them, and re-layouts  15.4 us (16%)
  matrix products  13.8 us (15%)
  other arithmetic  8.81 us (9%)
    dot_general x9, matrix products, dot(): lax.dot_general(left, right, (((left_dim,), (right_dim,)), ((), ())), pre...  10.8 us
    all_to_all x1, waiting for transfers between devices, local(): lax.all_to_all(jnp.broadcast_to(message.reshape(1, exp_size, experts, -1)...  8.05 us
    all_to_all x1, starting transfers between devices, local(): lax.all_to_all(jnp.broadcast_to(slot_keys.T[None], (exp_size, experts, wi...  7.25 us
    unnamed x17, local copies, waits for them, and re-layouts  5.63 us
    all_to_all x1, waiting for transfers between devices, local(): lax.all_to_all(jnp.broadcast_to(rows[None], (devices,) + rows.shape), bot...  4.76 us
    all_to_all x1, waiting for transfers between devices, local(): lax.all_to_all(jnp.broadcast_to(keys_part.reshape(1, exp_size, experts, h...  4.33 us
    all_to_all x1, starting transfers between devices, local(): lax.all_to_all(jnp.broadcast_to(message.reshape(1, exp_size, experts, -1)...  3.38 us
    all_to_all x1, starting transfers between devices, local(): lax.all_to_all(jnp.broadcast_to(rows[None], (devices,) + rows.shape), bot...  3.31 us
  transfers between devices with their start and end apart: 6, of which 4 were waited for; matrix products, arithmetic and copies ran while one was open for 16% of the time, Pallas kernels for 0%

profile of v1, /device:TPU:0, one launch (start us, length us, event | category | flops | bytes accessed | tf_op | source)
XLA Modules:
  0.0 92.9 jit_solution(7136168008375981192)
XLA Ops:
  0.6 0.9 reduce.14
  1.5 0.5 broadcast.213
  2.1 0.8 reduce.28
  2.8 0.6 reshape.371
  3.4 7.3 %all-to-all-start = ((bf16[8,2,640]{2,1,0:T(2,128)(2,1)}), bf16[8,2,640]{2,1,0:T(2,128)(2,1)S(1)}, u32[]{:S(2)}, u32[]{:S(2)}) async-start(bf16[8,2,640]{2,1,0:T(2,128)(2,1)} %reshape.371), calls=%async_computation | async-start | bytes 40960 | tf_op jit(solution)/shard_map/all_to_all | solution.py:52
  10.7 0.5 collective-permute-start.1
  11.2 1.7 %constant_dynamic-update-slice_fusion.1 = bf16[256,1280]{1,0:T(8,128)(2,1)} fusion(bf16[128,1280]{1,0:T(8,128)(2,1)} %param.5), kind=kLoop, calls=%fused_computation.49 | loop fusion | bytes 655360
  12.9 1.7 %constant_dynamic-update-slice_fusion.3 = bf16[256,1280]{1,0:T(8,128)(2,1)} fusion(bf16[128,1280]{1,0:T(8,128)(2,1)} %param.9), kind=kLoop, calls=%fused_computation.51 | loop fusion | bytes 655360
  14.6 2.7 %all-to-all-done = bf16[8,2,640]{2,1,0:T(2,128)(2,1)S(1)} async-done(((bf16[8,2,640]{2,1,0:T(2,128)(2,1)}), bf16[8,2,640]{2,1,0:T(2,128)(2,1)S(1)}, u32[]{:S(2)}, u32[]{:S(2)}) %all-to-all-start) | async-done | bytes 20512 | tf_op jit(solution)/shard_map/all_to_all | solution.py:52
  17.3 1.7 %constant_dynamic-update-slice_fusion = bf16[256,1280]{1,0:T(8,128)(2,1)} fusion(bf16[256,1280]{1,0:T(8,128)(2,1)} %constant_dynamic-update-slice_fusion.1, bf16[128,1280]{1,0:T(8,128)(2,1)} %collective-permute-done), kind=kLoop, calls=%fused_computation.48 | loop fusion | bytes 655360 | tf_op jit(solution)/shard_map/concatenate | solution.py:47
  19.1 1.5 %fusion.61 = (f32[256]{0:T(256)S(1)}, f32[8]{0:T(128)S(1)}, f32[256,8]{0,1:T(8,128)S(1)}) fusion(bf16[256,1280]{1,0:T(8,128)(2,1)} %constant_dynamic-update-slice_fusion, bf16[8,1,1280]{2,1,0:T(2,128)(2,1)S(1)} %reshape.372), kind=kOutput, calls=%fused_computation.100 | convolution fusion | flops 5246712 | bytes 685088 | tf_op jit(solution)/shard_map/dot_general | solution.py:32
  20.6 0.1 reduce-precision_convert_fusion
  20.7 0.2 fusion.52
  20.9 1.1 %fusion.28 = f32[16,640]{1,0:T(8,128)S(1)} fusion(bf16[256,1280]{1,0:T(8,128)(2,1)} %constant_dynamic-update-slice_fusion, s32[]{:T(128)S(6)} %select_n.4, bf16[8,256]{1,0:T(8,128)(2,1)S(1)} %get-tuple-element.22, bf16[8,256]{1,0:T(8,128)(2,1)S(1)} %get-tuple-element.21), kind=kOutput, calls=%fused_computation.27 | convolution fusion | flops 5259264 | bytes 376836 | tf_op jit(solution)/shard_map/dot_general | solution.py:32
  22.1 1.7 %constant_dynamic-update-slice_fusion.2 = bf16[256,1280]{1,0:T(8,128)(2,1)} fusion(bf16[256,1280]{1,0:T(8,128)(2,1)} %constant_dynamic-update-slice_fusion.3, bf16[128,1280]{1,0:T(8,128)(2,1)} %collective-permute-done.1), kind=kLoop, calls=%fused_computation.50 | loop fusion | bytes 655360 | tf_op jit(solution)/shard_map/concatenate | solution.py:48
  23.8 1.1 %fusion.24 = f32[8,640]{1,0:T(8,128)S(1)} fusion(bf16[8,256]{1,0:T(8,128)(2,1)S(1)} %bitcast_convert_fusion, bf16[256,1280]{1,0:T(8,128)(2,1)} %constant_dynamic-update-slice_fusion.2, s32[]{:T(128)S(6)} %select_n.4), kind=kOutput, calls=%fused_computation.23 | convolution fusion | flops 2621440 | bytes 352260 | tf_op jit(solution)/shard_map/dot_general | solution.py:32
  25.2 0.9 copy.13
  26.0 3.4 %all-to-all-start.1 = ((f32[32,1,1408]{2,1,0:T(1,128)}), f32[32,1,1408]{2,1,0:T(1,128)S(1)}, u32[]{:S(2)}, u32[]{:S(2)}) async-start(f32[32,1,1408]{2,1,0:T(1,128)} %copy.13), calls=%async_computation.1 | async-start | bytes 360448 | tf_op jit(solution)/shard_map/all_to_all | solution.py:81
  29.4 8.1 %all-to-all-done.1 = f32[32,1,1408]{2,1,0:T(1,128)S(1)} async-done(((f32[32,1,1408]{2,1,0:T(1,128)}), f32[32,1,1408]{2,1,0:T(1,128)S(1)}, u32[]{:S(2)}, u32[]{:S(2)}) %all-to-all-start.1) | async-done | bytes 180256 | tf_op jit(solution)/shard_map/all_to_all | solution.py:81
  37.5 0.6 slice_reduce_fusion.2
  43.0 0.8 slice_reduce_fusion.1
  43.8 0.1 fusion.30
  43.9 0.6 fusion.56
  49.5 0.7 convert_bitcast_fusion
  50.3 1.0 %fusion.10 = f32[1280]{0:T(1024)S(1)} fusion(bf16[1280,1]{0,1:T(2,128)(2,1)S(1)} %bitcast.124, bf16[1,1280,1280]{2,1,0:T(8,128)(2,1)S(1)} %copy-done), kind=kOutput, calls=%fused_computation.17 | convolution fusion | flops 3276800 | bytes 3284480 | tf_op jit(solution)/shard_map/efd,ed->ef/dot_general | solution.py:101
  51.3 0.9 copy-done.1
  52.2 1.0 %fusion.19 = f32[1280]{0:T(1024)S(1)} fusion(bf16[1280,1]{0,1:T(2,128)(2,1)S(1)} %bitcast.125, bf16[1,1280,1280]{2,1,0:T(8,128)(2,1)S(1)} %copy-done.1), kind=kOutput, calls=%fused_computation.20 | convolution fusion | flops 3276800 | bytes 3284480 | tf_op jit(solution)/shard_map/efd,ed->ef/dot_general | solution.py:102
  53.2 0.5 fusion.13
  53.8 0.6 convert_convert_fusion
  60.3 0.6 fusion.16
  61.5 2.0 %stack.48 = bf16[1,9]{1,0:T(2,128)(2,1)S(1)} concatenate(bf16[1,1]{1,0:T(2,128)(2,1)} %bitcast.6, bf16[1,1]{1,0:T(2,128)(2,1)} %bitcast.7, bf16[1,1]{1,0:T(2,128)(2,1)} %bitcast.8, bf16[1,1]{1,0:T(2,128)(2,1)} %bitcast.10, bf16[1,1]{1,0:T(2,128)(2,1)} %bitcast.11, bf16[1,1]{1,0:T(2,128)(2,1)} %bitcast.12, bf16[1,1]{1,0:T(2,128)(2,1)} %bitcast.14, bf16[1,1]{1,0:T(2,128)(2,1)} %bitcast.15, ...), dimensions={1} | concatenate | bytes 36 | tf_op jit(solution)/shard_map/stack | solution.py:113
  63.6 0.8 broadcast_in_dim.27
  64.4 3.3 %all-to-all-start.2 = ((bf16[32,1,2,1408]{3,2,1,0:T(2,128)(2,1)}), bf16[32,1,2,1408]{3,2,1,0:T(2,128)(2,1)}, u32[]{:S(2)}, u32[]{:S(2)}) async-start(bf16[32,1,2,1408]{3,2,1,0:T(2,128)(2,1)} %broadcast_in_dim.27), calls=%async_computation.2 | async-start | bytes 360448 | tf_op jit(solution)/shard_map/all_to_all | solution.py:122
  67.7 3.3 %multiply_convert_fusion = (bf16[1,1280,1280]{2,1,0:T(8,128)(2,1)}, bf16[1,1280,1280]{2,1,0:T(8,128)(2,1)}) fusion(f32[1280]{0:T(1024)S(1)} %convert_element_type.200, f32[1280]{0:T(1024)S(1)} %get-tuple-element.13, f32[1280]{0:T(1024)S(1)} %get-tuple-element.23, f32[1280]{0:T(1024)S(1)} %get-tuple-element.26), kind=kLoop, calls=%fused_computation | loop fusion | flops 6553600 | bytes 6574080 | tf_op jit(solution)/shard_map/convert_element_type | solution.py:166
  71.0 4.8 %all-to-all-done.2 = bf16[32,1,2,1408]{3,2,1,0:T(2,128)(2,1)} async-done(((bf16[32,1,2,1408]{3,2,1,0:T(2,128)(2,1)}), bf16[32,1,2,1408]{3,2,1,0:T(2,128)(2,1)}, u32[]{:S(2)}, u32[]{:S(2)}) %all-to-all-start.2) | async-done | bytes 180256 | tf_op jit(solution)/shard_map/all_to_all | solution.py:122
  75.7 0.9 %copy.33 = bf16[32,1,2,1408]{3,0,2,1:T(8,128)(2,1)S(1)} copy(bf16[32,1,2,1408]{3,2,1,0:T(2,128)(2,1)} %all-to-all-done.2) | data formatting | bytes 360448 | tf_op jit(solution)/shard_map/all_to_all | solution.py:122
  76.7 1.3 %convolution_reduce_fusion.1 = f32[8,256]{1,0:T(8,128)S(1)} fusion(bf16[256,1280]{1,0:T(8,128)(2,1)} %constant_dynamic-update-slice_fusion.2, bf16[4,8,2,1408]{3,1,0,2:T(8,128)(2,1)S(1)} %bitcast.113), kind=kOutput, calls=%fused_computation.16 | convolution fusion | flops 20977664 | bytes 745472 | tf_op jit(solution)/shard_map/dot_general | solution.py:32
  78.0 1.4 %convolution_reduce_fusion = f32[8,256]{1,0:T(8,128)S(1)} fusion(bf16[256,1280]{1,0:T(8,128)(2,1)} %constant_dynamic-update-slice_fusion, bf16[4,8,2,1408]{3,1,0,2:T(8,128)(2,1)S(1)} %bitcast.114), kind=kOutput, calls=%fused_computation.15 | convolution fusion | flops 20977664 | bytes 745472 | tf_op jit(solution)/shard_map/dot_general | solution.py:32
  79.4 0.2 copy.15
  79.7 0.1 fusion.47
  79.8 1.1 %fusion.26 = f32[8,640]{1,0:T(8,128)S(1)} fusion(bf16[8,256]{1,0:T(8,128)(2,1)S(1)} %get-tuple-element.17, bf16[256,1280]{1,0:T(8,128)(2,1)} %constant_dynamic-update-slice_fusion, s32[]{:T(128)S(6)} %select_n.4), kind=kOutput, calls=%fused_computation.25 | convolution fusion | flops 2621440 | bytes 352260 | tf_op jit(solution)/shard_map/dot_general | solution.py:32
  80.9 0.7 broadcast_in_dim.29
  81.6 3.2 %all-to-all-start.3 = ((f32[32,1,640]{2,1,0:T(1,128)}), f32[32,1,640]{2,1,0:T(1,128)S(1)}, u32[]{:S(2)}, u32[]{:S(2)}) async-start(f32[32,1,640]{2,1,0:T(1,128)} %broadcast_in_dim.29), calls=%async_computation.3 | async-start | bytes 163840 | tf_op jit(solution)/shard_map/all_to_all | solution.py:144
  84.8 0.3 convolution_bitcast_fusion
  85.1 1.8 %fusion.9 = bf16[128,1280]{1,0:T(8,128)(2,1)} fusion(f32[128,1280]{1,0:T(8,128)S(1)} %convolution_bitcast_fusion, bf16[8,1,1280]{2,1,0:T(2,128)(2,1)} %copy-done.2, bf16[8,256]{1,0:T(8,128)(2,1)S(1)} %get-tuple-element.17), kind=kOutput, calls=%fused_computation.14 | convolution fusion | flops 2949120 | bytes 1005568 | tf_op jit(solution)/shard_map/dot_general | solution.py:32
  86.9 1.0 %fusion.8 = bf16[128,1280]{1,0:T(8,128)(2,1)} fusion(bf16[4,8,2,1408]{3,1,0,2:T(8,128)(2,1)S(1)} %bitcast.117, bf16[8,128]{1,0:T(8,128)(2,1)S(1)} %slice-done), kind=kOutput, calls=%fused_computation.13 | convolution fusion | flops 10649600 | bytes 411648 | tf_op jit(solution)/shard_map/dot_general | solution.py:32
  87.9 4.3 %all-to-all-done.3 = f32[32,1,640]{2,1,0:T(1,128)S(1)} async-done(((f32[32,1,640]{2,1,0:T(1,128)}), f32[32,1,640]{2,1,0:T(1,128)S(1)}, u32[]{:S(2)}, u32[]{:S(2)}) %all-to-all-start.3) | async-done | bytes 81952 | tf_op jit(solution)/shard_map/all_to_all | solution.py:144
  92.3 0.6 copy.21
  (42 shorter events, 0.6 us)
Async XLA Ops:
  0.6 49.6 %copy-start = (bf16[1,1280,1280]{2,1,0:T(8,128)(2,1)S(1)}, bf16[1,1280,1280]{2,1,0:T(8,128)(2,1)}, u32[]{:S(2)}) copy-start(bf16[1,1280,1280]{2,1,0:T(8,128)(2,1)} %param.7) | copy-start | bytes 9830404
  3.4 13.9 %all-to-all-start = ((bf16[8,2,640]{2,1,0:T(2,128)(2,1)}), bf16[8,2,640]{2,1,0:T(2,128)(2,1)S(1)}, u32[]{:S(2)}, u32[]{:S(2)}) async-start(bf16[8,2,640]{2,1,0:T(2,128)(2,1)} %reshape.371), calls=%async_computation | async-start | bytes 40960 | tf_op jit(solution)/shard_map/all_to_all | solution.py:52
  10.7 6.6 %collective-permute-start = (bf16[128,1280]{1,0:T(8,128)(2,1)}, bf16[128,1280]{1,0:T(8,128)(2,1)}, u32[]{:S(2)}, u32[]{:S(2)}) collective-permute-start(bf16[128,1280]{1,0:T(8,128)(2,1)} %param.5), channel_id=1, source_target_pairs={{0,8},{8,0},{16,24},{24,16},{1,9},{9,1},{17,25},{25,17},{2,10},{10... | collective-permute-start | bytes 983048 | tf_op jit(solution)/shard_map/ppermute | solution.py:47
  10.7 11.3 %collective-permute-start.1 = (bf16[128,1280]{1,0:T(8,128)(2,1)}, bf16[128,1280]{1,0:T(8,128)(2,1)}, u32[]{:S(2)}, u32[]{:S(2)}) collective-permute-start(bf16[128,1280]{1,0:T(8,128)(2,1)} %param.9), channel_id=1, source_target_pairs={{0,8},{8,0},{16,24},{24,16},{1,9},{9,1},{17,25},{25,17},{2,10},{10... | collective-permute-start | bytes 983048 | tf_op jit(solution)/shard_map/ppermute | solution.py:48
  17.3 7.7 %copy-start.2 = (bf16[8,1,1280]{2,1,0:T(2,128)(2,1)}, bf16[8,1,1280]{2,1,0:T(2,128)(2,1)S(1)}, u32[]{:S(2)}) copy-start(bf16[8,1,1280]{2,1,0:T(2,128)(2,1)S(1)} %reshape.372) | copy-start | bytes 61444
  20.9 32.3 %copy-start.3 = (bf16[8,256]{1,0:T(8,128)(2,1)}, bf16[8,256]{1,0:T(8,128)(2,1)S(1)}, u32[]{:S(2)}) copy-start(bf16[8,256]{1,0:T(8,128)(2,1)S(1)} %bitcast_convert_fusion) | copy-start | bytes 12292
  26.0 11.4 %all-to-all-start.1 = ((f32[32,1,1408]{2,1,0:T(1,128)}), f32[32,1,1408]{2,1,0:T(1,128)S(1)}, u32[]{:S(2)}, u32[]{:S(2)}) async-start(f32[32,1,1408]{2,1,0:T(1,128)} %copy.13), calls=%async_computation.1 | async-start | bytes 360448 | tf_op jit(solution)/shard_map/all_to_all | solution.py:81
  50.3 1.9 %copy-start.1 = (bf16[1,1280,1280]{2,1,0:T(8,128)(2,1)S(1)}, bf16[1,1280,1280]{2,1,0:T(8,128)(2,1)}, u32[]{:S(2)}) copy-start(bf16[1,1280,1280]{2,1,0:T(8,128)(2,1)} %param.8) | copy-start | bytes 9830404
  64.4 11.4 %all-to-all-start.2 = ((bf16[32,1,2,1408]{3,2,1,0:T(2,128)(2,1)}), bf16[32,1,2,1408]{3,2,1,0:T(2,128)(2,1)}, u32[]{:S(2)}, u32[]{:S(2)}) async-start(bf16[32,1,2,1408]{3,2,1,0:T(2,128)(2,1)} %broadcast_in_dim.27), calls=%async_computation.2 | async-start | bytes 360448 | tf_op jit(solution)/shard_map/all_to_all | solution.py:122
  71.0 16.0 %slice-start = ((bf16[8,256]{1,0:T(8,128)(2,1)}), bf16[8,128]{1,0:T(8,128)(2,1)S(1)}, s32[]{:S(2)}) async-start(bf16[8,256]{1,0:T(8,128)(2,1)} %copy-done.3), calls=%async_computation.4 | async-start | bytes 4096 | tf_op jit(solution)/shard_map/slice | solution.py:159
  81.6 10.6 %all-to-all-start.3 = ((f32[32,1,640]{2,1,0:T(1,128)}), f32[32,1,640]{2,1,0:T(1,128)S(1)}, u32[]{:S(2)}, u32[]{:S(2)}) async-start(f32[32,1,640]{2,1,0:T(1,128)} %broadcast_in_dim.29), calls=%async_computation.3 | async-start | bytes 163840 | tf_op jit(solution)/shard_map/all_to_all | solution.py:144

commit v2 on v0

v2 whole, which is shorter than its diff:
```python
import functools

import jax
import jax.numpy as jnp
from jax import lax
from jax.experimental import pallas as pl
from jax.experimental.pallas import tpu as pltpu
from jax.sharding import PartitionSpec as P

tanh_coeff = 0.7978845608028654
cubic_coeff = 0.044715
LANES = 128


def dot(left, right, left_dim, right_dim):
    return lax.dot_general(
        left, right, (((left_dim,), (right_dim,)), ((), ())), preferred_element_type=jnp.float32
    )


def gelu_parts(values):
    tanh_part = jnp.tanh(tanh_coeff * (values + cubic_coeff * values * values * values))
    value = 0.5 * values * (1.0 + tanh_part)
    slope = 0.5 * (1.0 + tanh_part) + 0.5 * values * (1.0 - tanh_part * tanh_part) * tanh_coeff * (
        1.0 + 3.0 * cubic_coeff * values * values
    )
    return value, slope


def padded(rows, multiple):
    return -(-rows // multiple) * multiple


def bf16_terms(values, count):
    terms = []
    for _ in range(count):
        term = values.astype(jnp.bfloat16).astype(jnp.float32)
        terms.append(term)
        values = values - term
    return terms


def in_lanes(columns, lane):
    row = jnp.zeros((columns[0].shape[0], LANES), jnp.float32)
    for i, column in enumerate(columns):
        row = jnp.where(lane == i, column, row)
    return row


def from_lanes(row, lane, first, count):
    keep = (lane >= first) & (lane < first + count)
    return jnp.sum(jnp.where(keep, row, 0.0), axis=1, keepdims=True)


def lanes_of(rows):
    return lax.broadcasted_iota(jnp.int32, (rows, LANES), 1)


def call(kernel, out_shape, scratch_shapes, inputs, smem=0):
    return pl.pallas_call(
        kernel,
        out_shape=out_shape,
        in_specs=[pl.BlockSpec(memory_space=pltpu.SMEM)] * smem
        + [pl.BlockSpec(memory_space=pltpu.VMEM)] * (len(inputs) - smem),
        out_specs=jax.tree.map(lambda _: pl.BlockSpec(memory_space=pltpu.VMEM), out_shape),
        scratch_shapes=scratch_shapes,
        compiler_params=pltpu.CompilerParams(vmem_limit_bytes=24 * 1024 * 1024),
    )(*inputs)


def keys_kernel(key_ref, out_ref, rows_ref):
    width = key_ref.shape[1]
    rows_ref[...] = jnp.zeros_like(rows_ref)
    key = key_ref[...].astype(jnp.float32)
    for j in range(width // LANES):
        rows_ref[j : j + 1, :] = key[:, j * LANES : (j + 1) * LANES]
    block = rows_ref[...].astype(jnp.bfloat16)
    for i in range(out_ref.shape[0]):
        out_ref[i] = block


def sums_kernel(
    side_ref, keys_ref, tokens_ref, tokens_other_ref, cotangent_ref, cotangent_other_ref,
    message_ref, logits_ref, comb_ref, keys_all_ref, keys_rows_ref, rows_ref,
):
    slots = keys_ref.shape[0]
    width = tokens_ref.shape[1]
    half = width // 2
    chunks = half // LANES
    first = pl.multiple_of(side_ref[0] * half, LANES)

    keys_rows_ref[...] = keys_ref[...].astype(jnp.float32)
    keys = jnp.concatenate(
        [keys_rows_ref[:, j, :] for j in range(width // LANES)], axis=1
    ).astype(jnp.bfloat16)
    keys_all_ref[...] = keys
    logits = jnp.concatenate(
        [dot(keys, tokens_ref[...], 1, 1), dot(keys, tokens_other_ref[...], 1, 1)], axis=1
    )
    logits_ref[...] = logits
    own = tokens_ref.shape[0]

    row_terms = jnp.exp(logits - jnp.max(logits, axis=0, keepdims=True))
    comb_prob = row_terms / jnp.sum(row_terms, axis=0, keepdims=True)
    comb_ref[...] = comb_prob
    combine = comb_prob.astype(jnp.bfloat16)
    grad_sums = dot(combine[:, :own], cotangent_ref[:, pl.ds(first, half)], 1, 0) + dot(
        combine[:, own:], cotangent_other_ref[:, pl.ds(first, half)], 1, 0
    )

    peak = jnp.max(logits, axis=1, keepdims=True)
    terms = jnp.exp(logits - peak)
    total = jnp.sum(terms, axis=1, keepdims=True)
    parts = jnp.concatenate(bf16_terms(terms, 2), axis=0).astype(jnp.bfloat16)
    sums = dot(parts[:, :own], tokens_ref[:, pl.ds(first, half)], 1, 0) + dot(
        parts[:, own:], tokens_other_ref[:, pl.ds(first, half)], 1, 0
    )
    high, low = bf16_terms(sums[:slots] + sums[slots:], 2)
    for j in range(chunks):
        columns = slice(j * LANES, (j + 1) * LANES)
        rows_ref[:, j, :] = high[:, columns]
        rows_ref[:, chunks + j, :] = low[:, columns]
        rows_ref[:, 2 * chunks + j, :] = grad_sums[:, columns]
    stats = in_lanes(bf16_terms(peak, 3) + bf16_terms(total, 3), lanes_of(slots))
    rows_ref[:, 3 * chunks, :] = stats
    for j in range(3 * chunks + 1, rows_ref.shape[1]):
        rows_ref[:, j, :] = jnp.zeros_like(stats)
    block = rows_ref[...].astype(jnp.bfloat16)
    for q in range(message_ref.shape[0] // slots):
        message_ref[q * slots : (q + 1) * slots] = block


def expert_kernel(
    exp_size, parts_ref, w_in_ref, w_out_ref,
    message_ref, slot_in_ref, slot_out_grad_ref, activation_ref, pre_grad_ref, parts_rows_ref, rows_ref,
):
    devices = parts_ref.shape[0]
    seq_size = devices // exp_size
    width = w_in_ref.shape[1]
    chunks = width // LANES
    per_side = chunks // 2
    parts_rows_ref[...] = parts_ref[...].astype(jnp.float32)
    stats = parts_rows_ref[:, 3 * per_side, :]
    lane = lanes_of(devices)
    peaks = from_lanes(stats, lane, 0, 3)
    totals = from_lanes(stats, lane, 3, 3)
    slot_peak = jnp.max(peaks, axis=0, keepdims=True)
    scale = jnp.exp(peaks - slot_peak)

    def of_side(values, side):
        total = values[side * exp_size : (side + 1) * exp_size]
        for q in range(side + 2, seq_size, 2):
            total = total + values[q * exp_size : (q + 1) * exp_size]
        return jnp.sum(total, axis=0, keepdims=True)

    slot_total = of_side(totals * scale, 0)
    slot_chunks, grad_chunks = [[], []], [[], []]
    for j in range(per_side):
        weighted = (parts_rows_ref[:, j, :] + parts_rows_ref[:, per_side + j, :]) * scale
        grads = parts_rows_ref[:, 2 * per_side + j, :]
        for side in range(2):
            slot_chunks[side].append(of_side(weighted, side))
            grad_chunks[side].append(of_side(grads, side))
    slot_row = jnp.concatenate(slot_chunks[0] + slot_chunks[1], axis=1) / slot_total
    slot_in = slot_row.astype(jnp.bfloat16)
    slot_out_grad = jnp.concatenate(grad_chunks[0] + grad_chunks[1], axis=1).astype(jnp.bfloat16)
    slot_in_ref[...] = slot_in
    slot_out_grad_ref[...] = slot_out_grad

    pre_act = dot(slot_in, w_in_ref[...], 1, 1)
    act_grad = dot(slot_out_grad, w_out_ref[...], 1, 1)
    value, slope = gelu_parts(pre_act)
    activation = value.astype(jnp.bfloat16)
    pre_grad = (act_grad * slope).astype(jnp.bfloat16)
    activation_ref[...] = activation
    pre_grad_ref[...] = pre_grad
    out_part = dot(activation, w_out_ref[...], 1, 0)
    grad_part = dot(pre_grad, w_in_ref[...], 1, 0).astype(jnp.bfloat16).astype(jnp.float32)
    correction = jnp.sum(slot_row * grad_part, axis=1, keepdims=True)
    for j in range(chunks):
        columns = slice(j * LANES, (j + 1) * LANES)
        rows_ref[j : j + 1, :] = out_part[:, columns]
        rows_ref[chunks + j : chunks + j + 1, :] = grad_part[:, columns]
    stats = in_lanes(
        bf16_terms(slot_peak, 3) + bf16_terms(slot_total, 3) + bf16_terms(correction, 3), lanes_of(1)
    )
    rows_ref[2 * chunks : 2 * chunks + 1, :] = stats
    for j in range(2 * chunks + 1, rows_ref.shape[0]):
        rows_ref[j : j + 1, :] = jnp.zeros_like(stats)
    block = rows_ref[...].astype(jnp.bfloat16)
    for i in range(devices):
        message_ref[i] = block


def grads_kernel(
    side_ref, parts_ref, logits_ref, comb_ref, tokens_ref, tokens_other_ref, cotangent_ref, cotangent_other_ref,
    message_ref, slot_out_ref, slot_in_grad_ref, dispatch_ref, logit_grad_ref, parts_rows_ref,
):
    devices = parts_ref.shape[0]
    slots, _ = logits_ref.shape
    seq_size = devices // slots
    own, width = tokens_ref.shape
    half = width // 2
    chunks = width // LANES
    first = pl.multiple_of(side_ref[0] * half, LANES)
    parts_rows_ref[...] = parts_ref[...].astype(jnp.float32)
    out_rows = jnp.concatenate([parts_rows_ref[:, j, :] for j in range(chunks)], axis=1)
    grad_rows = jnp.concatenate([parts_rows_ref[:, chunks + j, :] for j in range(chunks)], axis=1)
    stats = parts_rows_ref[:, 2 * chunks, :]
    lane = lanes_of(slots)

    def over_seq(values):
        total = values[:slots]
        for q in range(1, seq_size):
            total = total + values[q * slots : (q + 1) * slots]
        return total

    peak = from_lanes(stats[:slots], lane, 0, 3)
    total = from_lanes(stats[:slots], lane, 3, 3)
    correction = from_lanes(over_seq(stats), lane, 6, 3)
    slot_out_ref[...] = over_seq(out_rows).astype(jnp.bfloat16)
    slot_in_grad_ref[...] = over_seq(grad_rows).astype(jnp.bfloat16)
    out_rows = out_rows.astype(jnp.bfloat16)
    grad_rows = grad_rows.astype(jnp.bfloat16)
    comb_grad = over_seq(
        jnp.concatenate(
            [dot(out_rows, cotangent_ref[...], 1, 1), dot(out_rows, cotangent_other_ref[...], 1, 1)], axis=1
        )
    )
    disp_grad = over_seq(
        jnp.concatenate(
            [dot(grad_rows, tokens_ref[...], 1, 1), dot(grad_rows, tokens_other_ref[...], 1, 1)], axis=1
        )
    )
    comb_prob = comb_ref[...]
    disp_prob = jnp.exp(logits_ref[...] - peak) / total
    comb_mean = jnp.sum(comb_prob * comb_grad, axis=0, keepdims=True)
    logit_grad = (
        comb_prob * (comb_grad - comb_mean) + disp_prob * (disp_grad - correction)
    ).astype(jnp.bfloat16)
    dispatch_ref[...] = disp_prob[:, :own].astype(jnp.bfloat16)
    logit_grad_ref[...] = logit_grad[:, :own]
    keys_part = dot(logit_grad[:, :own], tokens_ref[:, pl.ds(first, half)], 1, 0) + dot(
        logit_grad[:, own:], tokens_other_ref[:, pl.ds(first, half)], 1, 0
    )
    for s in range(slots):
        for q in range(seq_size):
            message_ref[q * slots + s] = keys_part[s : s + 1]


def local(tokens, slot_keys, w_in, w_out, cotangent):
    both = ("seq", "exp")
    seq_size, exp_size = lax.axis_size("seq"), lax.axis_size("exp")
    devices = seq_size * exp_size
    experts, hidden, width = w_in.shape
    assert experts == 1 and seq_size % 2 == 0
    slots = exp_size
    half = width // 2
    own = tokens.shape[0]
    side = lax.rem(lax.axis_index("seq"), 2).astype(jnp.int32).reshape(1)
    swap = [(i, i ^ 1) for i in range(seq_size)]
    f32, bf16 = jnp.float32, jnp.bfloat16
    shape = jax.ShapeDtypeStruct

    key_rows = padded(width // LANES, 16)
    key_message = call(
        keys_kernel,
        shape((exp_size, key_rows, LANES), bf16),
        [pltpu.VMEM((key_rows, LANES), f32)],
        [slot_keys.T],
    )
    keys = lax.all_to_all(key_message, "exp", 0, 0, tiled=True)
    tokens_other = lax.ppermute(tokens, "seq", swap)
    cotangent_other = lax.ppermute(cotangent, "seq", swap)

    sum_rows = padded(3 * half // LANES + 1, 16)
    message, logits, comb_prob, keys_all = call(
        sums_kernel,
        (
            shape((devices, sum_rows, LANES), bf16),
            shape((slots, 2 * own), f32),
            shape((slots, 2 * own), f32),
            shape((slots, width), bf16),
        ),
        [pltpu.VMEM((slots, key_rows, LANES), f32), pltpu.VMEM((slots, sum_rows, LANES), f32)],
        [side, keys, tokens, tokens_other, cotangent, cotangent_other],
        smem=1,
    )
    parts = lax.all_to_all(message, both, 0, 0, tiled=True)

    row_count = padded(2 * width // LANES + 1, 8)
    message, slot_in, slot_out_grad, activation, pre_grad = call(
        functools.partial(expert_kernel, exp_size),
        (
            shape((devices, row_count, LANES), bf16),
            shape((1, width), bf16),
            shape((1, width), bf16),
            shape((1, hidden), bf16),
            shape((1, hidden), bf16),
        ),
        [pltpu.VMEM((devices, sum_rows, LANES), f32), pltpu.VMEM((row_count, LANES), f32)],
        [parts, w_in[0], w_out[0]],
    )
    gathered = lax.all_to_all(message, both, 0, 0, tiled=True)
    w_out_grad = (
        activation.astype(f32)[:, :, None] * slot_out_grad.astype(f32)[:, None, :]
    ).astype(bf16)
    w_in_grad = (pre_grad.astype(f32)[:, :, None] * slot_in.astype(f32)[:, None, :]).astype(bf16)

    message, slot_out, slot_in_grad, dispatch, logit_grad = call(
        grads_kernel,
        (
            shape((devices, 1, half), f32),
            shape((slots, width), bf16),
            shape((slots, width), bf16),
            shape((slots, own), bf16),
            shape((slots, own), bf16),
        ),
        [pltpu.VMEM((devices, row_count, LANES), f32)],
        [side, gathered, logits, comb_prob, tokens, tokens_other, cotangent, cotangent_other],
        smem=1,
    )
    keys_parts = lax.all_to_all(message, both, 0, 0, tiled=True)
    layer_out = dot(comb_prob[:, :own].astype(bf16), slot_out, 0, 0).astype(bf16)
    tokens_grad = (dot(dispatch, slot_in_grad, 0, 0) + dot(logit_grad, keys_all, 0, 0)).astype(bf16)
    keys_parts = keys_parts.reshape(seq_size // 2, 2, exp_size, half)
    keys_grad = jnp.sum(keys_parts, axis=(0, 2)).reshape(1, width).T
    return (layer_out, tokens_grad, keys_grad, w_in_grad, w_out_grad)


def solution(mesh):
    return jax.shard_map(
        local,
        mesh=mesh,
        in_specs=(
            P(("seq", "exp"), None),
            P(None, "exp"),
            P("exp", "seq", None),
            P("exp", "seq", None),
            P(("seq", "exp"), None),
        ),
        out_specs=(
            P(("seq", "exp"), None),
            P(("seq", "exp"), None),
            P(None, "exp"),
            P("exp", "seq", None),
            P("exp", "seq", None),
        ),
        check_vma=False,
    )
```

time: 289 us -> 59.9 us (0.21)
  blocking collectives: 266 us -> 9.56 us
  waiting for transfers between devices: 0 us -> 16 us
  starting transfers between devices: 0 us -> 13.4 us
  matrix products: 12.7 us -> 2.31 us
  Pallas kernels: 0 us -> 6.07 us
  local copies, waits for them, and re-layouts: 2.19 us -> 7.1 us
    psum x4 -> x0, blocking collectives: 133 us -> none  [the longest x2 82.8 us: to_owners(): summed_all = lax.psum(make_rows(0, total_rows), ('seq', 'exp'))]
    all_gather x3 -> x0, blocking collectives: 94 us -> none  [the longest x2 61.2 us: to_tokens(): lax.all_gather(summed.astype(jnp.bfloat16), 'exp', axis=0, tiled=True)]
    unnamed x1 -> x0, blocking collectives: 39.4 us -> none
    all_to_all x0 -> x3, waiting for transfers between devices: none -> 16 us  [the longest x1 6.69 us: local(): keys = lax.all_to_all(key_message, 'exp', 0, 0, tiled=True)]
    all_to_all x0 -> x3, starting transfers between devices: none -> 12.8 us  [the longest x1 7.23 us: local(): keys = lax.all_to_all(key_message, 'exp', 0, 0, tiled=True)]
    dot_general x13 -> x3, matrix products: 12.7 us -> 2.31 us  [dot(): lax.dot_general(left, right, (((left_dim,), (right_dim,)), ((), ())), pre...]
    all_to_all x0 -> x1, blocking collectives: none -> 9.56 us  [local(): parts = lax.all_to_all(message, both, 0, 0, tiled=True)]
    pallas_call x0 -> x4, Pallas kernels: none -> 6.07 us  [call(): pl.pallas_call(kernel, out_shape=out_shape, in_specs=[pl.BlockSpec(memory...]
  transfers between devices with their start and end apart: 0 -> 5, of which waited for: 0 -> 3; matrix products, arithmetic and copies ran while one was open for 0% -> 11% of each run, Pallas kernels for 0% -> 1%
where the time goes in v2:
time: 59.9 us; the launch traced here: 59.5 us
  waiting for transfers between devices  16 us (27%)
  starting transfers between devices  13.4 us (22%)
  blocking collectives  9.56 us (16%)
  local copies, waits for them, and re-layouts  7.1 us (12%)
  Pallas kernels  6.07 us (10%)
  other arithmetic  4.33 us (7%)
  matrix products  2.31 us (4%)
  between operations  0.71 us (1%)
    all_to_all x1, blocking collectives, local(): parts = lax.all_to_all(message, both, 0, 0, tiled=True)  9.56 us
    all_to_all x1, starting transfers between devices, local(): keys = lax.all_to_all(key_message, 'exp', 0, 0, tiled=True)  7.23 us
    unnamed x16, local copies, waits for them, and re-layouts  7.1 us
    all_to_all x1, waiting for transfers between devices, local(): keys = lax.all_to_all(key_message, 'exp', 0, 0, tiled=True)  6.69 us
    pallas_call x4, Pallas kernels, call(): pl.pallas_call(kernel, out_shape=out_shape, in_specs=[pl.BlockSpec(memory...  6.07 us
    all_to_all x1, waiting for transfers between devices, local(): keys_parts = lax.all_to_all(message, both, 0, 0, tiled=True)  5.11 us
    all_to_all x1, waiting for transfers between devices, local(): gathered = lax.all_to_all(message, both, 0, 0, tiled=True)  4.21 us
    all_to_all x1, starting transfers between devices, local(): keys_parts = lax.all_to_all(message, both, 0, 0, tiled=True)  2.95 us
  transfers between devices with their start and end apart: 5, of which 3 were waited for; matrix products, arithmetic and copies ran while one was open for 11% of the time, Pallas kernels for 1%

profile of v2, /device:TPU:0, one launch (start us, length us, event | category | flops | bytes accessed | tf_op | source)
XLA Modules:
  0.0 59.5 jit_solution(14422585219934852383)
XLA Ops:
  0.6 0.5 collective-permute-start
  1.1 0.1 collective-permute-start.1
  1.2 0.0 copy-start.6
  1.2 0.7 %copy-done.6 = bf16[1280,1]{0,1:T(2,128)(2,1)S(1)} copy-done((bf16[1280,1]{0,1:T(2,128)(2,1)S(1)}, bf16[1280,1]{0,1:T(2,128)(2,1)}, u32[]{:S(2)}) %copy-start.6) | copy-done | bytes 2584
  1.9 0.6 %shard_map.92 = bf16[8,16,128]{2,1,0:T(8,128)(2,1)} custom-call(bf16[1,1280]{1,0:T(2,128)(2,1)S(1)} %bitcast.16), custom_call_target="tpu_custom_call" | custom-call | tf_op jit(solution)/shard_map/pallas_call | solution.py:60
  2.5 7.2 %all-to-all-start = ((bf16[8,16,128]{2,1,0:T(8,128)(2,1)}), bf16[8,16,128]{2,1,0:T(8,128)(2,1)S(1)}, u32[]{:S(2)}, u32[]{:S(2)}) async-start(bf16[8,16,128]{2,1,0:T(8,128)(2,1)} %shard_map.92), calls=%async_computation | async-start | bytes 65536 | tf_op jit(solution)/shard_map/all_to_all | solution.py:272
  9.8 6.7 %all-to-all-done.keys_ref = bf16[8,16,128]{2,1,0:T(8,128)(2,1)S(1)} async-done(((bf16[8,16,128]{2,1,0:T(8,128)(2,1)}), bf16[8,16,128]{2,1,0:T(8,128)(2,1)S(1)}, u32[]{:S(2)}, u32[]{:S(2)}) %all-to-all-start) | async-done | bytes 32800 | tf_op jit(solution)/shard_map/all_to_all | solution.py:272
  16.5 0.0 collective-permute-done.tokens_other_ref
  16.5 0.0 collective-permute-done.1.cotangent_other_ref
  16.5 0.0 copy-start.2
  16.5 1.0 %copy-done.2 = bf16[128,1280]{1,0:T(8,128)(2,1)S(1)} copy-done((bf16[128,1280]{1,0:T(8,128)(2,1)S(1)}, bf16[128,1280]{1,0:T(8,128)(2,1)}, u32[]{:S(2)}) %copy-start.2) | copy-done | bytes 327704
  17.4 0.0 copy-start.4
  17.4 1.0 %copy-done.4 = bf16[128,1280]{1,0:T(8,128)(2,1)S(1)} copy-done((bf16[128,1280]{1,0:T(8,128)(2,1)S(1)}, bf16[128,1280]{1,0:T(8,128)(2,1)}, u32[]{:S(2)}) %copy-start.4) | copy-done | bytes 327704
  18.4 0.6 shard_map.93
  19.0 9.6 %all_to_all.20.parts_ref = bf16[32,16,128]{2,1,0:T(8,128)(2,1)S(1)} all-to-all(bf16[32,16,128]{2,1,0:T(8,128)(2,1)S(1)} %get-tuple-element.20), channel_id=1, replica_groups=mesh['seq'=4,'exp'=8] {'seq','exp'}, dimensions={0} | all-to-all | bytes 262144 | tf_op jit(solution)/shard_map/all_to_all | solution.py:289
  28.6 0.0 copy-start
  28.6 1.9 %copy-done = bf16[1,1280,1280]{2,1,0:T(8,128)(2,1)S(1)} copy-done((bf16[1,1280,1280]{2,1,0:T(8,128)(2,1)S(1)}, bf16[1,1280,1280]{2,1,0:T(8,128)(2,1)}, u32[]{:S(2)}) %copy-start) | copy-done | bytes 3276824
  30.5 0.0 copy-start.1
  30.5 1.9 %copy-done.1 = bf16[1,1280,1280]{2,1,0:T(8,128)(2,1)S(1)} copy-done((bf16[1,1280,1280]{2,1,0:T(8,128)(2,1)S(1)}, bf16[1,1280,1280]{2,1,0:T(8,128)(2,1)}, u32[]{:S(2)}) %copy-start.1) | copy-done | bytes 3276824
  32.4 3.5 %shard_map.94 = (bf16[32,24,128]{2,1,0:T(8,128)(2,1)}, bf16[1,1280]{1,0:T(2,128)(2,1)S(1)}, bf16[1,1280]{1,0:T(2,128)(2,1)S(1)}, bf16[1,1280]{1,0:T(2,128)(2,1)S(1)}, bf16[1,1280]{1,0:T(2,128)(2,1)S(1)}) custom-call(bf16[32,16,128]{2,1,0:T(8,128)(2,1)S(1)} %all_to_all.20.parts_ref, bf16[1280,1280]{1,0:T(8,128)(2,1)S(1)} %bitcast.14, ...), custom_call_target="tpu_custom_call" | custom-call | tf_op jit(solution)/shard_map/pallas_call | solution.py:60
  35.9 2.6 %all-to-all-start.2 = ((bf16[32,24,128]{2,1,0:T(8,128)(2,1)}), bf16[32,24,128]{2,1,0:T(8,128)(2,1)S(1)}, u32[]{:S(2)}, u32[]{:S(2)}) async-start(bf16[32,24,128]{2,1,0:T(8,128)(2,1)} %get-tuple-element.21), calls=%async_computation.2 | async-start | bytes 393216 | tf_op jit(solution)/shard_map/all_to_all | solution.py:304
  38.6 0.0 copy-start.3
  38.6 0.0 copy-start.5
  38.6 2.1 %multiply_convert_fusion = bf16[1,1280,1280]{2,1,0:T(8,128)(2,1)} fusion(f32[1280]{0:T(1024)S(1)} %get-tuple-element.33, f32[1280]{0:T(1024)S(1)} %get-tuple-element.34), kind=kLoop, calls=%fused_computation | loop fusion | flops 3276800 | bytes 3287040 | tf_op jit(solution)/shard_map/convert_element_type | solution.py:307
  40.7 2.1 %multiply_convert_fusion.1 = bf16[1,1280,1280]{2,1,0:T(8,128)(2,1)} fusion(f32[1280]{0:T(1024)S(1)} %get-tuple-element.35, f32[1280]{0:T(1024)S(1)} %get-tuple-element.36), kind=kLoop, calls=%fused_computation.1 | loop fusion | flops 3276800 | bytes 3287040 | tf_op jit(solution)/shard_map/convert_element_type | solution.py:308
  42.9 4.2 %all-to-all-done.2.parts_ref = bf16[32,24,128]{2,1,0:T(8,128)(2,1)S(1)} async-done(((bf16[32,24,128]{2,1,0:T(8,128)(2,1)}), bf16[32,24,128]{2,1,0:T(8,128)(2,1)S(1)}, u32[]{:S(2)}, u32[]{:S(2)}) %all-to-all-start.2) | async-done | bytes 196640 | tf_op jit(solution)/shard_map/all_to_all | solution.py:304
  47.1 0.0 copy-done.3
  47.1 0.0 copy-done.5
  47.1 1.4 %shard_map.95 = (f32[32,1,640]{2,1,0:T(1,128)}, bf16[8,1280]{1,0:T(8,128)(2,1)S(1)}, bf16[8,1280]{1,0:T(8,128)(2,1)S(1)}, bf16[8,128]{1,0:T(8,128)(2,1)S(1)}, bf16[8,128]{1,0:T(8,128)(2,1)S(1)}) custom-call(s32[1]{0:T(128)} %bitcast.side_ref, bf16[32,24,128]{2,1,0:T(8,128)(2,1)S(1)} %all-to-all-done.2.parts_ref, f32[8,256]{1,0:T(8,128)S(1)} %get-tuple-element.22.logits_ref, ...), custom_call_target="tpu_custom_call" | custom-call | tf_op jit(solution)/shard_map/pallas_call | solution.py:60
  48.4 3.0 %all-to-all-start.3 = ((f32[32,1,640]{2,1,0:T(1,128)}), f32[32,1,640]{2,1,0:T(1,128)S(1)}, u32[]{:S(2)}, u32[]{:S(2)}) async-start(f32[32,1,640]{2,1,0:T(1,128)} %get-tuple-element.28), calls=%async_computation.3 | async-start | bytes 163840 | tf_op jit(solution)/shard_map/all_to_all | solution.py:323
  51.4 0.3 fusion.1
  51.7 1.0 %fusion = bf16[128,1280]{1,0:T(8,128)(2,1)} fusion(f32[128,1280]{1,0:T(8,128)S(1)} %fusion.1, bf16[8,128]{1,0:T(8,128)(2,1)S(1)} %get-tuple-element.24, bf16[8,1280]{1,0:T(8,128)(2,1)S(1)} %get-tuple-element.25), kind=kOutput, calls=%fused_computation.3 | convolution fusion | flops 2949120 | bytes 1005568 | tf_op jit(solution)/shard_map/dot_general | solution.py:16
  52.7 1.0 %convolution_convert_fusion = bf16[128,1280]{1,0:T(8,128)(2,1)} fusion(bf16[8,1280]{1,0:T(8,128)(2,1)S(1)} %get-tuple-element.23, f32[8,256]{1,0:T(8,128)S(1)} %get-tuple-element.19.comb_ref), kind=kOutput, calls=%fused_computation.4 | convolution fusion | flops 2785280 | bytes 350208 | tf_op jit(solution)/shard_map/dot_general | solution.py:16
  53.7 5.1 %all-to-all-done.3 = f32[32,1,640]{2,1,0:T(1,128)S(1)} async-done(((f32[32,1,640]{2,1,0:T(1,128)}), f32[32,1,640]{2,1,0:T(1,128)S(1)}, u32[]{:S(2)}, u32[]{:S(2)}) %all-to-all-start.3) | async-done | bytes 81952 | tf_op jit(solution)/shard_map/all_to_all | solution.py:323
  58.9 0.6 %copy.11 = f32[1,1,2,640]{3,1,2,0:T(1,128)} copy(f32[1,1,2,640]{3,2,1,0:T(2,128)S(1)} %bitcast.18) | data formatting | bytes 10240
  (4 shorter events, 0.1 us)
Async XLA Ops:
  0.6 15.8 %collective-permute-start = (bf16[128,1280]{1,0:T(8,128)(2,1)}, bf16[128,1280]{1,0:T(8,128)(2,1)S(1)}, u32[]{:S(2)}, u32[]{:S(2)}) collective-permute-start(bf16[128,1280]{1,0:T(8,128)(2,1)} %tokens_ref.3), channel_id=1, source_target_pairs={{0,8},{8,0},{16,24},{24,16},{1,9},{9,1},{17,25},{25,17},{2,10},{10... | collective-permute-start | bytes 983048 | tf_op jit(solution)/shard_map/ppermute | solution.py:273
  1.1 15.3 %collective-permute-start.1 = (bf16[128,1280]{1,0:T(8,128)(2,1)}, bf16[128,1280]{1,0:T(8,128)(2,1)S(1)}, u32[]{:S(2)}, u32[]{:S(2)}) collective-permute-start(bf16[128,1280]{1,0:T(8,128)(2,1)} %cotangent_ref.3), channel_id=1, source_target_pairs={{0,8},{8,0},{16,24},{24,16},{1,9},{9,1},{17,25},{25,17},{2,10},{10... | collective-permute-start | bytes 983048 | tf_op jit(solution)/shard_map/ppermute | solution.py:274
  1.2 0.7 %copy-start.6 = (bf16[1280,1]{0,1:T(2,128)(2,1)S(1)}, bf16[1280,1]{0,1:T(2,128)(2,1)}, u32[]{:S(2)}) copy-start(bf16[1280,1]{0,1:T(2,128)(2,1)} %param.6) | copy-start | bytes 7684
  2.5 13.9 %all-to-all-start = ((bf16[8,16,128]{2,1,0:T(8,128)(2,1)}), bf16[8,16,128]{2,1,0:T(8,128)(2,1)S(1)}, u32[]{:S(2)}, u32[]{:S(2)}) async-start(bf16[8,16,128]{2,1,0:T(8,128)(2,1)} %shard_map.92), calls=%async_computation | async-start | bytes 65536 | tf_op jit(solution)/shard_map/all_to_all | solution.py:272
  16.5 1.0 %copy-start.2 = (bf16[128,1280]{1,0:T(8,128)(2,1)S(1)}, bf16[128,1280]{1,0:T(8,128)(2,1)}, u32[]{:S(2)}) copy-start(bf16[128,1280]{1,0:T(8,128)(2,1)} %tokens_ref.3) | copy-start | bytes 983044
  17.4 1.0 %copy-start.4 = (bf16[128,1280]{1,0:T(8,128)(2,1)S(1)}, bf16[128,1280]{1,0:T(8,128)(2,1)}, u32[]{:S(2)}) copy-start(bf16[128,1280]{1,0:T(8,128)(2,1)} %cotangent_ref.3) | copy-start | bytes 983044
  28.6 1.9 %copy-start = (bf16[1,1280,1280]{2,1,0:T(8,128)(2,1)S(1)}, bf16[1,1280,1280]{2,1,0:T(8,128)(2,1)}, u32[]{:S(2)}) copy-start(bf16[1,1280,1280]{2,1,0:T(8,128)(2,1)} %param.7) | copy-start | bytes 9830404
  30.5 1.9 %copy-start.1 = (bf16[1,1280,1280]{2,1,0:T(8,128)(2,1)S(1)}, bf16[1,1280,1280]{2,1,0:T(8,128)(2,1)}, u32[]{:S(2)}) copy-start(bf16[1,1280,1280]{2,1,0:T(8,128)(2,1)} %param.8) | copy-start | bytes 9830404
  35.9 11.1 %all-to-all-start.2 = ((bf16[32,24,128]{2,1,0:T(8,128)(2,1)}), bf16[32,24,128]{2,1,0:T(8,128)(2,1)S(1)}, u32[]{:S(2)}, u32[]{:S(2)}) async-start(bf16[32,24,128]{2,1,0:T(8,128)(2,1)} %get-tuple-element.21), calls=%async_computation.2 | async-start | bytes 393216 | tf_op jit(solution)/shard_map/all_to_all | solution.py:304
  38.6 8.5 %copy-start.3 = (bf16[128,1280]{1,0:T(8,128)(2,1)S(1)}, bf16[128,1280]{1,0:T(8,128)(2,1)}, u32[]{:S(2)}) copy-start(bf16[128,1280]{1,0:T(8,128)(2,1)} %tokens_ref.3) | copy-start | bytes 983044
  38.6 8.5 %copy-start.5 = (bf16[128,1280]{1,0:T(8,128)(2,1)S(1)}, bf16[128,1280]{1,0:T(8,128)(2,1)}, u32[]{:S(2)}) copy-start(bf16[128,1280]{1,0:T(8,128)(2,1)} %cotangent_ref.3) | copy-start | bytes 983044
  48.4 10.4 %all-to-all-start.3 = ((f32[32,1,640]{2,1,0:T(1,128)}), f32[32,1,640]{2,1,0:T(1,128)S(1)}, u32[]{:S(2)}, u32[]{:S(2)}) async-start(f32[32,1,640]{2,1,0:T(1,128)} %get-tuple-element.28), calls=%async_computation.3 | async-start | bytes 163840 | tf_op jit(solution)/shard_map/all_to_all | solution.py:323

commit v3 on v2

--- a/solution.py
+++ b/solution.py
@@ -56,12 +56,11 @@
     return lax.broadcasted_iota(jnp.int32, (rows, LANES), 1)
 
 
-def call(kernel, out_shape, scratch_shapes, inputs, smem=0):
+def call(kernel, out_shape, scratch_shapes, inputs):
     return pl.pallas_call(
         kernel,
         out_shape=out_shape,
-        in_specs=[pl.BlockSpec(memory_space=pltpu.SMEM)] * smem
-        + [pl.BlockSpec(memory_space=pltpu.VMEM)] * (len(inputs) - smem),
+        in_specs=[pl.BlockSpec(memory_space=pltpu.VMEM)] * len(inputs),
         out_specs=jax.tree.map(lambda _: pl.BlockSpec(memory_space=pltpu.VMEM), out_shape),
         scratch_shapes=scratch_shapes,
         compiler_params=pltpu.CompilerParams(vmem_limit_bytes=24 * 1024 * 1024),
@@ -80,14 +79,14 @@
 
 
 def sums_kernel(
-    side_ref, keys_ref, tokens_ref, tokens_other_ref, cotangent_ref, cotangent_other_ref,
+    keys_ref, tokens_ref, tokens_other_ref, cotangent_ref, cotangent_other_ref,
     message_ref, logits_ref, comb_ref, keys_all_ref, keys_rows_ref, rows_ref,
 ):
     slots = keys_ref.shape[0]
     width = tokens_ref.shape[1]
     half = width // 2
     chunks = half // LANES
-    first = pl.multiple_of(side_ref[0] * half, LANES)
+    first = pl.multiple_of(lax.rem(lax.axis_index("seq"), 2) * half, LANES)
 
     keys_rows_ref[...] = keys_ref[...].astype(jnp.float32)
     keys = jnp.concatenate(
@@ -193,7 +192,7 @@
 
 
 def grads_kernel(
-    side_ref, parts_ref, logits_ref, comb_ref, tokens_ref, tokens_other_ref, cotangent_ref, cotangent_other_ref,
+    parts_ref, logits_ref, comb_ref, tokens_ref, tokens_other_ref, cotangent_ref, cotangent_other_ref,
     message_ref, slot_out_ref, slot_in_grad_ref, dispatch_ref, logit_grad_ref, parts_rows_ref,
 ):
     devices = parts_ref.shape[0]
@@ -202,7 +201,7 @@
     own, width = tokens_ref.shape
     half = width // 2
     chunks = width // LANES
-    first = pl.multiple_of(side_ref[0] * half, LANES)
+    first = pl.multiple_of(lax.rem(lax.axis_index("seq"), 2) * half, LANES)
     parts_rows_ref[...] = parts_ref[...].astype(jnp.float32)
     out_rows = jnp.concatenate([parts_rows_ref[:, j, :] for j in range(chunks)], axis=1)
     grad_rows = jnp.concatenate([parts_rows_ref[:, chunks + j, :] for j in range(chunks)], axis=1)
@@ -257,11 +256,15 @@
     slots = exp_size
     half = width // 2
     own = tokens.shape[0]
-    side = lax.rem(lax.axis_index("seq"), 2).astype(jnp.int32).reshape(1)
     swap = [(i, i ^ 1) for i in range(seq_size)]
     f32, bf16 = jnp.float32, jnp.bfloat16
     shape = jax.ShapeDtypeStruct
 
+    stay = [(i, i) for i in range(seq_size)]
+    w_in_near = lax.ppermute(w_in, "seq", stay)
+    w_out_near = lax.ppermute(w_out, "seq", stay)
+    tokens_near = lax.ppermute(tokens, "seq", stay)
+    cotangent_near = lax.ppermute(cotangent, "seq", stay)
     key_rows = padded(width // LANES, 16)
     key_message = call(
         keys_kernel,
@@ -283,8 +286,7 @@
             shape((slots, width), bf16),
         ),
         [pltpu.VMEM((slots, key_rows, LANES), f32), pltpu.VMEM((slots, sum_rows, LANES), f32)],
-        [side, keys, tokens, tokens_other, cotangent, cotangent_other],
-        smem=1,
+        [keys, tokens_near, tokens_other, cotangent_near, cotangent_other],
     )
     parts = lax.all_to_all(message, both, 0, 0, tiled=True)
 
@@ -299,7 +301,7 @@
             shape((1, hidden), bf16),
         ),
         [pltpu.VMEM((devices, sum_rows, LANES), f32), pltpu.VMEM((row_count, LANES), f32)],
-        [parts, w_in[0], w_out[0]],
+        [parts, w_in_near[0], w_out_near[0]],
     )
     gathered = lax.all_to_all(message, both, 0, 0, tiled=True)
     w_out_grad = (
@@ -317,8 +319,7 @@
             shape((slots, own), bf16),
         ),
         [pltpu.VMEM((devices, row_count, LANES), f32)],
-        [side, gathered, logits, comb_prob, tokens, tokens_other, cotangent, cotangent_other],
-        smem=1,
+        [gathered, logits, comb_prob, tokens_near, tokens_other, cotangent_near, cotangent_other],
     )
     keys_parts = lax.all_to_all(message, both, 0, 0, tiled=True)
     layer_out = dot(comb_prob[:, :own].astype(bf16), slot_out, 0, 0).astype(bf16)

time: 59.9 us -> 59.4 us (level)
  blocking collectives: 9.56 us -> 23.2 us
  waiting for transfers between devices: 16 us -> 9.79 us
  local copies, waits for them, and re-layouts: 7.1 us -> 1.29 us
  starting transfers between devices: 13.4 us -> 11.8 us
  Pallas kernels: 6.07 us -> 5.45 us
    all_to_all x0 -> x1, blocking collectives: none -> 13.7 us  [local(): keys = lax.all_to_all(key_message, 'exp', 0, 0, tiled=True)]
    all_to_all x1 -> x0, starting transfers between devices: 7.23 us -> none  [local(): keys = lax.all_to_all(key_message, 'exp', 0, 0, tiled=True)]
    all_to_all x1 -> x0, waiting for transfers between devices: 6.69 us -> none  [local(): keys = lax.all_to_all(key_message, 'exp', 0, 0, tiled=True)]
    unnamed x16 -> x4, local copies, waits for them, and re-layouts: 7.1 us -> 1.29 us
    ppermute x0 -> x4, starting transfers between devices: none -> 5.8 us  [the longest x1 1.93 us: local(): w_in_near = lax.ppermute(w_in, 'seq', stay)]
    pallas_call x4, Pallas kernels: 6.07 us -> 5.45 us  [call(): pl.pallas_call(kernel, out_shape=out_shape, in_specs=[pl.BlockSpec(memory...]
  transfers between devices with their start and end apart: 5 -> 8, of which waited for: 3 -> 3; matrix products, arithmetic and copies ran while one was open for 11% -> 11% of each run, Pallas kernels for 1% -> 1%
where the time goes in v3:
time: 59.4 us; the launch traced here: 58.9 us
  blocking collectives  23.2 us (39%)
  starting transfers between devices  11.8 us (20%)
  waiting for transfers between devices  9.79 us (16%)
  Pallas kernels  5.45 us (9%)
  other arithmetic  4.33 us (7%)
  matrix products  2.32 us (4%)
  local copies, waits for them, and re-layouts  1.29 us (2%)
  between operations  0.69 us (1%)
    all_to_all x1, blocking collectives, local(): keys = lax.all_to_all(key_message, 'exp', 0, 0, tiled=True)  13.7 us
    all_to_all x1, blocking collectives, local(): parts = lax.all_to_all(message, both, 0, 0, tiled=True)  9.56 us
    pallas_call x4, Pallas kernels, call(): pl.pallas_call(kernel, out_shape=out_shape, in_specs=[pl.BlockSpec(memory...  5.45 us
    all_to_all x1, waiting for transfers between devices, local(): keys_parts = lax.all_to_all(message, both, 0, 0, tiled=True)  5.11 us
    all_to_all x1, waiting for transfers between devices, local(): gathered = lax.all_to_all(message, both, 0, 0, tiled=True)  4.23 us
    all_to_all x1, starting transfers between devices, local(): keys_parts = lax.all_to_all(message, both, 0, 0, tiled=True)  2.95 us
    all_to_all x1, starting transfers between devices, local(): gathered = lax.all_to_all(message, both, 0, 0, tiled=True)  2.58 us
    dot_general x3, matrix products, dot(): lax.dot_general(left, right, (((left_dim,), (right_dim,)), ((), ())), pre...  2.32 us
  transfers between devices with their start and end apart: 8, of which 3 were waited for; matrix products, arithmetic and copies ran while one was open for 11% of the time, Pallas kernels for 1%

profile of v3, /device:TPU:0, one launch (start us, length us, event | category | flops | bytes accessed | tf_op | source)
XLA Modules:
  0.0 58.9 jit_solution(1270663261912016515)
XLA Ops:
  0.6 1.9 %collective-permute-start.4 = (bf16[1,1280,1280]{2,1,0:T(8,128)(2,1)}, bf16[1,1280,1280]{2,1,0:T(8,128)(2,1)S(1)}, u32[]{:S(2)}, u32[]{:S(2)}) collective-permute-start(bf16[1,1280,1280]{2,1,0:T(8,128)(2,1)} %param.7), channel_id=1, source_target_pairs={{0,0},{8,8},{16,16},{24,24},{1,1},{9,9},{17,17},{25,25},{2,2},{10,... | collective-permute-start | bytes 9830408 | tf_op jit(solution)/shard_map/ppermute | solution.py:264
  2.6 1.9 %collective-permute-start.5 = (bf16[1,1280,1280]{2,1,0:T(8,128)(2,1)}, bf16[1,1280,1280]{2,1,0:T(8,128)(2,1)S(1)}, u32[]{:S(2)}, u32[]{:S(2)}) collective-permute-start(bf16[1,1280,1280]{2,1,0:T(8,128)(2,1)} %param.8), channel_id=1, source_target_pairs={{0,0},{8,8},{16,16},{24,24},{1,1},{9,9},{17,17},{25,25},{2,2},{10,... | collective-permute-start | bytes 9830408 | tf_op jit(solution)/shard_map/ppermute | solution.py:265
  4.5 0.5 collective-permute-start.1
  4.9 1.0 %collective-permute-start = (bf16[128,1280]{1,0:T(8,128)(2,1)}, bf16[128,1280]{1,0:T(8,128)(2,1)S(1)}, u32[]{:S(2)}, u32[]{:S(2)}) collective-permute-start(bf16[128,1280]{1,0:T(8,128)(2,1)} %param.5), channel_id=1, source_target_pairs={{0,0},{8,8},{16,16},{24,24},{1,1},{9,9},{17,17},{25,25},{2,2},{10,... | collective-permute-start | bytes 983048 | tf_op jit(solution)/shard_map/ppermute | solution.py:266
  5.9 0.1 collective-permute-start.3
  6.0 0.4 collective-permute-done.1.tokens_other_ref
  6.4 1.0 %collective-permute-start.2 = (bf16[128,1280]{1,0:T(8,128)(2,1)}, bf16[128,1280]{1,0:T(8,128)(2,1)S(1)}, u32[]{:S(2)}, u32[]{:S(2)}) collective-permute-start(bf16[128,1280]{1,0:T(8,128)(2,1)} %param.9), channel_id=1, source_target_pairs={{0,0},{8,8},{16,16},{24,24},{1,1},{9,9},{17,17},{25,25},{2,2},{10,... | collective-permute-start | bytes 983048 | tf_op jit(solution)/shard_map/ppermute | solution.py:267
  7.4 0.0 copy-start
  7.4 0.7 %copy-done = bf16[1280,1]{0,1:T(2,128)(2,1)S(1)} copy-done((bf16[1280,1]{0,1:T(2,128)(2,1)S(1)}, bf16[1280,1]{0,1:T(2,128)(2,1)}, u32[]{:S(2)}) %copy-start) | copy-done | bytes 2584
  8.1 13.7 %all_to_all.20.keys_ref = bf16[8,16,128]{2,1,0:T(8,128)(2,1)S(1)} all-to-all(bf16[8,16,128]{2,1,0:T(8,128)(2,1)S(1)} %shard_map.92), channel_id=1, replica_groups=mesh['seq'=4,'exp'=8] {'exp'}, dimensions={0} | all-to-all | bytes 65536 | tf_op jit(solution)/shard_map/all_to_all | solution.py:275
  21.7 0.0 collective-permute-done.tokens_ref
  21.7 0.0 collective-permute-done.3.cotangent_other_ref
  21.7 0.0 collective-permute-done.2.cotangent_ref
  21.8 0.6 shard_map.93
  22.3 9.6 %all_to_all.21.parts_ref = bf16[32,16,128]{2,1,0:T(8,128)(2,1)S(1)} all-to-all(bf16[32,16,128]{2,1,0:T(8,128)(2,1)S(1)} %get-tuple-element.20), channel_id=1, replica_groups=mesh['seq'=4,'exp'=8] {'seq','exp'}, dimensions={0} | all-to-all | bytes 262144 | tf_op jit(solution)/shard_map/all_to_all | solution.py:291
  31.9 0.0 collective-permute-done.4
  31.9 0.0 collective-permute-done.5
  31.9 3.5 %shard_map.94 = (bf16[32,24,128]{2,1,0:T(8,128)(2,1)}, bf16[1,1280]{1,0:T(2,128)(2,1)S(1)}, bf16[1,1280]{1,0:T(2,128)(2,1)S(1)}, bf16[1,1280]{1,0:T(2,128)(2,1)S(1)}, bf16[1,1280]{1,0:T(2,128)(2,1)S(1)}) custom-call(bf16[32,16,128]{2,1,0:T(8,128)(2,1)S(1)} %all_to_all.21.parts_ref, bf16[1280,1280]{1,0:T(8,128)(2,1)S(1)} %bitcast.13, ...), custom_call_target="tpu_custom_call" | custom-call | tf_op jit(solution)/shard_map/pallas_call | solution.py:60
  35.4 2.6 %all-to-all-start.2 = ((bf16[32,24,128]{2,1,0:T(8,128)(2,1)}), bf16[32,24,128]{2,1,0:T(8,128)(2,1)S(1)}, u32[]{:S(2)}, u32[]{:S(2)}) async-start(bf16[32,24,128]{2,1,0:T(8,128)(2,1)} %get-tuple-element.21), calls=%async_computation.2 | async-start | bytes 393216 | tf_op jit(solution)/shard_map/all_to_all | solution.py:306
  38.1 2.1 %multiply_convert_fusion = bf16[1,1280,1280]{2,1,0:T(8,128)(2,1)} fusion(f32[1280]{0:T(1024)S(1)} %get-tuple-element.33, f32[1280]{0:T(1024)S(1)} %get-tuple-element.34), kind=kLoop, calls=%fused_computation | loop fusion | flops 3276800 | bytes 3287040 | tf_op jit(solution)/shard_map/convert_element_type | solution.py:309
  40.2 2.1 %multiply_convert_fusion.1 = bf16[1,1280,1280]{2,1,0:T(8,128)(2,1)} fusion(f32[1280]{0:T(1024)S(1)} %get-tuple-element.35, f32[1280]{0:T(1024)S(1)} %get-tuple-element.36), kind=kLoop, calls=%fused_computation.1 | loop fusion | flops 3276800 | bytes 3287040 | tf_op jit(solution)/shard_map/convert_element_type | solution.py:310
  42.3 4.2 %all-to-all-done.2.parts_ref = bf16[32,24,128]{2,1,0:T(8,128)(2,1)S(1)} async-done(((bf16[32,24,128]{2,1,0:T(8,128)(2,1)}), bf16[32,24,128]{2,1,0:T(8,128)(2,1)S(1)}, u32[]{:S(2)}, u32[]{:S(2)}) %all-to-all-start.2) | async-done | bytes 196640 | tf_op jit(solution)/shard_map/all_to_all | solution.py:306
  46.6 1.3 %shard_map.95 = (f32[32,1,640]{2,1,0:T(1,128)}, bf16[8,1280]{1,0:T(8,128)(2,1)S(1)}, bf16[8,1280]{1,0:T(8,128)(2,1)S(1)}, bf16[8,128]{1,0:T(8,128)(2,1)S(1)}, bf16[8,128]{1,0:T(8,128)(2,1)S(1)}) custom-call(bf16[32,24,128]{2,1,0:T(8,128)(2,1)S(1)} %all-to-all-done.2.parts_ref, f32[8,256]{1,0:T(8,128)S(1)} %get-tuple-element.22.logits_ref, ...), custom_call_target="tpu_custom_call" | custom-call | tf_op jit(solution)/shard_map/pallas_call | solution.py:60
  47.9 2.9 %all-to-all-start.3 = ((f32[32,1,640]{2,1,0:T(1,128)}), f32[32,1,640]{2,1,0:T(1,128)S(1)}, u32[]{:S(2)}, u32[]{:S(2)}) async-start(f32[32,1,640]{2,1,0:T(1,128)} %get-tuple-element.28), calls=%async_computation.3 | async-start | bytes 163840 | tf_op jit(solution)/shard_map/all_to_all | solution.py:324
  50.9 0.3 fusion.1
  51.1 1.0 %fusion = bf16[128,1280]{1,0:T(8,128)(2,1)} fusion(f32[128,1280]{1,0:T(8,128)S(1)} %fusion.1, bf16[8,128]{1,0:T(8,128)(2,1)S(1)} %get-tuple-element.24, bf16[8,1280]{1,0:T(8,128)(2,1)S(1)} %get-tuple-element.25), kind=kOutput, calls=%fused_computation.3 | convolution fusion | flops 2949120 | bytes 1005568 | tf_op jit(solution)/shard_map/dot_general | solution.py:16
  52.2 1.0 %convolution_convert_fusion = bf16[128,1280]{1,0:T(8,128)(2,1)} fusion(bf16[8,1280]{1,0:T(8,128)(2,1)S(1)} %get-tuple-element.23, f32[8,256]{1,0:T(8,128)S(1)} %get-tuple-element.19.comb_ref), kind=kOutput, calls=%fused_computation.4 | convolution fusion | flops 2785280 | bytes 350208 | tf_op jit(solution)/shard_map/dot_general | solution.py:16
  53.2 5.1 %all-to-all-done.3 = f32[32,1,640]{2,1,0:T(1,128)S(1)} async-done(((f32[32,1,640]{2,1,0:T(1,128)}), f32[32,1,640]{2,1,0:T(1,128)S(1)}, u32[]{:S(2)}, u32[]{:S(2)}) %all-to-all-start.3) | async-done | bytes 81952 | tf_op jit(solution)/shard_map/all_to_all | solution.py:324
  58.3 0.6 %copy.11 = f32[1,1,2,640]{3,1,2,0:T(1,128)} copy(f32[1,1,2,640]{3,2,1,0:T(2,128)S(1)} %bitcast.17) | data formatting | bytes 10240
  (5 shorter events, 0.1 us)
Async XLA Ops:
  0.6 31.3 %collective-permute-start.4 = (bf16[1,1280,1280]{2,1,0:T(8,128)(2,1)}, bf16[1,1280,1280]{2,1,0:T(8,128)(2,1)S(1)}, u32[]{:S(2)}, u32[]{:S(2)}) collective-permute-start(bf16[1,1280,1280]{2,1,0:T(8,128)(2,1)} %param.7), channel_id=1, source_target_pairs={{0,0},{8,8},{16,16},{24,24},{1,1},{9,9},{17,17},{25,25},{2,2},{10,... | collective-permute-start | bytes 9830408 | tf_op jit(solution)/shard_map/ppermute | solution.py:264
  2.6 29.3 %collective-permute-start.5 = (bf16[1,1280,1280]{2,1,0:T(8,128)(2,1)}, bf16[1,1280,1280]{2,1,0:T(8,128)(2,1)S(1)}, u32[]{:S(2)}, u32[]{:S(2)}) collective-permute-start(bf16[1,1280,1280]{2,1,0:T(8,128)(2,1)} %param.8), channel_id=1, source_target_pairs={{0,0},{8,8},{16,16},{24,24},{1,1},{9,9},{17,17},{25,25},{2,2},{10,... | collective-permute-start | bytes 9830408 | tf_op jit(solution)/shard_map/ppermute | solution.py:265
  4.5 1.9 %collective-permute-start.1 = (bf16[128,1280]{1,0:T(8,128)(2,1)}, bf16[128,1280]{1,0:T(8,128)(2,1)S(1)}, u32[]{:S(2)}, u32[]{:S(2)}) collective-permute-start(bf16[128,1280]{1,0:T(8,128)(2,1)} %param.5), channel_id=1, source_target_pairs={{0,8},{8,0},{16,24},{24,16},{1,9},{9,1},{17,25},{25,17},{2,10},{10... | collective-permute-start | bytes 983048 | tf_op jit(solution)/shard_map/ppermute | solution.py:276
  4.9 16.8 %collective-permute-start = (bf16[128,1280]{1,0:T(8,128)(2,1)}, bf16[128,1280]{1,0:T(8,128)(2,1)S(1)}, u32[]{:S(2)}, u32[]{:S(2)}) collective-permute-start(bf16[128,1280]{1,0:T(8,128)(2,1)} %param.5), channel_id=1, source_target_pairs={{0,0},{8,8},{16,16},{24,24},{1,1},{9,9},{17,17},{25,25},{2,2},{10,... | collective-permute-start | bytes 983048 | tf_op jit(solution)/shard_map/ppermute | solution.py:266
  5.9 15.8 %collective-permute-start.3 = (bf16[128,1280]{1,0:T(8,128)(2,1)}, bf16[128,1280]{1,0:T(8,128)(2,1)S(1)}, u32[]{:S(2)}, u32[]{:S(2)}) collective-permute-start(bf16[128,1280]{1,0:T(8,128)(2,1)} %param.9), channel_id=1, source_target_pairs={{0,8},{8,0},{16,24},{24,16},{1,9},{9,1},{17,25},{25,17},{2,10},{10... | collective-permute-start | bytes 983048 | tf_op jit(solution)/shard_map/ppermute | solution.py:277
  6.4 15.3 %collective-permute-start.2 = (bf16[128,1280]{1,0:T(8,128)(2,1)}, bf16[128,1280]{1,0:T(8,128)(2,1)S(1)}, u32[]{:S(2)}, u32[]{:S(2)}) collective-permute-start(bf16[128,1280]{1,0:T(8,128)(2,1)} %param.9), channel_id=1, source_target_pairs={{0,0},{8,8},{16,16},{24,24},{1,1},{9,9},{17,17},{25,25},{2,2},{10,... | collective-permute-start | bytes 983048 | tf_op jit(solution)/shard_map/ppermute | solution.py:267
  7.4 0.7 %copy-start = (bf16[1280,1]{0,1:T(2,128)(2,1)S(1)}, bf16[1280,1]{0,1:T(2,128)(2,1)}, u32[]{:S(2)}) copy-start(bf16[1280,1]{0,1:T(2,128)(2,1)} %param.6) | copy-start | bytes 7684
  35.4 11.1 %all-to-all-start.2 = ((bf16[32,24,128]{2,1,0:T(8,128)(2,1)}), bf16[32,24,128]{2,1,0:T(8,128)(2,1)S(1)}, u32[]{:S(2)}, u32[]{:S(2)}) async-start(bf16[32,24,128]{2,1,0:T(8,128)(2,1)} %get-tuple-element.21), calls=%async_computation.2 | async-start | bytes 393216 | tf_op jit(solution)/shard_map/all_to_all | solution.py:306
  47.9 10.4 %all-to-all-start.3 = ((f32[32,1,640]{2,1,0:T(1,128)}), f32[32,1,640]{2,1,0:T(1,128)S(1)}, u32[]{:S(2)}, u32[]{:S(2)}) async-start(f32[32,1,640]{2,1,0:T(1,128)} %get-tuple-element.28), calls=%async_computation.3 | async-start | bytes 163840 | tf_op jit(solution)/shard_map/all_to_all | solution.py:324

commit v4 on v3

--- a/solution.py
+++ b/solution.py
@@ -52,18 +52,23 @@
     return jnp.sum(jnp.where(keep, row, 0.0), axis=1, keepdims=True)
 
 
+def block_of(rows):
+    return 256 if rows % 256 == 0 else rows
+
+
 def lanes_of(rows):
     return lax.broadcasted_iota(jnp.int32, (rows, LANES), 1)
 
 
-def call(kernel, out_shape, scratch_shapes, inputs):
+def call(kernel, out_shape, scratch_shapes, inputs, unplaced=0, room=24 * 1024 * 1024):
+    spaces = [pltpu.VMEM] * (len(inputs) - unplaced) + [pltpu.HBM] * unplaced
     return pl.pallas_call(
         kernel,
         out_shape=out_shape,
-        in_specs=[pl.BlockSpec(memory_space=pltpu.VMEM)] * len(inputs),
+        in_specs=[pl.BlockSpec(memory_space=space) for space in spaces],
         out_specs=jax.tree.map(lambda _: pl.BlockSpec(memory_space=pltpu.VMEM), out_shape),
         scratch_shapes=scratch_shapes,
-        compiler_params=pltpu.CompilerParams(vmem_limit_bytes=24 * 1024 * 1024),
+        compiler_params=pltpu.CompilerParams(vmem_limit_bytes=room),
     )(*inputs)
 
 
@@ -79,9 +84,14 @@
 
 
 def sums_kernel(
-    keys_ref, tokens_ref, tokens_other_ref, cotangent_ref, cotangent_other_ref,
-    message_ref, logits_ref, comb_ref, keys_all_ref, keys_rows_ref, rows_ref,
+    keys_ref, tokens_other_ref, cotangent_other_ref, tokens_far_ref, cotangent_far_ref,
+    message_ref, logits_ref, comb_ref, keys_all_ref,
+    tokens_ref, cotangent_ref, keys_rows_ref, rows_ref, sems,
 ):
+    tokens_copy = pltpu.make_async_copy(tokens_far_ref, tokens_ref, sems.at[0])
+    cotangent_copy = pltpu.make_async_copy(cotangent_far_ref, cotangent_ref, sems.at[1])
+    tokens_copy.start()
+    cotangent_copy.start()
     slots = keys_ref.shape[0]
     width = tokens_ref.shape[1]
     half = width // 2
@@ -93,9 +103,9 @@
         [keys_rows_ref[:, j, :] for j in range(width // LANES)], axis=1
     ).astype(jnp.bfloat16)
     keys_all_ref[...] = keys
-    logits = jnp.concatenate(
-        [dot(keys, tokens_ref[...], 1, 1), dot(keys, tokens_other_ref[...], 1, 1)], axis=1
-    )
+    other_logits = dot(keys, tokens_other_ref[...], 1, 1)
+    tokens_copy.wait()
+    logits = jnp.concatenate([dot(keys, tokens_ref[...], 1, 1), other_logits], axis=1)
     logits_ref[...] = logits
     own = tokens_ref.shape[0]
 
@@ -103,6 +113,7 @@
     comb_prob = row_terms / jnp.sum(row_terms, axis=0, keepdims=True)
     comb_ref[...] = comb_prob
     combine = comb_prob.astype(jnp.bfloat16)
+    cotangent_copy.wait()
     grad_sums = dot(combine[:, :own], cotangent_ref[:, pl.ds(first, half)], 1, 0) + dot(
         combine[:, own:], cotangent_other_ref[:, pl.ds(first, half)], 1, 0
     )
@@ -130,9 +141,20 @@
 
 
 def expert_kernel(
-    exp_size, parts_ref, w_in_ref, w_out_ref,
-    message_ref, slot_in_ref, slot_out_grad_ref, activation_ref, pre_grad_ref, parts_rows_ref, rows_ref,
+    exp_size, parts_ref, w_in_far_ref, w_out_far_ref,
+    message_ref, slot_in_ref, slot_out_grad_ref, activation_ref, pre_grad_ref,
+    w_in_ref, w_out_ref, parts_rows_ref, rows_ref, sems,
 ):
+    hidden = w_in_ref.shape[0]
+    block_rows = block_of(hidden)
+    blocks = [pl.ds(i * block_rows, block_rows) for i in range(hidden // block_rows)]
+    copies = [
+        [pltpu.make_async_copy(far.at[rows], near.at[rows], sems.at[w, i]) for i, rows in enumerate(blocks)]
+        for w, (far, near) in enumerate([(w_in_far_ref, w_in_ref), (w_out_far_ref, w_out_ref)])
+    ]
+    for pair in copies:
+        for copy in pair:
+            copy.start()
     devices = parts_ref.shape[0]
     seq_size = devices // exp_size
     width = w_in_ref.shape[1]
@@ -166,8 +188,15 @@
     slot_in_ref[...] = slot_in
     slot_out_grad_ref[...] = slot_out_grad
 
-    pre_act = dot(slot_in, w_in_ref[...], 1, 1)
-    act_grad = dot(slot_out_grad, w_out_ref[...], 1, 1)
+    def times_rows(row, copies_of, w_ref):
+        outs = []
+        for copy, rows in zip(copies_of, blocks):
+            copy.wait()
+            outs.append(dot(row, w_ref[rows, :], 1, 1))
+        return jnp.concatenate(outs, axis=1)
+
+    pre_act = times_rows(slot_in, copies[0], w_in_ref)
+    act_grad = times_rows(slot_out_grad, copies[1], w_out_ref)
     value, slope = gelu_parts(pre_act)
     activation = value.astype(jnp.bfloat16)
     pre_grad = (act_grad * slope).astype(jnp.bfloat16)
@@ -260,11 +289,6 @@
     f32, bf16 = jnp.float32, jnp.bfloat16
     shape = jax.ShapeDtypeStruct
 
-    stay = [(i, i) for i in range(seq_size)]
-    w_in_near = lax.ppermute(w_in, "seq", stay)
-    w_out_near = lax.ppermute(w_out, "seq", stay)
-    tokens_near = lax.ppermute(tokens, "seq", stay)
-    cotangent_near = lax.ppermute(cotangent, "seq", stay)
     key_rows = padded(width // LANES, 16)
     key_message = call(
         keys_kernel,
@@ -285,8 +309,16 @@
             shape((slots, 2 * own), f32),
             shape((slots, width), bf16),
         ),
-        [pltpu.VMEM((slots, key_rows, LANES), f32), pltpu.VMEM((slots, sum_rows, LANES), f32)],
-        [keys, tokens_near, tokens_other, cotangent_near, cotangent_other],
+        [
+            pltpu.VMEM(tokens.shape, bf16),
+            pltpu.VMEM(cotangent.shape, bf16),
+            pltpu.VMEM((slots, key_rows, LANES), f32),
+            pltpu.VMEM((slots, sum_rows, LANES), f32),
+            pltpu.SemaphoreType.DMA((2,)),
+        ],
+        [keys, tokens_other, cotangent_other, tokens, cotangent],
+        unplaced=2,
+        room=(64 * 1024 - 11300) * 1024,
     )
     parts = lax.all_to_all(message, both, 0, 0, tiled=True)
 
@@ -300,8 +332,16 @@
             shape((1, hidden), bf16),
             shape((1, hidden), bf16),
         ),
-        [pltpu.VMEM((devices, sum_rows, LANES), f32), pltpu.VMEM((row_count, LANES), f32)],
-        [parts, w_in_near[0], w_out_near[0]],
+        [
+            pltpu.VMEM((hidden, width), bf16),
+            pltpu.VMEM((hidden, width), bf16),
+            pltpu.VMEM((devices, sum_rows, LANES), f32),
+            pltpu.VMEM((row_count, LANES), f32),
+            pltpu.SemaphoreType.DMA((2, hidden // block_of(hidden))),
+        ],
+        [parts, w_in[0], w_out[0]],
+        unplaced=2,
+        room=(64 * 1024 - 13300) * 1024,
     )
     gathered = lax.all_to_all(message, both, 0, 0, tiled=True)
     w_out_grad = (
@@ -319,7 +359,7 @@
             shape((slots, own), bf16),
         ),
         [pltpu.VMEM((devices, row_count, LANES), f32)],
-        [gathered, logits, comb_prob, tokens_near, tokens_other, cotangent_near, cotangent_other],
+        [gathered, logits, comb_prob, tokens, tokens_other, cotangent, cotangent_other],
     )
     keys_parts = lax.all_to_all(message, both, 0, 0, tiled=True)
     layer_out = dot(comb_prob[:, :own].astype(bf16), slot_out, 0, 0).astype(bf16)

time: 59.4 us -> 58.1 us (0.978)
  starting transfers between devices: 11.8 us -> 6.15 us
  Pallas kernels: 5.45 us -> 10.3 us
    ppermute x4 -> x0, starting transfers between devices: 5.8 us -> none  [the longest x1 1.93 us: local(): w_in_near = lax.ppermute(w_in, 'seq', stay)]
    pallas_call x4, Pallas kernels: 5.45 us -> 10.3 us  [call(): pl.pallas_call(kernel, out_shape=out_shape, in_specs=[pl.BlockSpec(memory...]
    unnamed x4 -> x8, local copies, waits for them, and re-layouts: 1.29 us -> 1.31 us
  transfers between devices with their start and end apart: 8 -> 4, of which waited for: 3 -> 2; matrix products, arithmetic and copies ran while one was open for 11% -> 11% of each run, Pallas kernels for 1% -> 0%
where the time goes in v4:
time: 58.1 us; the launch traced here: 57.7 us
  blocking collectives  23.3 us (40%)
  Pallas kernels  10.3 us (18%)
  waiting for transfers between devices  9.33 us (16%)
  starting transfers between devices  6.15 us (11%)
  other arithmetic  4.33 us (7%)
  matrix products  2.32 us (4%)
  local copies, waits for them, and re-layouts  1.31 us (2%)
  between operations  0.71 us (1%)
    all_to_all x1, blocking collectives, local(): keys = lax.all_to_all(key_message, 'exp', 0, 0, tiled=True)  13.7 us
    pallas_call x4, Pallas kernels, call(): pl.pallas_call(kernel, out_shape=out_shape, in_specs=[pl.BlockSpec(memory...  10.3 us
    all_to_all x1, blocking collectives, local(): parts = lax.all_to_all(message, both, 0, 0, tiled=True)  9.56 us
    all_to_all x1, waiting for transfers between devices, local(): keys_parts = lax.all_to_all(message, both, 0, 0, tiled=True)  5.11 us
    all_to_all x1, waiting for transfers between devices, local(): gathered = lax.all_to_all(message, both, 0, 0, tiled=True)  4.21 us
    all_to_all x1, starting transfers between devices, local(): keys_parts = lax.all_to_all(message, both, 0, 0, tiled=True)  2.95 us
    all_to_all x1, starting transfers between devices, local(): gathered = lax.all_to_all(message, both, 0, 0, tiled=True)  2.6 us
    dot_general x3, matrix products, dot(): lax.dot_general(left, right, (((left_dim,), (right_dim,)), ((), ())), pre...  2.32 us
  transfers between devices with their start and end apart: 4, of which 2 were waited for; matrix products, arithmetic and copies ran while one was open for 11% of the time, Pallas kernels for 0%

profile of v4, /device:TPU:0, one launch (start us, length us, event | category | flops | bytes accessed | tf_op | source)
XLA Modules:
  0.0 57.7 jit_solution(12839131114190139686)
XLA Ops:
  0.6 0.5 collective-permute-start
  1.1 0.1 collective-permute-start.1
  1.2 0.0 copy-start.2
  1.2 0.7 %copy-done.2 = bf16[1280,1]{0,1:T(2,128)(2,1)S(1)} copy-done((bf16[1280,1]{0,1:T(2,128)(2,1)S(1)}, bf16[1280,1]{0,1:T(2,128)(2,1)}, u32[]{:S(2)}) %copy-start.2) | copy-done | bytes 2584
  1.9 13.7 %all_to_all.20.keys_ref = bf16[8,16,128]{2,1,0:T(8,128)(2,1)S(1)} all-to-all(bf16[8,16,128]{2,1,0:T(8,128)(2,1)S(1)} %shard_map.92), channel_id=1, replica_groups=mesh['seq'=4,'exp'=8] {'exp'}, dimensions={0} | all-to-all | bytes 65536 | tf_op jit(solution)/shard_map/all_to_all | solution.py:299
  15.6 0.0 collective-permute-done.tokens_other_ref
  15.6 0.0 collective-permute-done.1.cotangent_other_ref
  15.7 1.6 %shard_map.93 = (bf16[32,16,128]{2,1,0:T(8,128)(2,1)S(1)}, f32[8,256]{1,0:T(8,128)S(1)}, f32[8,256]{1,0:T(8,128)S(1)}, bf16[8,1280]{1,0:T(8,128)(2,1)S(1)}) custom-call(bf16[8,16,128]{2,1,0:T(8,128)(2,1)S(1)} %all_to_all.20.keys_ref, bf16[128,1280]{1,0:T(8,128)(2,1)S(1)} %collective-permute-done.tokens_other_ref, ...), custom_call_target="tpu_custom_call" | custom-call | tf_op jit(solution)/shard_map/pallas_call | solution.py:65
  17.3 9.6 %all_to_all.21.parts_ref = bf16[32,16,128]{2,1,0:T(8,128)(2,1)S(1)} all-to-all(bf16[32,16,128]{2,1,0:T(8,128)(2,1)S(1)} %get-tuple-element.20), channel_id=1, replica_groups=mesh['seq'=4,'exp'=8] {'seq','exp'}, dimensions={0} | all-to-all | bytes 262144 | tf_op jit(solution)/shard_map/all_to_all | solution.py:323
  26.8 7.4 %shard_map.94 = (bf16[32,24,128]{2,1,0:T(8,128)(2,1)}, bf16[1,1280]{1,0:T(2,128)(2,1)S(1)}, bf16[1,1280]{1,0:T(2,128)(2,1)S(1)}, bf16[1,1280]{1,0:T(2,128)(2,1)S(1)}, bf16[1,1280]{1,0:T(2,128)(2,1)S(1)}) custom-call(bf16[32,16,128]{2,1,0:T(8,128)(2,1)S(1)} %all_to_all.21.parts_ref, bf16[1280,1280]{1,0:T(8,128)(2,1)} %bitcast.14, bf16[1280,1280]{1,0:T(8,128)(2,1)} %bitcast.15), custom_call_target="tpu_custom_call" | custom-call | tf_op jit(solution)/shard_map/pallas_call | solution.py:65
  34.2 2.6 %all-to-all-start.2 = ((bf16[32,24,128]{2,1,0:T(8,128)(2,1)}), bf16[32,24,128]{2,1,0:T(8,128)(2,1)S(1)}, u32[]{:S(2)}, u32[]{:S(2)}) async-start(bf16[32,24,128]{2,1,0:T(8,128)(2,1)} %get-tuple-element.21), calls=%async_computation.2 | async-start | bytes 393216 | tf_op jit(solution)/shard_map/all_to_all | solution.py:346
  36.9 0.0 copy-start
  36.9 0.0 copy-start.1
  36.9 2.1 %multiply_convert_fusion = bf16[1,1280,1280]{2,1,0:T(8,128)(2,1)} fusion(f32[1280]{0:T(1024)S(1)} %get-tuple-element.33, f32[1280]{0:T(1024)S(1)} %get-tuple-element.34), kind=kLoop, calls=%fused_computation | loop fusion | flops 3276800 | bytes 3287040 | tf_op jit(solution)/shard_map/convert_element_type | solution.py:349
  39.0 2.1 %multiply_convert_fusion.1 = bf16[1,1280,1280]{2,1,0:T(8,128)(2,1)} fusion(f32[1280]{0:T(1024)S(1)} %get-tuple-element.35, f32[1280]{0:T(1024)S(1)} %get-tuple-element.36), kind=kLoop, calls=%fused_computation.1 | loop fusion | flops 3276800 | bytes 3287040 | tf_op jit(solution)/shard_map/convert_element_type | solution.py:350
  41.2 4.2 %all-to-all-done.2.parts_ref = bf16[32,24,128]{2,1,0:T(8,128)(2,1)S(1)} async-done(((bf16[32,24,128]{2,1,0:T(8,128)(2,1)}), bf16[32,24,128]{2,1,0:T(8,128)(2,1)S(1)}, u32[]{:S(2)}, u32[]{:S(2)}) %all-to-all-start.2) | async-done | bytes 196640 | tf_op jit(solution)/shard_map/all_to_all | solution.py:346
  45.4 0.0 copy-done
  45.4 0.0 copy-done.1
  45.4 1.4 %shard_map.95 = (f32[32,1,640]{2,1,0:T(1,128)}, bf16[8,1280]{1,0:T(8,128)(2,1)S(1)}, bf16[8,1280]{1,0:T(8,128)(2,1)S(1)}, bf16[8,128]{1,0:T(8,128)(2,1)S(1)}, bf16[8,128]{1,0:T(8,128)(2,1)S(1)}) custom-call(bf16[32,24,128]{2,1,0:T(8,128)(2,1)S(1)} %all-to-all-done.2.parts_ref, f32[8,256]{1,0:T(8,128)S(1)} %get-tuple-element.22.logits_ref, ...), custom_call_target="tpu_custom_call" | custom-call | tf_op jit(solution)/shard_map/pallas_call | solution.py:65
  46.7 2.9 %all-to-all-start.3 = ((f32[32,1,640]{2,1,0:T(1,128)}), f32[32,1,640]{2,1,0:T(1,128)S(1)}, u32[]{:S(2)}, u32[]{:S(2)}) async-start(f32[32,1,640]{2,1,0:T(1,128)} %get-tuple-element.28), calls=%async_computation.3 | async-start | bytes 163840 | tf_op jit(solution)/shard_map/all_to_all | solution.py:364
  49.7 0.3 fusion.1
  50.0 1.0 %fusion = bf16[128,1280]{1,0:T(8,128)(2,1)} fusion(f32[128,1280]{1,0:T(8,128)S(1)} %fusion.1, bf16[8,128]{1,0:T(8,128)(2,1)S(1)} %get-tuple-element.24, bf16[8,1280]{1,0:T(8,128)(2,1)S(1)} %get-tuple-element.25), kind=kOutput, calls=%fused_computation.3 | convolution fusion | flops 2949120 | bytes 1005568 | tf_op jit(solution)/shard_map/dot_general | solution.py:16
  51.0 1.0 %convolution_convert_fusion = bf16[128,1280]{1,0:T(8,128)(2,1)} fusion(bf16[8,1280]{1,0:T(8,128)(2,1)S(1)} %get-tuple-element.23, f32[8,256]{1,0:T(8,128)S(1)} %get-tuple-element.19.comb_ref), kind=kOutput, calls=%fused_computation.4 | convolution fusion | flops 2785280 | bytes 350208 | tf_op jit(solution)/shard_map/dot_general | solution.py:16
  52.0 5.1 %all-to-all-done.3 = f32[32,1,640]{2,1,0:T(1,128)S(1)} async-done(((f32[32,1,640]{2,1,0:T(1,128)}), f32[32,1,640]{2,1,0:T(1,128)S(1)}, u32[]{:S(2)}, u32[]{:S(2)}) %all-to-all-start.3) | async-done | bytes 81952 | tf_op jit(solution)/shard_map/all_to_all | solution.py:364
  57.1 0.6 %copy.11 = f32[1,1,2,640]{3,1,2,0:T(1,128)} copy(f32[1,1,2,640]{3,2,1,0:T(2,128)S(1)} %bitcast.17) | data formatting | bytes 10240
  (5 shorter events, 0.1 us)
Async XLA Ops:
  0.6 15.0 %collective-permute-start = (bf16[128,1280]{1,0:T(8,128)(2,1)}, bf16[128,1280]{1,0:T(8,128)(2,1)S(1)}, u32[]{:S(2)}, u32[]{:S(2)}) collective-permute-start(bf16[128,1280]{1,0:T(8,128)(2,1)} %tokens_ref.1), channel_id=1, source_target_pairs={{0,8},{8,0},{16,24},{24,16},{1,9},{9,1},{17,25},{25,17},{2,10},{10... | collective-permute-start | bytes 983048 | tf_op jit(solution)/shard_map/ppermute | solution.py:300
  1.1 14.5 %collective-permute-start.1 = (bf16[128,1280]{1,0:T(8,128)(2,1)}, bf16[128,1280]{1,0:T(8,128)(2,1)S(1)}, u32[]{:S(2)}, u32[]{:S(2)}) collective-permute-start(bf16[128,1280]{1,0:T(8,128)(2,1)} %cotangent_ref.1), channel_id=1, source_target_pairs={{0,8},{8,0},{16,24},{24,16},{1,9},{9,1},{17,25},{25,17},{2,10},{10... | collective-permute-start | bytes 983048 | tf_op jit(solution)/shard_map/ppermute | solution.py:301
  1.2 0.7 %copy-start.2 = (bf16[1280,1]{0,1:T(2,128)(2,1)S(1)}, bf16[1280,1]{0,1:T(2,128)(2,1)}, u32[]{:S(2)}) copy-start(bf16[1280,1]{0,1:T(2,128)(2,1)} %param.6) | copy-start | bytes 7684
  34.2 11.2 %all-to-all-start.2 = ((bf16[32,24,128]{2,1,0:T(8,128)(2,1)}), bf16[32,24,128]{2,1,0:T(8,128)(2,1)S(1)}, u32[]{:S(2)}, u32[]{:S(2)}) async-start(bf16[32,24,128]{2,1,0:T(8,128)(2,1)} %get-tuple-element.21), calls=%async_computation.2 | async-start | bytes 393216 | tf_op jit(solution)/shard_map/all_to_all | solution.py:346
  36.9 8.5 %copy-start = (bf16[128,1280]{1,0:T(8,128)(2,1)S(1)}, bf16[128,1280]{1,0:T(8,128)(2,1)}, u32[]{:S(2)}) copy-start(bf16[128,1280]{1,0:T(8,128)(2,1)} %tokens_ref.1) | copy-start | bytes 983044
  36.9 8.5 %copy-start.1 = (bf16[128,1280]{1,0:T(8,128)(2,1)S(1)}, bf16[128,1280]{1,0:T(8,128)(2,1)}, u32[]{:S(2)}) copy-start(bf16[128,1280]{1,0:T(8,128)(2,1)} %cotangent_ref.1) | copy-start | bytes 983044
  46.7 10.4 %all-to-all-start.3 = ((f32[32,1,640]{2,1,0:T(1,128)}), f32[32,1,640]{2,1,0:T(1,128)S(1)}, u32[]{:S(2)}, u32[]{:S(2)}) async-start(f32[32,1,640]{2,1,0:T(1,128)} %get-tuple-element.28), calls=%async_computation.3 | async-start | bytes 163840 | tf_op jit(solution)/shard_map/all_to_all | solution.py:364

commit v5 on v4

--- a/solution.py
+++ b/solution.py
@@ -50,10 +50,6 @@
 def from_lanes(row, lane, first, count):
     keep = (lane >= first) & (lane < first + count)
     return jnp.sum(jnp.where(keep, row, 0.0), axis=1, keepdims=True)
-
-
-def block_of(rows):
-    return 256 if rows % 256 == 0 else rows
 
 
 def lanes_of(rows):
@@ -141,20 +137,9 @@
 
 
 def expert_kernel(
-    exp_size, parts_ref, w_in_far_ref, w_out_far_ref,
-    message_ref, slot_in_ref, slot_out_grad_ref, activation_ref, pre_grad_ref,
-    w_in_ref, w_out_ref, parts_rows_ref, rows_ref, sems,
+    exp_size, parts_ref, w_in_ref, w_out_ref,
+    message_ref, slot_in_ref, slot_out_grad_ref, hidden_rows_ref, parts_rows_ref, rows_ref,
 ):
-    hidden = w_in_ref.shape[0]
-    block_rows = block_of(hidden)
-    blocks = [pl.ds(i * block_rows, block_rows) for i in range(hidden // block_rows)]
-    copies = [
-        [pltpu.make_async_copy(far.at[rows], near.at[rows], sems.at[w, i]) for i, rows in enumerate(blocks)]
-        for w, (far, near) in enumerate([(w_in_far_ref, w_in_ref), (w_out_far_ref, w_out_ref)])
-    ]
-    for pair in copies:
-        for copy in pair:
-            copy.start()
     devices = parts_ref.shape[0]
     seq_size = devices // exp_size
     width = w_in_ref.shape[1]
@@ -188,20 +173,12 @@
     slot_in_ref[...] = slot_in
     slot_out_grad_ref[...] = slot_out_grad
 
-    def times_rows(row, copies_of, w_ref):
-        outs = []
-        for copy, rows in zip(copies_of, blocks):
-            copy.wait()
-            outs.append(dot(row, w_ref[rows, :], 1, 1))
-        return jnp.concatenate(outs, axis=1)
-
-    pre_act = times_rows(slot_in, copies[0], w_in_ref)
-    act_grad = times_rows(slot_out_grad, copies[1], w_out_ref)
+    pre_act = dot(slot_in, w_in_ref[...], 1, 1)
+    act_grad = dot(slot_out_grad, w_out_ref[...], 1, 1)
     value, slope = gelu_parts(pre_act)
     activation = value.astype(jnp.bfloat16)
     pre_grad = (act_grad * slope).astype(jnp.bfloat16)
-    activation_ref[...] = activation
-    pre_grad_ref[...] = pre_grad
+    hidden_rows_ref[...] = jnp.concatenate([value, act_grad * slope], axis=0).astype(jnp.bfloat16)
     out_part = dot(activation, w_out_ref[...], 1, 0)
     grad_part = dot(pre_grad, w_in_ref[...], 1, 0).astype(jnp.bfloat16).astype(jnp.float32)
     correction = jnp.sum(slot_row * grad_part, axis=1, keepdims=True)
@@ -299,6 +276,8 @@
     keys = lax.all_to_all(key_message, "exp", 0, 0, tiled=True)
     tokens_other = lax.ppermute(tokens, "seq", swap)
     cotangent_other = lax.ppermute(cotangent, "seq", swap)
+    w_in_other = lax.ppermute(w_in, "seq", swap)
+    w_out_other = lax.ppermute(w_out, "seq", swap)
 
     sum_rows = padded(3 * half // LANES + 1, 16)
     message, logits, comb_prob, keys_all = call(
@@ -323,27 +302,20 @@
     parts = lax.all_to_all(message, both, 0, 0, tiled=True)
 
     row_count = padded(2 * width // LANES + 1, 8)
-    message, slot_in, slot_out_grad, activation, pre_grad = call(
+    message, slot_in, slot_out_grad, hidden_rows = call(
         functools.partial(expert_kernel, exp_size),
         (
             shape((devices, row_count, LANES), bf16),
             shape((1, width), bf16),
             shape((1, width), bf16),
-            shape((1, hidden), bf16),
-            shape((1, hidden), bf16),
-        ),
-        [
-            pltpu.VMEM((hidden, width), bf16),
-            pltpu.VMEM((hidden, width), bf16),
-            pltpu.VMEM((devices, sum_rows, LANES), f32),
-            pltpu.VMEM((row_count, LANES), f32),
-            pltpu.SemaphoreType.DMA((2, hidden // block_of(hidden))),
-        ],
-        [parts, w_in[0], w_out[0]],
-        unplaced=2,
-        room=(64 * 1024 - 13300) * 1024,
+            shape((2, hidden), bf16),
+        ),
+        [pltpu.VMEM((devices, sum_rows, LANES), f32), pltpu.VMEM((row_count, LANES), f32)],
+        [parts, w_in_other[0], w_out_other[0]],
     )
     gathered = lax.all_to_all(message, both, 0, 0, tiled=True)
+    own_rows = lax.ppermute(hidden_rows, "seq", swap)
+    activation, pre_grad = own_rows[:1], own_rows[1:]
     w_out_grad = (
         activation.astype(f32)[:, :, None] * slot_out_grad.astype(f32)[:, None, :]
     ).astype(bf16)

time: 58.1 us -> 56.2 us (0.967)
  Pallas kernels: 10.3 us -> 6.5 us
  blocking collectives: 23.3 us -> 24.8 us
  starting transfers between devices: 6.15 us -> 6.82 us
    pallas_call x4, Pallas kernels: 10.3 us -> 6.5 us  [call(): pl.pallas_call(kernel, out_shape=out_shape, in_specs=[pl.BlockSpec(memory...]
    all_to_all x1, blocking collectives: 9.56 us -> 11.1 us  [local(): parts = lax.all_to_all(message, both, 0, 0, tiled=True)]
    all_to_all x1, waiting for transfers between devices: 4.21 us -> 3.01 us  [local(): gathered = lax.all_to_all(message, both, 0, 0, tiled=True)]
    ppermute x0 -> x3, waiting for transfers between devices: none -> 1.01 us  [the longest x1 1.01 us: local(): own_rows = lax.ppermute(hidden_rows, 'seq', swap)]
    ppermute x0 -> x3, starting transfers between devices: none -> 0.79 us  [the longest x1 0.52 us: local(): w_in_other = lax.ppermute(w_in, 'seq', swap)]
  transfers between devices with their start and end apart: 4 -> 7, of which waited for: 2 -> 3; matrix products, arithmetic and copies ran while one was open for 11% -> 12% of each run, Pallas kernels for 0% -> 3%
where the time goes in v5:
time: 56.2 us; the launch traced here: 55.9 us
  blocking collectives  24.8 us (44%)
  waiting for transfers between devices  9.15 us (16%)
  starting transfers between devices  6.82 us (12%)
  Pallas kernels  6.5 us (12%)
  other arithmetic  4.33 us (8%)
  matrix products  2.31 us (4%)
  local copies, waits for them, and re-layouts  1.31 us (2%)
  between operations  0.7 us (1%)
    all_to_all x1, blocking collectives, local(): keys = lax.all_to_all(key_message, 'exp', 0, 0, tiled=True)  13.7 us
    all_to_all x1, blocking collectives, local(): parts = lax.all_to_all(message, both, 0, 0, tiled=True)  11.1 us
    pallas_call x4, Pallas kernels, call(): pl.pallas_call(kernel, out_shape=out_shape, in_specs=[pl.BlockSpec(memory...  6.5 us
    all_to_all x1, waiting for transfers between devices, local(): keys_parts = lax.all_to_all(message, both, 0, 0, tiled=True)  5.11 us
    all_to_all x1, waiting for transfers between devices, local(): gathered = lax.all_to_all(message, both, 0, 0, tiled=True)  3.01 us
    all_to_all x1, starting transfers between devices, local(): keys_parts = lax.all_to_all(message, both, 0, 0, tiled=True)  2.95 us
    all_to_all x1, starting transfers between devices, local(): gathered = lax.all_to_all(message, both, 0, 0, tiled=True)  2.58 us
    dot_general x3, matrix products, dot(): lax.dot_general(left, right, (((left_dim,), (right_dim,)), ((), ())), pre...  2.31 us
  transfers between devices with their start and end apart: 7, of which 3 were waited for; matrix products, arithmetic and copies ran while one was open for 12% of the time, Pallas kernels for 3%

profile of v5, /device:TPU:0, one launch (start us, length us, event | category | flops | bytes accessed | tf_op | source)
XLA Modules:
  0.0 55.9 jit_solution(5256217339989474561)
XLA Ops:
  0.6 0.5 collective-permute-start.2
  1.1 0.1 collective-permute-start.3
  1.2 0.4 collective-permute-start
  1.7 0.1 collective-permute-start.1
  1.7 0.0 copy-start.2
  1.7 0.7 %copy-done.2 = bf16[1280,1]{0,1:T(2,128)(2,1)S(1)} copy-done((bf16[1280,1]{0,1:T(2,128)(2,1)S(1)}, bf16[1280,1]{0,1:T(2,128)(2,1)}, u32[]{:S(2)}) %copy-start.2) | copy-done | bytes 2584
  2.4 13.7 %all_to_all.20.keys_ref = bf16[8,16,128]{2,1,0:T(8,128)(2,1)S(1)} all-to-all(bf16[8,16,128]{2,1,0:T(8,128)(2,1)S(1)} %shard_map.92), channel_id=1, replica_groups=mesh['seq'=4,'exp'=8] {'exp'}, dimensions={0} | all-to-all | bytes 65536 | tf_op jit(solution)/shard_map/all_to_all | solution.py:276
  16.2 0.0 collective-permute-done.tokens_other_ref
  16.2 0.0 collective-permute-done.1.cotangent_other_ref
  16.2 1.6 %shard_map.93 = (bf16[32,16,128]{2,1,0:T(8,128)(2,1)S(1)}, f32[8,256]{1,0:T(8,128)S(1)}, f32[8,256]{1,0:T(8,128)S(1)}, bf16[8,1280]{1,0:T(8,128)(2,1)S(1)}) custom-call(bf16[8,16,128]{2,1,0:T(8,128)(2,1)S(1)} %all_to_all.20.keys_ref, bf16[128,1280]{1,0:T(8,128)(2,1)S(1)} %collective-permute-done.tokens_other_ref, ...), custom_call_target="tpu_custom_call" | custom-call | tf_op jit(solution)/shard_map/pallas_call | solution.py:61
  17.8 11.1 %all_to_all.21.parts_ref = bf16[32,16,128]{2,1,0:T(8,128)(2,1)S(1)} all-to-all(bf16[32,16,128]{2,1,0:T(8,128)(2,1)S(1)} %get-tuple-element.19), channel_id=1, replica_groups=mesh['seq'=4,'exp'=8] {'seq','exp'}, dimensions={0} | all-to-all | bytes 262144 | tf_op jit(solution)/shard_map/all_to_all | solution.py:302
  28.8 0.0 collective-permute-done.2
  28.8 0.0 collective-permute-done.3
  28.9 3.5 %shard_map.94 = (bf16[32,24,128]{2,1,0:T(8,128)(2,1)}, bf16[1,1280]{1,0:T(2,128)(2,1)S(1)}, bf16[1,1280]{1,0:T(2,128)(2,1)S(1)}, bf16[2,1280]{1,0:T(2,128)(2,1)S(1)}) custom-call(bf16[32,16,128]{2,1,0:T(8,128)(2,1)S(1)} %all_to_all.21.parts_ref, bf16[1280,1280]{1,0:T(8,128)(2,1)S(1)} %bitcast.13, bf16[1280,1280]{1,0:T(8,128)(2,1)S(1)} %bitcast.14), custom_call_target="tpu_custom_call" | custom-call | tf_op jit(solution)/shard_map/pallas_call | solution.py:61
  32.4 2.6 %all-to-all-start.2 = ((bf16[32,24,128]{2,1,0:T(8,128)(2,1)}), bf16[32,24,128]{2,1,0:T(8,128)(2,1)S(1)}, u32[]{:S(2)}, u32[]{:S(2)}) async-start(bf16[32,24,128]{2,1,0:T(8,128)(2,1)} %get-tuple-element.20), calls=%async_computation.2 | async-start | bytes 393216 | tf_op jit(solution)/shard_map/all_to_all | solution.py:316
  35.0 0.2 collective-permute-start.4
  35.2 1.0 %collective-permute-done.4 = bf16[2,1280]{1,0:T(2,128)(2,1)S(1)} collective-permute-done((bf16[2,1280]{1,0:T(2,128)(2,1)S(1)}, bf16[2,1280]{1,0:T(2,128)(2,1)S(1)}, u32[]{:S(2)}, u32[]{:S(2)}) %collective-permute-start.4) | collective-permute-done | bytes 5152 | tf_op jit(solution)/shard_map/ppermute | solution.py:317
  36.2 0.0 copy-start
  36.2 0.0 copy-start.1
  36.3 2.1 %multiply_convert_fusion = bf16[1,1280,1280]{2,1,0:T(8,128)(2,1)} fusion(f32[1280]{0:T(1024)S(1)} %get-tuple-element.33, f32[1280]{0:T(1024)S(1)} %get-tuple-element.31), kind=kLoop, calls=%fused_computation | loop fusion | flops 3276800 | bytes 3287040 | tf_op jit(solution)/shard_map/convert_element_type | solution.py:321
  38.4 2.1 %multiply_convert_fusion.1 = bf16[1,1280,1280]{2,1,0:T(8,128)(2,1)} fusion(f32[1280]{0:T(1024)S(1)} %get-tuple-element.34, f32[1280]{0:T(1024)S(1)} %get-tuple-element.32), kind=kLoop, calls=%fused_computation.1 | loop fusion | flops 3276800 | bytes 3287040 | tf_op jit(solution)/shard_map/convert_element_type | solution.py:322
  40.5 3.0 %all-to-all-done.2.parts_ref = bf16[32,24,128]{2,1,0:T(8,128)(2,1)S(1)} async-done(((bf16[32,24,128]{2,1,0:T(8,128)(2,1)}), bf16[32,24,128]{2,1,0:T(8,128)(2,1)S(1)}, u32[]{:S(2)}, u32[]{:S(2)}) %all-to-all-start.2) | async-done | bytes 196640 | tf_op jit(solution)/shard_map/all_to_all | solution.py:316
  43.5 0.0 copy-done
  43.5 0.0 copy-done.1
  43.5 1.3 %shard_map.95 = (f32[32,1,640]{2,1,0:T(1,128)}, bf16[8,1280]{1,0:T(8,128)(2,1)S(1)}, bf16[8,1280]{1,0:T(8,128)(2,1)S(1)}, bf16[8,128]{1,0:T(8,128)(2,1)S(1)}, bf16[8,128]{1,0:T(8,128)(2,1)S(1)}) custom-call(bf16[32,24,128]{2,1,0:T(8,128)(2,1)S(1)} %all-to-all-done.2.parts_ref, f32[8,256]{1,0:T(8,128)S(1)} %get-tuple-element.21.logits_ref, ...), custom_call_target="tpu_custom_call" | custom-call | tf_op jit(solution)/shard_map/pallas_call | solution.py:61
  44.9 2.9 %all-to-all-start.3 = ((f32[32,1,640]{2,1,0:T(1,128)}), f32[32,1,640]{2,1,0:T(1,128)S(1)}, u32[]{:S(2)}, u32[]{:S(2)}) async-start(f32[32,1,640]{2,1,0:T(1,128)} %get-tuple-element.27), calls=%async_computation.3 | async-start | bytes 163840 | tf_op jit(solution)/shard_map/all_to_all | solution.py:336
  47.8 0.3 fusion.3
  48.1 1.0 %fusion = bf16[128,1280]{1,0:T(8,128)(2,1)} fusion(f32[128,1280]{1,0:T(8,128)S(1)} %fusion.3, bf16[8,128]{1,0:T(8,128)(2,1)S(1)} %get-tuple-element.23, bf16[8,1280]{1,0:T(8,128)(2,1)S(1)} %get-tuple-element.24), kind=kOutput, calls=%fused_computation.3 | convolution fusion | flops 2949120 | bytes 1005568 | tf_op jit(solution)/shard_map/dot_general | solution.py:16
  49.1 1.0 %convolution_convert_fusion = bf16[128,1280]{1,0:T(8,128)(2,1)} fusion(bf16[8,1280]{1,0:T(8,128)(2,1)S(1)} %get-tuple-element.22, f32[8,256]{1,0:T(8,128)S(1)} %get-tuple-element.18.comb_ref), kind=kOutput, calls=%fused_computation.4 | convolution fusion | flops 2785280 | bytes 350208 | tf_op jit(solution)/shard_map/dot_general | solution.py:16
  50.1 5.1 %all-to-all-done.3 = f32[32,1,640]{2,1,0:T(1,128)S(1)} async-done(((f32[32,1,640]{2,1,0:T(1,128)}), f32[32,1,640]{2,1,0:T(1,128)S(1)}, u32[]{:S(2)}, u32[]{:S(2)}) %all-to-all-start.3) | async-done | bytes 81952 | tf_op jit(solution)/shard_map/all_to_all | solution.py:336
  55.3 0.6 %copy.11 = f32[1,1,2,640]{3,1,2,0:T(1,128)} copy(f32[1,1,2,640]{3,2,1,0:T(2,128)S(1)} %bitcast.17) | data formatting | bytes 10240
  (5 shorter events, 0.1 us)
Async XLA Ops:
  0.6 28.2 %collective-permute-start.2 = (bf16[1,1280,1280]{2,1,0:T(8,128)(2,1)}, bf16[1,1280,1280]{2,1,0:T(8,128)(2,1)S(1)}, u32[]{:S(2)}, u32[]{:S(2)}) collective-permute-start(bf16[1,1280,1280]{2,1,0:T(8,128)(2,1)} %param.7), channel_id=1, source_target_pairs={{0,8},{8,0},{16,24},{24,16},{1,9},{9,1},{17,25},{25,17},{2,10},{10... | collective-permute-start | bytes 9830408 | tf_op jit(solution)/shard_map/ppermute | solution.py:279
  1.1 27.7 %collective-permute-start.3 = (bf16[1,1280,1280]{2,1,0:T(8,128)(2,1)}, bf16[1,1280,1280]{2,1,0:T(8,128)(2,1)S(1)}, u32[]{:S(2)}, u32[]{:S(2)}) collective-permute-start(bf16[1,1280,1280]{2,1,0:T(8,128)(2,1)} %param.8), channel_id=1, source_target_pairs={{0,8},{8,0},{16,24},{24,16},{1,9},{9,1},{17,25},{25,17},{2,10},{10... | collective-permute-start | bytes 9830408 | tf_op jit(solution)/shard_map/ppermute | solution.py:280
  1.2 14.9 %collective-permute-start = (bf16[128,1280]{1,0:T(8,128)(2,1)}, bf16[128,1280]{1,0:T(8,128)(2,1)S(1)}, u32[]{:S(2)}, u32[]{:S(2)}) collective-permute-start(bf16[128,1280]{1,0:T(8,128)(2,1)} %tokens_ref.1), channel_id=1, source_target_pairs={{0,8},{8,0},{16,24},{24,16},{1,9},{9,1},{17,25},{25,17},{2,10},{10... | collective-permute-start | bytes 983048 | tf_op jit(solution)/shard_map/ppermute | solution.py:277
  1.7 14.5 %collective-permute-start.1 = (bf16[128,1280]{1,0:T(8,128)(2,1)}, bf16[128,1280]{1,0:T(8,128)(2,1)S(1)}, u32[]{:S(2)}, u32[]{:S(2)}) collective-permute-start(bf16[128,1280]{1,0:T(8,128)(2,1)} %cotangent_ref.1), channel_id=1, source_target_pairs={{0,8},{8,0},{16,24},{24,16},{1,9},{9,1},{17,25},{25,17},{2,10},{10... | collective-permute-start | bytes 983048 | tf_op jit(solution)/shard_map/ppermute | solution.py:278
  1.7 0.7 %copy-start.2 = (bf16[1280,1]{0,1:T(2,128)(2,1)S(1)}, bf16[1280,1]{0,1:T(2,128)(2,1)}, u32[]{:S(2)}) copy-start(bf16[1280,1]{0,1:T(2,128)(2,1)} %param.6) | copy-start | bytes 7684
  32.4 11.1 %all-to-all-start.2 = ((bf16[32,24,128]{2,1,0:T(8,128)(2,1)}), bf16[32,24,128]{2,1,0:T(8,128)(2,1)S(1)}, u32[]{:S(2)}, u32[]{:S(2)}) async-start(bf16[32,24,128]{2,1,0:T(8,128)(2,1)} %get-tuple-element.20), calls=%async_computation.2 | async-start | bytes 393216 | tf_op jit(solution)/shard_map/all_to_all | solution.py:316
  35.0 1.2 %collective-permute-start.4 = (bf16[2,1280]{1,0:T(2,128)(2,1)S(1)}, bf16[2,1280]{1,0:T(2,128)(2,1)S(1)}, u32[]{:S(2)}, u32[]{:S(2)}) collective-permute-start(bf16[2,1280]{1,0:T(2,128)(2,1)S(1)} %get-tuple-element.28), channel_id=1, source_target_pairs={{0,8},{8,0},{16,24},{24,16},{1,9},{9,1},{17,25},{25,17},{2,10},{10... | collective-permute-start | bytes 15368 | tf_op jit(solution)/shard_map/ppermute | solution.py:317
  36.2 7.3 %copy-start = (bf16[128,1280]{1,0:T(8,128)(2,1)S(1)}, bf16[128,1280]{1,0:T(8,128)(2,1)}, u32[]{:S(2)}) copy-start(bf16[128,1280]{1,0:T(8,128)(2,1)} %tokens_ref.1) | copy-start | bytes 983044
  36.2 7.3 %copy-start.1 = (bf16[128,1280]{1,0:T(8,128)(2,1)S(1)}, bf16[128,1280]{1,0:T(8,128)(2,1)}, u32[]{:S(2)}) copy-start(bf16[128,1280]{1,0:T(8,128)(2,1)} %cotangent_ref.1) | copy-start | bytes 983044
  44.9 10.4 %all-to-all-start.3 = ((f32[32,1,640]{2,1,0:T(1,128)}), f32[32,1,640]{2,1,0:T(1,128)S(1)}, u32[]{:S(2)}, u32[]{:S(2)}) async-start(f32[32,1,640]{2,1,0:T(1,128)} %get-tuple-element.27), calls=%async_computation.3 | async-start | bytes 163840 | tf_op jit(solution)/shard_map/all_to_all | solution.py:336

commit v6 on v5

--- a/solution.py
+++ b/solution.py
@@ -10,6 +10,7 @@
 tanh_coeff = 0.7978845608028654
 cubic_coeff = 0.044715
 LANES = 128
+VECTOR_SHARE = 0.65
 
 
 def dot(left, right, left_dim, right_dim):
@@ -134,6 +135,41 @@
     block = rows_ref[...].astype(jnp.bfloat16)
     for q in range(message_ref.shape[0] // slots):
         message_ref[q * slots : (q + 1) * slots] = block
+
+
+def lane_sums_times(row, w_ref, first, count):
+    row_chunks = [
+        row[:, j * LANES : (j + 1) * LANES].astype(jnp.float32) for j in range(row.shape[1] // LANES)
+    ]
+    highs, lows = [], []
+    for start in range(first, first + count, 16):
+        total = None
+        for j, chunk in enumerate(row_chunks):
+            term = w_ref[start : start + 16, j * LANES : (j + 1) * LANES].astype(jnp.float32) * chunk
+            total = term if total is None else total + term
+        high = total.astype(jnp.bfloat16)
+        highs.append(high)
+        lows.append((total - high.astype(jnp.float32)).astype(jnp.bfloat16))
+    ones = jnp.ones((8, LANES), jnp.bfloat16)
+    sums = dot(ones, jnp.concatenate(highs, axis=0), 1, 1) + dot(ones, jnp.concatenate(lows, axis=0), 1, 1)
+    return sums[:1]
+
+
+def rows_times(pairs):
+    results, taken = [], 0
+    for row, w_ref in pairs:
+        rows = w_ref.shape[0]
+        block = LANES if rows % LANES == 0 else rows
+        outs = []
+        for first in range(0, rows, block):
+            taken += VECTOR_SHARE
+            if taken >= 1.0 and block == LANES:
+                taken -= 1.0
+                outs.append(lane_sums_times(row, w_ref, first, block))
+            else:
+                outs.append(dot(row, w_ref[first : first + block, :], 1, 1))
+        results.append(jnp.concatenate(outs, axis=1))
+    return results
 
 
 def expert_kernel(
@@ -173,8 +209,7 @@
     slot_in_ref[...] = slot_in
     slot_out_grad_ref[...] = slot_out_grad
 
-    pre_act = dot(slot_in, w_in_ref[...], 1, 1)
-    act_grad = dot(slot_out_grad, w_out_ref[...], 1, 1)
+    pre_act, act_grad = rows_times([(slot_in, w_in_ref), (slot_out_grad, w_out_ref)])
     value, slope = gelu_parts(pre_act)
     activation = value.astype(jnp.bfloat16)
     pre_grad = (act_grad * slope).astype(jnp.bfloat16)
@@ -273,11 +308,12 @@
         [pltpu.VMEM((key_rows, LANES), f32)],
         [slot_keys.T],
     )
-    keys = lax.all_to_all(key_message, "exp", 0, 0, tiled=True)
     tokens_other = lax.ppermute(tokens, "seq", swap)
     cotangent_other = lax.ppermute(cotangent, "seq", swap)
-    w_in_other = lax.ppermute(w_in, "seq", swap)
-    w_out_other = lax.ppermute(w_out, "seq", swap)
+    keys = lax.all_to_all(key_message, "exp", 0, 0, tiled=True)
+    keys, w_in_late, w_out_late, tokens_other, cotangent_other = lax.optimization_barrier((keys, w_in, w_out, tokens_other, cotangent_other))
+    w_in_other = lax.ppermute(w_in_late, "seq", swap)
+    w_out_other = lax.ppermute(w_out_late, "seq", swap)
 
     sum_rows = padded(3 * half // LANES + 1, 16)
     message, logits, comb_prob, keys_all = call(

time: 56.2 us -> 54.2 us (0.964)
  blocking collectives: 24.8 us -> 23.3 us
    all_to_all x1, blocking collectives: 11.1 us -> 9.56 us  [local(): parts = lax.all_to_all(message, both, 0, 0, tiled=True)]
where the time goes in v6:
time: 54.2 us; the launch traced here: 53.9 us
  blocking collectives  23.3 us (43%)
  waiting for transfers between devices  9.15 us (17%)
  starting transfers between devices  6.82 us (13%)
  Pallas kernels  5.98 us (11%)
  other arithmetic  4.33 us (8%)
  matrix products  2.31 us (4%)
  local copies, waits for them, and re-layouts  1.31 us (2%)
  between operations  0.71 us (1%)
    all_to_all x1, blocking collectives, local(): keys = lax.all_to_all(key_message, 'exp', 0, 0, tiled=True)  13.7 us
    all_to_all x1, blocking collectives, local(): parts = lax.all_to_all(message, both, 0, 0, tiled=True)  9.56 us
    pallas_call x4, Pallas kernels, call(): pl.pallas_call(kernel, out_shape=out_shape, in_specs=[pl.BlockSpec(memory...  5.98 us
    all_to_all x1, waiting for transfers between devices, local(): keys_parts = lax.all_to_all(message, both, 0, 0, tiled=True)  5.11 us
    all_to_all x1, waiting for transfers between devices, local(): gathered = lax.all_to_all(message, both, 0, 0, tiled=True)  3.01 us
    all_to_all x1, starting transfers between devices, local(): keys_parts = lax.all_to_all(message, both, 0, 0, tiled=True)  2.95 us
    all_to_all x1, starting transfers between devices, local(): gathered = lax.all_to_all(message, both, 0, 0, tiled=True)  2.58 us
    dot_general x3, matrix products, dot(): lax.dot_general(left, right, (((left_dim,), (right_dim,)), ((), ())), pre...  2.31 us
  transfers between devices with their start and end apart: 7, of which 3 were waited for; matrix products, arithmetic and copies ran while one was open for 12% of the time, Pallas kernels for 3%

profile of v6, /device:TPU:0, one launch (start us, length us, event | category | flops | bytes accessed | tf_op | source)
XLA Modules:
  0.0 53.9 jit_solution(1378807150928244334)
XLA Ops:
  0.6 0.5 collective-permute-start
  1.1 0.1 collective-permute-start.1
  1.2 0.0 copy-start.2
  1.2 0.7 %copy-done.2 = bf16[1280,1]{0,1:T(2,128)(2,1)S(1)} copy-done((bf16[1280,1]{0,1:T(2,128)(2,1)S(1)}, bf16[1280,1]{0,1:T(2,128)(2,1)}, u32[]{:S(2)}) %copy-start.2) | copy-done | bytes 2584
  1.9 13.7 %all_to_all.20.keys_ref = bf16[8,16,128]{2,1,0:T(8,128)(2,1)S(1)} all-to-all(bf16[8,16,128]{2,1,0:T(8,128)(2,1)S(1)} %shard_map.92), channel_id=1, replica_groups=mesh['seq'=4,'exp'=8] {'exp'}, dimensions={0} | all-to-all | bytes 65536 | tf_op jit(solution)/shard_map/all_to_all | solution.py:313
  15.6 0.0 collective-permute-done.tokens_other_ref
  15.6 0.0 collective-permute-done.1.cotangent_other_ref
  15.7 0.0 collective-permute-start.2
  15.7 0.5 collective-permute-start.3
  16.2 1.6 %shard_map.93 = (bf16[32,16,128]{2,1,0:T(8,128)(2,1)S(1)}, f32[8,256]{1,0:T(8,128)S(1)}, f32[8,256]{1,0:T(8,128)S(1)}, bf16[8,1280]{1,0:T(8,128)(2,1)S(1)}) custom-call(bf16[8,16,128]{2,1,0:T(8,128)(2,1)S(1)} %all_to_all.20.keys_ref, bf16[128,1280]{1,0:T(8,128)(2,1)S(1)} %collective-permute-done.tokens_other_ref, ...), custom_call_target="tpu_custom_call" | custom-call | tf_op jit(solution)/shard_map/pallas_call | solution.py:62
  17.8 9.6 %all_to_all.21.parts_ref = bf16[32,16,128]{2,1,0:T(8,128)(2,1)S(1)} all-to-all(bf16[32,16,128]{2,1,0:T(8,128)(2,1)S(1)} %get-tuple-element.27), channel_id=1, replica_groups=mesh['seq'=4,'exp'=8] {'seq','exp'}, dimensions={0} | all-to-all | bytes 262144 | tf_op jit(solution)/shard_map/all_to_all | solution.py:338
  27.3 0.0 collective-permute-done.2
  27.4 0.0 collective-permute-done.3
  27.4 3.0 %shard_map.94 = (bf16[32,24,128]{2,1,0:T(8,128)(2,1)}, bf16[1,1280]{1,0:T(2,128)(2,1)S(1)}, bf16[1,1280]{1,0:T(2,128)(2,1)S(1)}, bf16[2,1280]{1,0:T(2,128)(2,1)S(1)}) custom-call(bf16[32,16,128]{2,1,0:T(8,128)(2,1)S(1)} %all_to_all.21.parts_ref, bf16[1280,1280]{1,0:T(8,128)(2,1)S(1)} %bitcast.13, bf16[1280,1280]{1,0:T(8,128)(2,1)S(1)} %bitcast.14), custom_call_target="tpu_custom_call" | custom-call | tf_op jit(solution)/shard_map/pallas_call | solution.py:62
  30.4 2.6 %all-to-all-start.2 = ((bf16[32,24,128]{2,1,0:T(8,128)(2,1)}), bf16[32,24,128]{2,1,0:T(8,128)(2,1)S(1)}, u32[]{:S(2)}, u32[]{:S(2)}) async-start(bf16[32,24,128]{2,1,0:T(8,128)(2,1)} %get-tuple-element.30), calls=%async_computation.2 | async-start | bytes 393216 | tf_op jit(solution)/shard_map/all_to_all | solution.py:352
  32.9 0.2 collective-permute-start.4
  33.2 1.0 %collective-permute-done.4 = bf16[2,1280]{1,0:T(2,128)(2,1)S(1)} collective-permute-done((bf16[2,1280]{1,0:T(2,128)(2,1)S(1)}, bf16[2,1280]{1,0:T(2,128)(2,1)S(1)}, u32[]{:S(2)}, u32[]{:S(2)}) %collective-permute-start.4) | collective-permute-done | bytes 5152 | tf_op jit(solution)/shard_map/ppermute | solution.py:353
  34.2 0.0 copy-start
  34.2 0.0 copy-start.1
  34.2 2.1 %multiply_convert_fusion = bf16[1,1280,1280]{2,1,0:T(8,128)(2,1)} fusion(f32[1280]{0:T(1024)S(1)} %get-tuple-element.43, f32[1280]{0:T(1024)S(1)} %get-tuple-element.41), kind=kLoop, calls=%fused_computation | loop fusion | flops 3276800 | bytes 3287040 | tf_op jit(solution)/shard_map/convert_element_type | solution.py:357
  36.4 2.1 %multiply_convert_fusion.1 = bf16[1,1280,1280]{2,1,0:T(8,128)(2,1)} fusion(f32[1280]{0:T(1024)S(1)} %get-tuple-element.44, f32[1280]{0:T(1024)S(1)} %get-tuple-element.42), kind=kLoop, calls=%fused_computation.1 | loop fusion | flops 3276800 | bytes 3287040 | tf_op jit(solution)/shard_map/convert_element_type | solution.py:358
  38.5 3.0 %all-to-all-done.2.parts_ref = bf16[32,24,128]{2,1,0:T(8,128)(2,1)S(1)} async-done(((bf16[32,24,128]{2,1,0:T(8,128)(2,1)}), bf16[32,24,128]{2,1,0:T(8,128)(2,1)S(1)}, u32[]{:S(2)}, u32[]{:S(2)}) %all-to-all-start.2) | async-done | bytes 196640 | tf_op jit(solution)/shard_map/all_to_all | solution.py:352
  41.5 0.0 copy-done
  41.5 0.0 copy-done.1
  41.5 1.3 %shard_map.95 = (f32[32,1,640]{2,1,0:T(1,128)}, bf16[8,1280]{1,0:T(8,128)(2,1)S(1)}, bf16[8,1280]{1,0:T(8,128)(2,1)S(1)}, bf16[8,128]{1,0:T(8,128)(2,1)S(1)}, bf16[8,128]{1,0:T(8,128)(2,1)S(1)}) custom-call(bf16[32,24,128]{2,1,0:T(8,128)(2,1)S(1)} %all-to-all-done.2.parts_ref, f32[8,256]{1,0:T(8,128)S(1)} %get-tuple-element.31.logits_ref, ...), custom_call_target="tpu_custom_call" | custom-call | tf_op jit(solution)/shard_map/pallas_call | solution.py:62
  42.8 2.9 %all-to-all-start.3 = ((f32[32,1,640]{2,1,0:T(1,128)}), f32[32,1,640]{2,1,0:T(1,128)S(1)}, u32[]{:S(2)}, u32[]{:S(2)}) async-start(f32[32,1,640]{2,1,0:T(1,128)} %get-tuple-element.37), calls=%async_computation.3 | async-start | bytes 163840 | tf_op jit(solution)/shard_map/all_to_all | solution.py:372
  45.8 0.3 fusion.3
  46.1 1.0 %fusion = bf16[128,1280]{1,0:T(8,128)(2,1)} fusion(f32[128,1280]{1,0:T(8,128)S(1)} %fusion.3, bf16[8,128]{1,0:T(8,128)(2,1)S(1)} %get-tuple-element.35, bf16[8,1280]{1,0:T(8,128)(2,1)S(1)} %get-tuple-element.36), kind=kOutput, calls=%fused_computation.3 | convolution fusion | flops 2949120 | bytes 1005568 | tf_op jit(solution)/shard_map/dot_general | solution.py:17
  47.1 1.0 %convolution_convert_fusion = bf16[128,1280]{1,0:T(8,128)(2,1)} fusion(bf16[8,1280]{1,0:T(8,128)(2,1)S(1)} %get-tuple-element.32, f32[8,256]{1,0:T(8,128)S(1)} %get-tuple-element.26.comb_ref), kind=kOutput, calls=%fused_computation.4 | convolution fusion | flops 2785280 | bytes 350208 | tf_op jit(solution)/shard_map/dot_general | solution.py:17
  48.1 5.1 %all-to-all-done.3 = f32[32,1,640]{2,1,0:T(1,128)S(1)} async-done(((f32[32,1,640]{2,1,0:T(1,128)}), f32[32,1,640]{2,1,0:T(1,128)S(1)}, u32[]{:S(2)}, u32[]{:S(2)}) %all-to-all-start.3) | async-done | bytes 81952 | tf_op jit(solution)/shard_map/all_to_all | solution.py:372
  53.3 0.6 %copy.11 = f32[1,1,2,640]{3,1,2,0:T(1,128)} copy(f32[1,1,2,640]{3,2,1,0:T(2,128)S(1)} %bitcast.17) | data formatting | bytes 10240
  (5 shorter events, 0.1 us)
Async XLA Ops:
  0.6 15.0 %collective-permute-start = (bf16[128,1280]{1,0:T(8,128)(2,1)}, bf16[128,1280]{1,0:T(8,128)(2,1)S(1)}, u32[]{:S(2)}, u32[]{:S(2)}) collective-permute-start(bf16[128,1280]{1,0:T(8,128)(2,1)} %tokens_ref.1), channel_id=1, source_target_pairs={{0,8},{8,0},{16,24},{24,16},{1,9},{9,1},{17,25},{25,17},{2,10},{10... | collective-permute-start | bytes 983048 | tf_op jit(solution)/shard_map/ppermute | solution.py:311
  1.1 14.5 %collective-permute-start.1 = (bf16[128,1280]{1,0:T(8,128)(2,1)}, bf16[128,1280]{1,0:T(8,128)(2,1)S(1)}, u32[]{:S(2)}, u32[]{:S(2)}) collective-permute-start(bf16[128,1280]{1,0:T(8,128)(2,1)} %cotangent_ref.1), channel_id=1, source_target_pairs={{0,8},{8,0},{16,24},{24,16},{1,9},{9,1},{17,25},{25,17},{2,10},{10... | collective-permute-start | bytes 983048 | tf_op jit(solution)/shard_map/ppermute | solution.py:312
  1.2 0.7 %copy-start.2 = (bf16[1280,1]{0,1:T(2,128)(2,1)S(1)}, bf16[1280,1]{0,1:T(2,128)(2,1)}, u32[]{:S(2)}) copy-start(bf16[1280,1]{0,1:T(2,128)(2,1)} %param.6) | copy-start | bytes 7684
  15.7 11.7 %collective-permute-start.2 = (bf16[1,1280,1280]{2,1,0:T(8,128)(2,1)}, bf16[1,1280,1280]{2,1,0:T(8,128)(2,1)S(1)}, u32[]{:S(2)}, u32[]{:S(2)}) collective-permute-start(bf16[1,1280,1280]{2,1,0:T(8,128)(2,1)} %param.7), channel_id=1, source_target_pairs={{0,8},{8,0},{16,24},{24,16},{1,9},{9,1},{17,25},{25,17},{2,10},{10... | collective-permute-start | bytes 9830408 | tf_op jit(solution)/shard_map/ppermute | solution.py:315
  15.7 11.7 %collective-permute-start.3 = (bf16[1,1280,1280]{2,1,0:T(8,128)(2,1)}, bf16[1,1280,1280]{2,1,0:T(8,128)(2,1)S(1)}, u32[]{:S(2)}, u32[]{:S(2)}) collective-permute-start(bf16[1,1280,1280]{2,1,0:T(8,128)(2,1)} %param.8), channel_id=1, source_target_pairs={{0,8},{8,0},{16,24},{24,16},{1,9},{9,1},{17,25},{25,17},{2,10},{10... | collective-permute-start | bytes 9830408 | tf_op jit(solution)/shard_map/ppermute | solution.py:316
  30.4 11.1 %all-to-all-start.2 = ((bf16[32,24,128]{2,1,0:T(8,128)(2,1)}), bf16[32,24,128]{2,1,0:T(8,128)(2,1)S(1)}, u32[]{:S(2)}, u32[]{:S(2)}) async-start(bf16[32,24,128]{2,1,0:T(8,128)(2,1)} %get-tuple-element.30), calls=%async_computation.2 | async-start | bytes 393216 | tf_op jit(solution)/shard_map/all_to_all | solution.py:352
  32.9 1.2 %collective-permute-start.4 = (bf16[2,1280]{1,0:T(2,128)(2,1)S(1)}, bf16[2,1280]{1,0:T(2,128)(2,1)S(1)}, u32[]{:S(2)}, u32[]{:S(2)}) collective-permute-start(bf16[2,1280]{1,0:T(2,128)(2,1)S(1)} %get-tuple-element.38), channel_id=1, source_target_pairs={{0,8},{8,0},{16,24},{24,16},{1,9},{9,1},{17,25},{25,17},{2,10},{10... | collective-permute-start | bytes 15368 | tf_op jit(solution)/shard_map/ppermute | solution.py:353
  34.2 7.3 %copy-start = (bf16[128,1280]{1,0:T(8,128)(2,1)S(1)}, bf16[128,1280]{1,0:T(8,128)(2,1)}, u32[]{:S(2)}) copy-start(bf16[128,1280]{1,0:T(8,128)(2,1)} %tokens_ref.1) | copy-start | bytes 983044
  34.2 7.3 %copy-start.1 = (bf16[128,1280]{1,0:T(8,128)(2,1)S(1)}, bf16[128,1280]{1,0:T(8,128)(2,1)}, u32[]{:S(2)}) copy-start(bf16[128,1280]{1,0:T(8,128)(2,1)} %cotangent_ref.1) | copy-start | bytes 983044
  42.8 10.4 %all-to-all-start.3 = ((f32[32,1,640]{2,1,0:T(1,128)}), f32[32,1,640]{2,1,0:T(1,128)S(1)}, u32[]{:S(2)}, u32[]{:S(2)}) async-start(f32[32,1,640]{2,1,0:T(1,128)} %get-tuple-element.37), calls=%async_computation.3 | async-start | bytes 163840 | tf_op jit(solution)/shard_map/all_to_all | solution.py:372

commit v7 on v6

--- a/solution.py
+++ b/solution.py
@@ -57,20 +57,35 @@
     return lax.broadcasted_iota(jnp.int32, (rows, LANES), 1)
 
 
-def call(kernel, out_shape, scratch_shapes, inputs, unplaced=0, room=24 * 1024 * 1024):
-    spaces = [pltpu.VMEM] * (len(inputs) - unplaced) + [pltpu.HBM] * unplaced
+def call(kernel, out_shape, scratch_shapes, inputs, far=0, far_out=0):
+    near = len(inputs) - far
+    spaces = [pltpu.VMEM] * near + [pltpu.HBM] * far
+    inputs = inputs[:near] + [pltpu.with_memory_space_constraint(x, pltpu.HBM) for x in inputs[near:]]
+    outs = len(out_shape)
+    out_spaces = [pltpu.VMEM] * (outs - far_out) + [pltpu.HBM] * far_out
     return pl.pallas_call(
         kernel,
         out_shape=out_shape,
         in_specs=[pl.BlockSpec(memory_space=space) for space in spaces],
-        out_specs=jax.tree.map(lambda _: pl.BlockSpec(memory_space=pltpu.VMEM), out_shape),
+        out_specs=tuple(pl.BlockSpec(memory_space=space) for space in out_spaces),
         scratch_shapes=scratch_shapes,
-        compiler_params=pltpu.CompilerParams(vmem_limit_bytes=room),
+        compiler_params=pltpu.CompilerParams(vmem_limit_bytes=24 * 1024 * 1024),
     )(*inputs)
 
 
-def keys_kernel(key_ref, out_ref, rows_ref):
+def keys_kernel(
+    key_in_ref, tokens_in_ref, cotangent_in_ref, out_ref, tokens_ref, cotangent_ref, key_ref, rows_ref, sems
+):
+    copies = [
+        pltpu.make_async_copy(source, target, sems.at[i])
+        for i, (source, target) in enumerate(
+            [(key_in_ref, key_ref), (tokens_in_ref, tokens_ref), (cotangent_in_ref, cotangent_ref)]
+        )
+    ]
+    for copy in copies:
+        copy.start()
     width = key_ref.shape[1]
+    copies[0].wait()
     rows_ref[...] = jnp.zeros_like(rows_ref)
     key = key_ref[...].astype(jnp.float32)
     for j in range(width // LANES):
@@ -78,17 +93,14 @@
     block = rows_ref[...].astype(jnp.bfloat16)
     for i in range(out_ref.shape[0]):
         out_ref[i] = block
+    copies[1].wait()
+    copies[2].wait()
 
 
 def sums_kernel(
-    keys_ref, tokens_other_ref, cotangent_other_ref, tokens_far_ref, cotangent_far_ref,
-    message_ref, logits_ref, comb_ref, keys_all_ref,
-    tokens_ref, cotangent_ref, keys_rows_ref, rows_ref, sems,
+    keys_ref, tokens_ref, tokens_other_ref, cotangent_ref, cotangent_other_ref,
+    message_ref, logits_ref, comb_ref, keys_all_ref, keys_rows_ref, rows_ref,
 ):
-    tokens_copy = pltpu.make_async_copy(tokens_far_ref, tokens_ref, sems.at[0])
-    cotangent_copy = pltpu.make_async_copy(cotangent_far_ref, cotangent_ref, sems.at[1])
-    tokens_copy.start()
-    cotangent_copy.start()
     slots = keys_ref.shape[0]
     width = tokens_ref.shape[1]
     half = width // 2
@@ -101,7 +113,6 @@
     ).astype(jnp.bfloat16)
     keys_all_ref[...] = keys
     other_logits = dot(keys, tokens_other_ref[...], 1, 1)
-    tokens_copy.wait()
     logits = jnp.concatenate([dot(keys, tokens_ref[...], 1, 1), other_logits], axis=1)
     logits_ref[...] = logits
     own = tokens_ref.shape[0]
@@ -110,7 +121,6 @@
     comb_prob = row_terms / jnp.sum(row_terms, axis=0, keepdims=True)
     comb_ref[...] = comb_prob
     combine = comb_prob.astype(jnp.bfloat16)
-    cotangent_copy.wait()
     grad_sums = dot(combine[:, :own], cotangent_ref[:, pl.ds(first, half)], 1, 0) + dot(
         combine[:, own:], cotangent_other_ref[:, pl.ds(first, half)], 1, 0
     )
@@ -234,7 +244,7 @@
 
 def grads_kernel(
     parts_ref, logits_ref, comb_ref, tokens_ref, tokens_other_ref, cotangent_ref, cotangent_other_ref,
-    message_ref, slot_out_ref, slot_in_grad_ref, dispatch_ref, logit_grad_ref, parts_rows_ref,
+    message_ref, slot_out_ref, slot_in_grad_ref, factors_ref, parts_rows_ref,
 ):
     devices = parts_ref.shape[0]
     slots, _ = logits_ref.shape
@@ -278,14 +288,51 @@
     logit_grad = (
         comb_prob * (comb_grad - comb_mean) + disp_prob * (disp_grad - correction)
     ).astype(jnp.bfloat16)
-    dispatch_ref[...] = disp_prob[:, :own].astype(jnp.bfloat16)
-    logit_grad_ref[...] = logit_grad[:, :own]
+    factors = [comb_prob[:, :own], disp_prob[:, :own], logit_grad[:, :own]]
+    for i, factor in enumerate(factors):
+        factors_ref[i * slots : (i + 1) * slots] = factor.astype(jnp.bfloat16).astype(jnp.float32)
     keys_part = dot(logit_grad[:, :own], tokens_ref[:, pl.ds(first, half)], 1, 0) + dot(
         logit_grad[:, own:], tokens_other_ref[:, pl.ds(first, half)], 1, 0
     )
     for s in range(slots):
         for q in range(seq_size):
             message_ref[q * slots + s] = keys_part[s : s + 1]
+
+
+def block_of(rows):
+    return 128 if rows % 128 == 0 else rows
+
+
+def weight_grads_kernel(hidden_rows_ref, slot_in_ref, slot_out_grad_ref, w_in_grad_ref, w_out_grad_ref, near_ref, sems):
+    hidden = near_ref.shape[1]
+    block = block_of(hidden)
+    hidden_rows = hidden_rows_ref[...].astype(jnp.float32)
+    copies = []
+    for w, (hidden_index, row_ref, far_ref) in enumerate(
+        [(0, slot_out_grad_ref, w_out_grad_ref), (1, slot_in_ref, w_in_grad_ref)]
+    ):
+        row = row_ref[...].astype(jnp.float32)
+        for i in range(hidden // block):
+            rows = pl.ds(i * block, block)
+            part = hidden_rows[hidden_index : hidden_index + 1, i * block : (i + 1) * block]
+            column = jnp.transpose(jnp.broadcast_to(part, (8, block)))[:, :1]
+            near_ref[w, rows, :] = (column * row).astype(jnp.bfloat16)
+            copy = pltpu.make_async_copy(near_ref.at[w, rows], far_ref.at[0, rows], sems.at[w, i])
+            copy.start()
+            copies.append(copy)
+    for copy in copies:
+        copy.wait()
+
+
+def outputs_kernel(factors_ref, slot_out_ref, slot_in_grad_ref, keys_ref, layer_out_ref, tokens_grad_ref):
+    slots = slot_out_ref.shape[0]
+    combine = jnp.transpose(factors_ref[:slots, :]).astype(jnp.bfloat16)
+    layer_out_ref[...] = dot(combine, slot_out_ref[...], 1, 0).astype(jnp.bfloat16)
+    others = jnp.transpose(factors_ref[slots:, :]).astype(jnp.bfloat16)
+    rows = jnp.concatenate(
+        [slot_in_grad_ref[...].astype(jnp.float32), keys_ref[...].astype(jnp.float32)], axis=0
+    ).astype(jnp.bfloat16)
+    tokens_grad_ref[...] = dot(others, rows, 1, 0).astype(jnp.bfloat16)
 
 
 def local(tokens, slot_keys, w_in, w_out, cotangent):
@@ -302,11 +349,16 @@
     shape = jax.ShapeDtypeStruct
 
     key_rows = padded(width // LANES, 16)
-    key_message = call(
+    key_message, tokens_near, cotangent_near = call(
         keys_kernel,
-        shape((exp_size, key_rows, LANES), bf16),
-        [pltpu.VMEM((key_rows, LANES), f32)],
-        [slot_keys.T],
+        (
+            shape((exp_size, key_rows, LANES), bf16),
+            shape(tokens.shape, bf16),
+            shape(cotangent.shape, bf16),
+        ),
+        [pltpu.VMEM((1, width), bf16), pltpu.VMEM((key_rows, LANES), f32), pltpu.SemaphoreType.DMA((3,))],
+        [slot_keys.T, tokens, cotangent],
+        far=3,
     )
     tokens_other = lax.ppermute(tokens, "seq", swap)
     cotangent_other = lax.ppermute(cotangent, "seq", swap)
@@ -325,15 +377,10 @@
             shape((slots, width), bf16),
         ),
         [
-            pltpu.VMEM(tokens.shape, bf16),
-            pltpu.VMEM(cotangent.shape, bf16),
             pltpu.VMEM((slots, key_rows, LANES), f32),
             pltpu.VMEM((slots, sum_rows, LANES), f32),
-            pltpu.SemaphoreType.DMA((2,)),
         ],
-        [keys, tokens_other, cotangent_other, tokens, cotangent],
-        unplaced=2,
-        room=(64 * 1024 - 11300) * 1024,
+        [keys, tokens_near, tokens_other, cotangent_near, cotangent_other],
     )
     parts = lax.all_to_all(message, both, 0, 0, tiled=True)
 
@@ -351,27 +398,36 @@
     )
     gathered = lax.all_to_all(message, both, 0, 0, tiled=True)
     own_rows = lax.ppermute(hidden_rows, "seq", swap)
-    activation, pre_grad = own_rows[:1], own_rows[1:]
-    w_out_grad = (
-        activation.astype(f32)[:, :, None] * slot_out_grad.astype(f32)[:, None, :]
-    ).astype(bf16)
-    w_in_grad = (pre_grad.astype(f32)[:, :, None] * slot_in.astype(f32)[:, None, :]).astype(bf16)
-
-    message, slot_out, slot_in_grad, dispatch, logit_grad = call(
+    w_in_grad, w_out_grad = call(
+        weight_grads_kernel,
+        (shape((1, hidden, width), bf16), shape((1, hidden, width), bf16)),
+        [
+            pltpu.VMEM((2, hidden, width), bf16),
+            pltpu.SemaphoreType.DMA((2, hidden // block_of(hidden))),
+        ],
+        [own_rows, slot_in, slot_out_grad],
+        far_out=2,
+    )
+    gathered, w_in_grad, w_out_grad = lax.optimization_barrier((gathered, w_in_grad, w_out_grad))
+
+    message, slot_out, slot_in_grad, factors = call(
         grads_kernel,
         (
             shape((devices, 1, half), f32),
             shape((slots, width), bf16),
             shape((slots, width), bf16),
-            shape((slots, own), bf16),
-            shape((slots, own), bf16),
+            shape((3 * slots, own), f32),
         ),
         [pltpu.VMEM((devices, row_count, LANES), f32)],
-        [gathered, logits, comb_prob, tokens, tokens_other, cotangent, cotangent_other],
+        [gathered, logits, comb_prob, tokens_near, tokens_other, cotangent_near, cotangent_other],
     )
     keys_parts = lax.all_to_all(message, both, 0, 0, tiled=True)
-    layer_out = dot(comb_prob[:, :own].astype(bf16), slot_out, 0, 0).astype(bf16)
-    tokens_grad = (dot(dispatch, slot_in_grad, 0, 0) + dot(logit_grad, keys_all, 0, 0)).astype(bf16)
+    layer_out, tokens_grad = call(
+        outputs_kernel,
+        (shape((own, width), bf16), shape((own, width), bf16)),
+        [],
+        [factors, slot_out, slot_in_grad, keys_all],
+    )
     keys_parts = keys_parts.reshape(seq_size // 2, 2, exp_size, half)
     keys_grad = jnp.sum(keys_parts, axis=(0, 2)).reshape(1, width).T
     return (layer_out, tokens_grad, keys_grad, w_in_grad, w_out_grad)

time: 54.2 us -> 53.7 us (level)
  Pallas kernels: 5.98 us -> 10.6 us
  other arithmetic: 4.33 us -> 0.03 us
  matrix products: 2.31 us -> 0 us
  waiting for transfers between devices: 9.15 us -> 11.4 us
  local copies, waits for them, and re-layouts: 1.31 us -> 0.61 us
    pallas_call x4 -> x6, Pallas kernels: 5.98 us -> 10.6 us  [call(): pl.pallas_call(kernel, out_shape=out_shape, in_specs=[pl.BlockSpec(memory...]
    convert_element_type x3 -> x0, other arithmetic: 4.28 us -> none  [the longest x1 2.12 us: local(): w_out_grad = (activation.astype(f32)[:, :, None] * slot_out_grad.astype(f...]
    dot_general x3 -> x0, matrix products: 2.31 us -> none  [dot(): lax.dot_general(left, right, (((left_dim,), (right_dim,)), ((), ())), pre...]
    all_to_all x1, waiting for transfers between devices: 5.11 us -> 6.3 us  [local(): keys_parts = lax.all_to_all(message, both, 0, 0, tiled=True)]
    all_to_all x1, waiting for transfers between devices: 3.01 us -> 3.91 us  [local(): gathered = lax.all_to_all(message, both, 0, 0, tiled=True)]
    unnamed x8 -> x2, local copies, waits for them, and re-layouts: 1.31 us -> 0.61 us
  transfers between devices with their start and end apart: 7 -> 7, of which waited for: 3 -> 4; matrix products, arithmetic and copies ran while one was open for 12% -> 0% of each run, Pallas kernels for 3% -> 12%
where the time goes in v7:
time: 53.7 us; the launch traced here: 53.4 us
  blocking collectives  23.3 us (43%)
  waiting for transfers between devices  11.4 us (21%)
  Pallas kernels  10.6 us (20%)
  starting transfers between devices  6.81 us (13%)
  between operations  0.69 us (1%)
  local copies, waits for them, and re-layouts  0.61 us (1%)
    all_to_all x1, blocking collectives, local(): keys = lax.all_to_all(key_message, 'exp', 0, 0, tiled=True)  13.7 us
    pallas_call x6, Pallas kernels, call(): pl.pallas_call(kernel, out_shape=out_shape, in_specs=[pl.BlockSpec(memory...  10.6 us
    all_to_all x1, blocking collectives, local(): parts = lax.all_to_all(message, both, 0, 0, tiled=True)  9.56 us
    all_to_all x1, waiting for transfers between devices, local(): keys_parts = lax.all_to_all(message, both, 0, 0, tiled=True)  6.3 us
    all_to_all x1, waiting for transfers between devices, local(): gathered = lax.all_to_all(message, both, 0, 0, tiled=True)  3.91 us
    all_to_all x1, starting transfers between devices, local(): keys_parts = lax.all_to_all(message, both, 0, 0, tiled=True)  2.95 us
    all_to_all x1, starting transfers between devices, local(): gathered = lax.all_to_all(message, both, 0, 0, tiled=True)  2.58 us
  transfers between devices with their start and end apart: 7, of which 4 were waited for; matrix products, arithmetic and copies ran while one was open for 0% of the time, Pallas kernels for 12%

profile of v7, /device:TPU:0, one launch (start us, length us, event | category | flops | bytes accessed | tf_op | source)
XLA Modules:
  0.0 53.4 jit_solution(18263525466583628413)
XLA Ops:
  0.6 0.5 collective-permute-start
  1.1 0.1 collective-permute-start.1
  1.2 1.1 %shard_map.92 = (bf16[8,16,128]{2,1,0:T(8,128)(2,1)S(1)}, bf16[128,1280]{1,0:T(8,128)(2,1)S(1)}, bf16[128,1280]{1,0:T(8,128)(2,1)S(1)}) custom-call(bf16[1,1280]{1,0:T(2,128)(2,1)} %bitcast.12, bf16[128,1280]{1,0:T(8,128)(2,1)} %tokens_in_ref.1, bf16[128,1280]{1,0:T(8,128)(2,1)} %cotangent_in_ref.1), custom_call_target="tpu_custom_call" | custom-call | tf_op jit(solution)/shard_map/pallas_call | solution.py:66
  2.3 13.7 %all_to_all.20.keys_ref = bf16[8,16,128]{2,1,0:T(8,128)(2,1)S(1)} all-to-all(bf16[8,16,128]{2,1,0:T(8,128)(2,1)S(1)} %get-tuple-element.32), channel_id=1, replica_groups=mesh['seq'=4,'exp'=8] {'exp'}, dimensions={0} | all-to-all | bytes 65536 | tf_op jit(solution)/shard_map/all_to_all | solution.py:365
  16.1 0.0 collective-permute-done.tokens_other_ref
  16.1 0.0 collective-permute-done.1.cotangent_other_ref
  16.1 0.0 collective-permute-start.2
  16.1 0.5 collective-permute-start.3
  16.6 0.6 %shard_map.93 = (bf16[32,16,128]{2,1,0:T(8,128)(2,1)S(1)}, f32[8,256]{1,0:T(8,128)S(1)}, f32[8,256]{1,0:T(8,128)S(1)}, bf16[8,1280]{1,0:T(8,128)(2,1)S(1)}) custom-call(bf16[8,16,128]{2,1,0:T(8,128)(2,1)S(1)} %all_to_all.20.keys_ref, bf16[128,1280]{1,0:T(8,128)(2,1)S(1)} %get-tuple-element.34.tokens_ref, ...), custom_call_target="tpu_custom_call" | custom-call | tf_op jit(solution)/shard_map/pallas_call | solution.py:66
  17.2 9.6 %all_to_all.21.parts_ref = bf16[32,16,128]{2,1,0:T(8,128)(2,1)S(1)} all-to-all(bf16[32,16,128]{2,1,0:T(8,128)(2,1)S(1)} %get-tuple-element.38), channel_id=1, replica_groups=mesh['seq'=4,'exp'=8] {'seq','exp'}, dimensions={0} | all-to-all | bytes 262144 | tf_op jit(solution)/shard_map/all_to_all | solution.py:385
  26.7 0.0 collective-permute-done.2
  26.7 0.1 collective-permute-done.3
  26.8 3.0 %shard_map.94 = (bf16[32,24,128]{2,1,0:T(8,128)(2,1)}, bf16[1,1280]{1,0:T(2,128)(2,1)S(1)}, bf16[1,1280]{1,0:T(2,128)(2,1)S(1)}, bf16[2,1280]{1,0:T(2,128)(2,1)S(1)}) custom-call(bf16[32,16,128]{2,1,0:T(8,128)(2,1)S(1)} %all_to_all.21.parts_ref, bf16[1280,1280]{1,0:T(8,128)(2,1)S(1)} %bitcast.8, bf16[1280,1280]{1,0:T(8,128)(2,1)S(1)} %bitcast.9), custom_call_target="tpu_custom_call" | custom-call | tf_op jit(solution)/shard_map/pallas_call | solution.py:66
  29.8 2.6 %all-to-all-start.2 = ((bf16[32,24,128]{2,1,0:T(8,128)(2,1)}), bf16[32,24,128]{2,1,0:T(8,128)(2,1)S(1)}, u32[]{:S(2)}, u32[]{:S(2)}) async-start(bf16[32,24,128]{2,1,0:T(8,128)(2,1)} %get-tuple-element.41), calls=%async_computation.2 | async-start | bytes 393216 | tf_op jit(solution)/shard_map/all_to_all | solution.py:399
  32.4 0.2 collective-permute-start.4
  32.6 1.1 %collective-permute-done.4.hidden_rows_ref = bf16[2,1280]{1,0:T(2,128)(2,1)S(1)} collective-permute-done((bf16[2,1280]{1,0:T(2,128)(2,1)S(1)}, bf16[2,1280]{1,0:T(2,128)(2,1)S(1)}, u32[]{:S(2)}, u32[]{:S(2)}) %collective-permute-start.4) | collective-permute-done | bytes 5152 | tf_op jit(solution)/shard_map/ppermute | solution.py:400
  33.7 3.4 %shard_map.95 = (bf16[1,1280,1280]{2,1,0:T(8,128)(2,1)}, bf16[1,1280,1280]{2,1,0:T(8,128)(2,1)}) custom-call(bf16[2,1280]{1,0:T(2,128)(2,1)S(1)} %collective-permute-done.4.hidden_rows_ref, bf16[1,1280]{1,0:T(2,128)(2,1)S(1)} %get-tuple-element.43.slot_in_ref, bf16[1,1280]{1,0:T(2,128)(2,1)S(1)} %get-tuple-element.44.slot_out_grad_ref), custom_call_target="tpu_custom_call" | custom-call | tf_op jit(solution)/shard_map/pallas_call | solution.py:66
  37.1 3.9 %all-to-all-done.2.parts_ref = bf16[32,24,128]{2,1,0:T(8,128)(2,1)S(1)} async-done(((bf16[32,24,128]{2,1,0:T(8,128)(2,1)}), bf16[32,24,128]{2,1,0:T(8,128)(2,1)S(1)}, u32[]{:S(2)}, u32[]{:S(2)}) %all-to-all-start.2) | async-done | bytes 196640 | tf_op jit(solution)/shard_map/all_to_all | solution.py:399
  41.0 1.4 %shard_map.96 = (f32[32,1,640]{2,1,0:T(1,128)}, bf16[8,1280]{1,0:T(8,128)(2,1)S(1)}, bf16[8,1280]{1,0:T(8,128)(2,1)S(1)}, f32[24,128]{1,0:T(8,128)S(1)}) custom-call(bf16[32,24,128]{2,1,0:T(8,128)(2,1)S(1)} %all-to-all-done.2.parts_ref, f32[8,256]{1,0:T(8,128)S(1)} %get-tuple-element.48.logits_ref, f32[8,256]{1,0:T(8,128)S(1)} %get-tuple-element.49.comb_ref, ...), custom_call_target="tpu_custom_call" | custom-call | tf_op jit(solution)/shard_map/pallas_call | solution.py:66
  42.3 2.9 %all-to-all-start.3 = ((f32[32,1,640]{2,1,0:T(1,128)}), f32[32,1,640]{2,1,0:T(1,128)S(1)}, u32[]{:S(2)}, u32[]{:S(2)}) async-start(f32[32,1,640]{2,1,0:T(1,128)} %get-tuple-element.56), calls=%async_computation.3 | async-start | bytes 163840 | tf_op jit(solution)/shard_map/all_to_all | solution.py:424
  45.3 1.1 %shard_map.97 = (bf16[128,1280]{1,0:T(8,128)(2,1)}, bf16[128,1280]{1,0:T(8,128)(2,1)}) custom-call(f32[24,128]{1,0:T(8,128)S(1)} %get-tuple-element.50.factors_ref, bf16[8,1280]{1,0:T(8,128)(2,1)S(1)} %get-tuple-element.51.slot_out_ref, bf16[8,1280]{1,0:T(8,128)(2,1)S(1)} %get-tuple-element.52.slot_in_grad_ref, bf16[8,1280]{1,0:T(8,128)(2,1)S(1)} %get-tuple-element.53.keys_ref), custom_call_target="tpu_custom_call" | custom-call | tf_op jit(solution)/shard_map/pallas_call | solution.py:66
  46.4 6.3 %all-to-all-done.3 = f32[32,1,640]{2,1,0:T(1,128)S(1)} async-done(((f32[32,1,640]{2,1,0:T(1,128)}), f32[32,1,640]{2,1,0:T(1,128)S(1)}, u32[]{:S(2)}, u32[]{:S(2)}) %all-to-all-start.3) | async-done | bytes 81952 | tf_op jit(solution)/shard_map/all_to_all | solution.py:424
  52.8 0.6 %copy.11 = f32[1,1,2,640]{3,1,2,0:T(1,128)} copy(f32[1,1,2,640]{3,2,1,0:T(2,128)S(1)} %bitcast.11) | data formatting | bytes 10240
  (2 shorter events, 0.0 us)
Async XLA Ops:
  0.6 15.4 %collective-permute-start = (bf16[128,1280]{1,0:T(8,128)(2,1)}, bf16[128,1280]{1,0:T(8,128)(2,1)S(1)}, u32[]{:S(2)}, u32[]{:S(2)}) collective-permute-start(bf16[128,1280]{1,0:T(8,128)(2,1)} %tokens_in_ref.1), channel_id=1, source_target_pairs={{0,8},{8,0},{16,24},{24,16},{1,9},{9,1},{17,25},{25,17},{2,10},{10... | collective-permute-start | bytes 983048 | tf_op jit(solution)/shard_map/ppermute | solution.py:363
  1.1 14.9 %collective-permute-start.1 = (bf16[128,1280]{1,0:T(8,128)(2,1)}, bf16[128,1280]{1,0:T(8,128)(2,1)S(1)}, u32[]{:S(2)}, u32[]{:S(2)}) collective-permute-start(bf16[128,1280]{1,0:T(8,128)(2,1)} %cotangent_in_ref.1), channel_id=1, source_target_pairs={{0,8},{8,0},{16,24},{24,16},{1,9},{9,1},{17,25},{25,17},{2,10},{10... | collective-permute-start | bytes 983048 | tf_op jit(solution)/shard_map/ppermute | solution.py:364
  16.1 10.6 %collective-permute-start.2 = (bf16[1,1280,1280]{2,1,0:T(8,128)(2,1)}, bf16[1,1280,1280]{2,1,0:T(8,128)(2,1)S(1)}, u32[]{:S(2)}, u32[]{:S(2)}) collective-permute-start(bf16[1,1280,1280]{2,1,0:T(8,128)(2,1)} %param.7), channel_id=1, source_target_pairs={{0,8},{8,0},{16,24},{24,16},{1,9},{9,1},{17,25},{25,17},{2,10},{10... | collective-permute-start | bytes 9830408 | tf_op jit(solution)/shard_map/ppermute | solution.py:367
  16.1 10.7 %collective-permute-start.3 = (bf16[1,1280,1280]{2,1,0:T(8,128)(2,1)}, bf16[1,1280,1280]{2,1,0:T(8,128)(2,1)S(1)}, u32[]{:S(2)}, u32[]{:S(2)}) collective-permute-start(bf16[1,1280,1280]{2,1,0:T(8,128)(2,1)} %param.8), channel_id=1, source_target_pairs={{0,8},{8,0},{16,24},{24,16},{1,9},{9,1},{17,25},{25,17},{2,10},{10... | collective-permute-start | bytes 9830408 | tf_op jit(solution)/shard_map/ppermute | solution.py:368
  29.8 11.1 %all-to-all-start.2 = ((bf16[32,24,128]{2,1,0:T(8,128)(2,1)}), bf16[32,24,128]{2,1,0:T(8,128)(2,1)S(1)}, u32[]{:S(2)}, u32[]{:S(2)}) async-start(bf16[32,24,128]{2,1,0:T(8,128)(2,1)} %get-tuple-element.41), calls=%async_computation.2 | async-start | bytes 393216 | tf_op jit(solution)/shard_map/all_to_all | solution.py:399
  32.4 1.2 %collective-permute-start.4 = (bf16[2,1280]{1,0:T(2,128)(2,1)S(1)}, bf16[2,1280]{1,0:T(2,128)(2,1)S(1)}, u32[]{:S(2)}, u32[]{:S(2)}) collective-permute-start(bf16[2,1280]{1,0:T(2,128)(2,1)S(1)} %get-tuple-element.42), channel_id=1, source_target_pairs={{0,8},{8,0},{16,24},{24,16},{1,9},{9,1},{17,25},{25,17},{2,10},{10... | collective-permute-start | bytes 15368 | tf_op jit(solution)/shard_map/ppermute | solution.py:400
  42.3 10.4 %all-to-all-start.3 = ((f32[32,1,640]{2,1,0:T(1,128)}), f32[32,1,640]{2,1,0:T(1,128)S(1)}, u32[]{:S(2)}, u32[]{:S(2)}) async-start(f32[32,1,640]{2,1,0:T(1,128)} %get-tuple-element.56), calls=%async_computation.3 | async-start | bytes 163840 | tf_op jit(solution)/shard_map/all_to_all | solution.py:424

commit v8 on v7

--- a/solution.py
+++ b/solution.py
@@ -324,15 +324,35 @@
         copy.wait()
 
 
-def outputs_kernel(factors_ref, slot_out_ref, slot_in_grad_ref, keys_ref, layer_out_ref, tokens_grad_ref):
+def outputs_kernel(
+    keys_parts_ref, factors_ref, slot_out_ref, slot_in_grad_ref, keys_ref,
+    layer_out_ref, tokens_grad_ref, keys_grad_ref, layer_near_ref, tokens_near_ref, keys_near_ref, sems,
+):
     slots = slot_out_ref.shape[0]
+    half = keys_parts_ref.shape[2]
+    copies = [
+        pltpu.make_async_copy(near, far, sems.at[i])
+        for i, (near, far) in enumerate(
+            [(layer_near_ref, layer_out_ref), (tokens_near_ref, tokens_grad_ref), (keys_near_ref, keys_grad_ref)]
+        )
+    ]
+    for side in range(2):
+        total = keys_parts_ref[side * slots : (side + 1) * slots, 0, :]
+        for first in range((side + 2) * slots, keys_parts_ref.shape[0], 2 * slots):
+            total = total + keys_parts_ref[first : first + slots, 0, :]
+        keys_near_ref[:, side * half : (side + 1) * half] = jnp.sum(total, axis=0, keepdims=True)
+    copies[2].start()
     combine = jnp.transpose(factors_ref[:slots, :]).astype(jnp.bfloat16)
-    layer_out_ref[...] = dot(combine, slot_out_ref[...], 1, 0).astype(jnp.bfloat16)
+    layer_near_ref[...] = dot(combine, slot_out_ref[...], 1, 0).astype(jnp.bfloat16)
+    copies[0].start()
     others = jnp.transpose(factors_ref[slots:, :]).astype(jnp.bfloat16)
     rows = jnp.concatenate(
         [slot_in_grad_ref[...].astype(jnp.float32), keys_ref[...].astype(jnp.float32)], axis=0
     ).astype(jnp.bfloat16)
-    tokens_grad_ref[...] = dot(others, rows, 1, 0).astype(jnp.bfloat16)
+    tokens_near_ref[...] = dot(others, rows, 1, 0).astype(jnp.bfloat16)
+    copies[1].start()
+    for copy in copies:
+        copy.wait()
 
 
 def local(tokens, slot_keys, w_in, w_out, cotangent):
@@ -422,15 +442,19 @@
         [gathered, logits, comb_prob, tokens_near, tokens_other, cotangent_near, cotangent_other],
     )
     keys_parts = lax.all_to_all(message, both, 0, 0, tiled=True)
-    layer_out, tokens_grad = call(
+    layer_out, tokens_grad, keys_grad = call(
         outputs_kernel,
-        (shape((own, width), bf16), shape((own, width), bf16)),
-        [],
-        [factors, slot_out, slot_in_grad, keys_all],
-    )
-    keys_parts = keys_parts.reshape(seq_size // 2, 2, exp_size, half)
-    keys_grad = jnp.sum(keys_parts, axis=(0, 2)).reshape(1, width).T
-    return (layer_out, tokens_grad, keys_grad, w_in_grad, w_out_grad)
+        (shape((own, width), bf16), shape((own, width), bf16), shape((1, width), f32)),
+        [
+            pltpu.VMEM((own, width), bf16),
+            pltpu.VMEM((own, width), bf16),
+            pltpu.VMEM((1, width), f32),
+            pltpu.SemaphoreType.DMA((3,)),
+        ],
+        [keys_parts, factors, slot_out, slot_in_grad, keys_all],
+        far_out=3,
+    )
+    return (layer_out, tokens_grad, keys_grad.T, w_in_grad, w_out_grad)
 
 
 def solution(mesh):

time: 53.7 us -> 53.4 us (level)
  blocking collectives: 23.3 us -> 33.5 us
  waiting for transfers between devices: 11.4 us -> 5.08 us
  starting transfers between devices: 6.81 us -> 3.86 us
  local copies, waits for them, and re-layouts: 0.61 us -> 0 us
  Pallas kernels: 10.6 us -> 9.99 us
    all_to_all x0 -> x1, blocking collectives: none -> 10.2 us  [local(): keys_parts = lax.all_to_all(message, both, 0, 0, tiled=True)]
    all_to_all x1 -> x0, waiting for transfers between devices: 6.3 us -> none  [local(): keys_parts = lax.all_to_all(message, both, 0, 0, tiled=True)]
    all_to_all x1 -> x0, starting transfers between devices: 2.95 us -> none  [local(): keys_parts = lax.all_to_all(message, both, 0, 0, tiled=True)]
    unnamed x2 -> x0, local copies, waits for them, and re-layouts: 0.61 us -> none
    pallas_call x6, Pallas kernels: 10.6 us -> 9.99 us  [call(): pl.pallas_call(kernel, out_shape=out_shape, in_specs=[pl.BlockSpec(memory...]
  transfers between devices with their start and end apart: 7 -> 6, of which waited for: 4 -> 3; matrix products, arithmetic and copies ran while one was open for 0% -> 0% of each run, Pallas kernels for 12% -> 10%
where the time goes in v8:
time: 53.4 us; the launch traced here: 53.1 us
  blocking collectives  33.5 us (63%)
  Pallas kernels  9.99 us (19%)
  waiting for transfers between devices  5.08 us (10%)
  starting transfers between devices  3.86 us (7%)
  between operations  0.68 us (1%)
    all_to_all x1, blocking collectives, local(): keys = lax.all_to_all(key_message, 'exp', 0, 0, tiled=True)  13.7 us
    all_to_all x1, blocking collectives, local(): keys_parts = lax.all_to_all(message, both, 0, 0, tiled=True)  10.2 us
    pallas_call x6, Pallas kernels, call(): pl.pallas_call(kernel, out_shape=out_shape, in_specs=[pl.BlockSpec(memory...  9.99 us
    all_to_all x1, blocking collectives, local(): parts = lax.all_to_all(message, both, 0, 0, tiled=True)  9.56 us
    all_to_all x1, waiting for transfers between devices, local(): gathered = lax.all_to_all(message, both, 0, 0, tiled=True)  3.91 us
    all_to_all x1, starting transfers between devices, local(): gathered = lax.all_to_all(message, both, 0, 0, tiled=True)  2.58 us
  transfers between devices with their start and end apart: 6, of which 3 were waited for; matrix products, arithmetic and copies ran while one was open for 0% of the time, Pallas kernels for 10%

profile of v8, /device:TPU:0, one launch (start us, length us, event | category | flops | bytes accessed | tf_op | source)
XLA Modules:
  0.0 53.1 jit_solution(3342511602165302262)
XLA Ops:
  0.6 0.5 collective-permute-start
  1.1 0.1 collective-permute-start.1
  1.2 1.1 %shard_map.92 = (bf16[8,16,128]{2,1,0:T(8,128)(2,1)S(1)}, bf16[128,1280]{1,0:T(8,128)(2,1)S(1)}, bf16[128,1280]{1,0:T(8,128)(2,1)S(1)}) custom-call(bf16[1,1280]{1,0:T(2,128)(2,1)} %bitcast.6, bf16[128,1280]{1,0:T(8,128)(2,1)} %tokens_in_ref.1, bf16[128,1280]{1,0:T(8,128)(2,1)} %cotangent_in_ref.1), custom_call_target="tpu_custom_call" | custom-call | tf_op jit(solution)/shard_map/pallas_call | solution.py:66
  2.3 13.7 %all_to_all.20.keys_ref = bf16[8,16,128]{2,1,0:T(8,128)(2,1)S(1)} all-to-all(bf16[8,16,128]{2,1,0:T(8,128)(2,1)S(1)} %get-tuple-element.33), channel_id=1, replica_groups=mesh['seq'=4,'exp'=8] {'exp'}, dimensions={0} | all-to-all | bytes 65536 | tf_op jit(solution)/shard_map/all_to_all | solution.py:385
  16.1 0.0 collective-permute-done.tokens_other_ref
  16.1 0.0 collective-permute-done.1.cotangent_other_ref
  16.1 0.0 collective-permute-start.2
  16.1 0.5 collective-permute-start.3
  16.6 0.6 %shard_map.93 = (bf16[32,16,128]{2,1,0:T(8,128)(2,1)S(1)}, f32[8,256]{1,0:T(8,128)S(1)}, f32[8,256]{1,0:T(8,128)S(1)}, bf16[8,1280]{1,0:T(8,128)(2,1)S(1)}) custom-call(bf16[8,16,128]{2,1,0:T(8,128)(2,1)S(1)} %all_to_all.20.keys_ref, bf16[128,1280]{1,0:T(8,128)(2,1)S(1)} %get-tuple-element.35.tokens_ref, ...), custom_call_target="tpu_custom_call" | custom-call | tf_op jit(solution)/shard_map/pallas_call | solution.py:66
  17.2 9.6 %all_to_all.21.parts_ref = bf16[32,16,128]{2,1,0:T(8,128)(2,1)S(1)} all-to-all(bf16[32,16,128]{2,1,0:T(8,128)(2,1)S(1)} %get-tuple-element.39), channel_id=1, replica_groups=mesh['seq'=4,'exp'=8] {'seq','exp'}, dimensions={0} | all-to-all | bytes 262144 | tf_op jit(solution)/shard_map/all_to_all | solution.py:405
  26.7 0.0 collective-permute-done.2
  26.7 0.1 collective-permute-done.3
  26.8 3.0 %shard_map.94 = (bf16[32,24,128]{2,1,0:T(8,128)(2,1)}, bf16[1,1280]{1,0:T(2,128)(2,1)S(1)}, bf16[1,1280]{1,0:T(2,128)(2,1)S(1)}, bf16[2,1280]{1,0:T(2,128)(2,1)S(1)}) custom-call(bf16[32,16,128]{2,1,0:T(8,128)(2,1)S(1)} %all_to_all.21.parts_ref, bf16[1280,1280]{1,0:T(8,128)(2,1)S(1)} %bitcast.4, bf16[1280,1280]{1,0:T(8,128)(2,1)S(1)} %bitcast.5), custom_call_target="tpu_custom_call" | custom-call | tf_op jit(solution)/shard_map/pallas_call | solution.py:66
  29.8 2.6 %all-to-all-start.2 = ((bf16[32,24,128]{2,1,0:T(8,128)(2,1)}), bf16[32,24,128]{2,1,0:T(8,128)(2,1)S(1)}, u32[]{:S(2)}, u32[]{:S(2)}) async-start(bf16[32,24,128]{2,1,0:T(8,128)(2,1)} %get-tuple-element.42), calls=%async_computation.2 | async-start | bytes 393216 | tf_op jit(solution)/shard_map/all_to_all | solution.py:419
  32.4 0.2 collective-permute-start.4
  32.6 1.1 %collective-permute-done.4.hidden_rows_ref = bf16[2,1280]{1,0:T(2,128)(2,1)S(1)} collective-permute-done((bf16[2,1280]{1,0:T(2,128)(2,1)S(1)}, bf16[2,1280]{1,0:T(2,128)(2,1)S(1)}, u32[]{:S(2)}, u32[]{:S(2)}) %collective-permute-start.4) | collective-permute-done | bytes 5152 | tf_op jit(solution)/shard_map/ppermute | solution.py:420
  33.7 3.4 %shard_map.95 = (bf16[1,1280,1280]{2,1,0:T(8,128)(2,1)}, bf16[1,1280,1280]{2,1,0:T(8,128)(2,1)}) custom-call(bf16[2,1280]{1,0:T(2,128)(2,1)S(1)} %collective-permute-done.4.hidden_rows_ref, bf16[1,1280]{1,0:T(2,128)(2,1)S(1)} %get-tuple-element.44.slot_in_ref, bf16[1,1280]{1,0:T(2,128)(2,1)S(1)} %get-tuple-element.45.slot_out_grad_ref), custom_call_target="tpu_custom_call" | custom-call | tf_op jit(solution)/shard_map/pallas_call | solution.py:66
  37.1 3.9 %all-to-all-done.2.parts_ref = bf16[32,24,128]{2,1,0:T(8,128)(2,1)S(1)} async-done(((bf16[32,24,128]{2,1,0:T(8,128)(2,1)}), bf16[32,24,128]{2,1,0:T(8,128)(2,1)S(1)}, u32[]{:S(2)}, u32[]{:S(2)}) %all-to-all-start.2) | async-done | bytes 196640 | tf_op jit(solution)/shard_map/all_to_all | solution.py:419
  41.0 0.7 %shard_map.96 = (f32[32,1,640]{2,1,0:T(1,128)S(1)}, bf16[8,1280]{1,0:T(8,128)(2,1)S(1)}, bf16[8,1280]{1,0:T(8,128)(2,1)S(1)}, f32[24,128]{1,0:T(8,128)S(1)}) custom-call(bf16[32,24,128]{2,1,0:T(8,128)(2,1)S(1)} %all-to-all-done.2.parts_ref, f32[8,256]{1,0:T(8,128)S(1)} %get-tuple-element.49.logits_ref, f32[8,256]{1,0:T(8,128)S(1)} %get-tuple-element.50.comb_ref, ...), custom_call_target="tpu_custom_call" | custom-call | tf_op jit(solution)/shard_map/pallas_call | solution.py:66
  41.7 10.2 %all_to_all.22.keys_parts_ref = f32[32,1,640]{2,1,0:T(1,128)S(1)} all-to-all(f32[32,1,640]{2,1,0:T(1,128)S(1)} %get-tuple-element.51), channel_id=1, replica_groups=mesh['seq'=4,'exp'=8] {'seq','exp'}, dimensions={0} | all-to-all | bytes 163840 | tf_op jit(solution)/shard_map/all_to_all | solution.py:444
  51.9 1.2 %shard_map.97 = (bf16[128,1280]{1,0:T(8,128)(2,1)}, bf16[128,1280]{1,0:T(8,128)(2,1)}, f32[1,1280]{1,0:T(1,128)}) custom-call(f32[32,1,640]{2,1,0:T(1,128)S(1)} %all_to_all.22.keys_parts_ref, f32[24,128]{1,0:T(8,128)S(1)} %get-tuple-element.52.factors_ref, bf16[8,1280]{1,0:T(8,128)(2,1)S(1)} %get-tuple-element.53.slot_out_ref, ...), custom_call_target="tpu_custom_call" | custom-call | tf_op jit(solution)/shard_map/pallas_call | solution.py:66
Async XLA Ops:
  0.6 15.4 %collective-permute-start = (bf16[128,1280]{1,0:T(8,128)(2,1)}, bf16[128,1280]{1,0:T(8,128)(2,1)S(1)}, u32[]{:S(2)}, u32[]{:S(2)}) collective-permute-start(bf16[128,1280]{1,0:T(8,128)(2,1)} %tokens_in_ref.1), channel_id=1, source_target_pairs={{0,8},{8,0},{16,24},{24,16},{1,9},{9,1},{17,25},{25,17},{2,10},{10... | collective-permute-start | bytes 983048 | tf_op jit(solution)/shard_map/ppermute | solution.py:383
  1.1 14.9 %collective-permute-start.1 = (bf16[128,1280]{1,0:T(8,128)(2,1)}, bf16[128,1280]{1,0:T(8,128)(2,1)S(1)}, u32[]{:S(2)}, u32[]{:S(2)}) collective-permute-start(bf16[128,1280]{1,0:T(8,128)(2,1)} %cotangent_in_ref.1), channel_id=1, source_target_pairs={{0,8},{8,0},{16,24},{24,16},{1,9},{9,1},{17,25},{25,17},{2,10},{10... | collective-permute-start | bytes 983048 | tf_op jit(solution)/shard_map/ppermute | solution.py:384
  16.1 10.6 %collective-permute-start.2 = (bf16[1,1280,1280]{2,1,0:T(8,128)(2,1)}, bf16[1,1280,1280]{2,1,0:T(8,128)(2,1)S(1)}, u32[]{:S(2)}, u32[]{:S(2)}) collective-permute-start(bf16[1,1280,1280]{2,1,0:T(8,128)(2,1)} %param.7), channel_id=1, source_target_pairs={{0,8},{8,0},{16,24},{24,16},{1,9},{9,1},{17,25},{25,17},{2,10},{10... | collective-permute-start | bytes 9830408 | tf_op jit(solution)/shard_map/ppermute | solution.py:387
  16.1 10.7 %collective-permute-start.3 = (bf16[1,1280,1280]{2,1,0:T(8,128)(2,1)}, bf16[1,1280,1280]{2,1,0:T(8,128)(2,1)S(1)}, u32[]{:S(2)}, u32[]{:S(2)}) collective-permute-start(bf16[1,1280,1280]{2,1,0:T(8,128)(2,1)} %param.8), channel_id=1, source_target_pairs={{0,8},{8,0},{16,24},{24,16},{1,9},{9,1},{17,25},{25,17},{2,10},{10... | collective-permute-start | bytes 9830408 | tf_op jit(solution)/shard_map/ppermute | solution.py:388
  29.8 11.1 %all-to-all-start.2 = ((bf16[32,24,128]{2,1,0:T(8,128)(2,1)}), bf16[32,24,128]{2,1,0:T(8,128)(2,1)S(1)}, u32[]{:S(2)}, u32[]{:S(2)}) async-start(bf16[32,24,128]{2,1,0:T(8,128)(2,1)} %get-tuple-element.42), calls=%async_computation.2 | async-start | bytes 393216 | tf_op jit(solution)/shard_map/all_to_all | solution.py:419
  32.4 1.2 %collective-permute-start.4 = (bf16[2,1280]{1,0:T(2,128)(2,1)S(1)}, bf16[2,1280]{1,0:T(2,128)(2,1)S(1)}, u32[]{:S(2)}, u32[]{:S(2)}) collective-permute-start(bf16[2,1280]{1,0:T(2,128)(2,1)S(1)} %get-tuple-element.43), channel_id=1, source_target_pairs={{0,8},{8,0},{16,24},{24,16},{1,9},{9,1},{17,25},{25,17},{2,10},{10... | collective-permute-start | bytes 15368 | tf_op jit(solution)/shard_map/ppermute | solution.py:420

commit v9 on v8

--- a/solution.py
+++ b/solution.py
@@ -11,6 +11,7 @@
 cubic_coeff = 0.044715
 LANES = 128
 VECTOR_SHARE = 0.65
+SUM_SHARE = 0.45
 
 
 def dot(left, right, left_dim, right_dim):
@@ -182,6 +183,39 @@
     return results
 
 
+def column_sums_times(row, w_ref, first, count):
+    column = jnp.transpose(jnp.broadcast_to(row.astype(jnp.float32), (8, count)))[:, :1]
+    total = None
+    for start in range(0, count, 16):
+        rows = w_ref[first + start : first + start + 16, :].astype(jnp.float32)
+        term = rows * column[start : start + 16]
+        total = term if total is None else total + term
+    return total
+
+
+def sums_times(pairs):
+    results, taken = [], 0
+    for row, w_ref in pairs:
+        rows = w_ref.shape[0]
+        block = LANES if rows % LANES == 0 else rows
+        vector_total, matrix_blocks = None, []
+        for first in range(0, rows, block):
+            taken += SUM_SHARE
+            if taken >= 1.0 and block == LANES:
+                taken -= 1.0
+                part = column_sums_times(row[:, first : first + block], w_ref, first, block)
+                vector_total = part if vector_total is None else vector_total + part
+            else:
+                matrix_blocks.append(dot(row[:, first : first + block], w_ref[first : first + block, :], 1, 0))
+        total = matrix_blocks[0]
+        for part in matrix_blocks[1:]:
+            total = total + part
+        if vector_total is not None:
+            total = total + jnp.sum(vector_total, axis=0, keepdims=True)
+        results.append(total)
+    return results
+
+
 def expert_kernel(
     exp_size, parts_ref, w_in_ref, w_out_ref,
     message_ref, slot_in_ref, slot_out_grad_ref, hidden_rows_ref, parts_rows_ref, rows_ref,
@@ -224,19 +258,16 @@
     activation = value.astype(jnp.bfloat16)
     pre_grad = (act_grad * slope).astype(jnp.bfloat16)
     hidden_rows_ref[...] = jnp.concatenate([value, act_grad * slope], axis=0).astype(jnp.bfloat16)
-    out_part = dot(activation, w_out_ref[...], 1, 0)
-    grad_part = dot(pre_grad, w_in_ref[...], 1, 0).astype(jnp.bfloat16).astype(jnp.float32)
+    out_part, grad_part = sums_times([(activation, w_out_ref), (pre_grad, w_in_ref)])
+    grad_part = grad_part.astype(jnp.bfloat16).astype(jnp.float32)
     correction = jnp.sum(slot_row * grad_part, axis=1, keepdims=True)
-    for j in range(chunks):
-        columns = slice(j * LANES, (j + 1) * LANES)
-        rows_ref[j : j + 1, :] = out_part[:, columns]
-        rows_ref[chunks + j : chunks + j + 1, :] = grad_part[:, columns]
     stats = in_lanes(
         bf16_terms(slot_peak, 3) + bf16_terms(slot_total, 3) + bf16_terms(correction, 3), lanes_of(1)
     )
-    rows_ref[2 * chunks : 2 * chunks + 1, :] = stats
-    for j in range(2 * chunks + 1, rows_ref.shape[0]):
-        rows_ref[j : j + 1, :] = jnp.zeros_like(stats)
+    rows_ref[0:1, :width] = out_part
+    rows_ref[1:2, :width] = grad_part
+    rows_ref[0:1, width:] = stats
+    rows_ref[1:2, width:] = jnp.zeros_like(stats)
     block = rows_ref[...].astype(jnp.bfloat16)
     for i in range(devices):
         message_ref[i] = block
@@ -254,9 +285,9 @@
     chunks = width // LANES
     first = pl.multiple_of(lax.rem(lax.axis_index("seq"), 2) * half, LANES)
     parts_rows_ref[...] = parts_ref[...].astype(jnp.float32)
-    out_rows = jnp.concatenate([parts_rows_ref[:, j, :] for j in range(chunks)], axis=1)
-    grad_rows = jnp.concatenate([parts_rows_ref[:, chunks + j, :] for j in range(chunks)], axis=1)
-    stats = parts_rows_ref[:, 2 * chunks, :]
+    out_rows = parts_rows_ref[:, 0, :width]
+    grad_rows = parts_rows_ref[:, 1, :width]
+    stats = parts_rows_ref[:, 0, width:]
     lane = lanes_of(slots)
 
     def over_seq(values):
@@ -404,16 +435,15 @@
     )
     parts = lax.all_to_all(message, both, 0, 0, tiled=True)
 
-    row_count = padded(2 * width // LANES + 1, 8)
     message, slot_in, slot_out_grad, hidden_rows = call(
         functools.partial(expert_kernel, exp_size),
         (
-            shape((devices, row_count, LANES), bf16),
+            shape((devices, 2, width + LANES), bf16),
             shape((1, width), bf16),
             shape((1, width), bf16),
             shape((2, hidden), bf16),
         ),
-        [pltpu.VMEM((devices, sum_rows, LANES), f32), pltpu.VMEM((row_count, LANES), f32)],
+        [pltpu.VMEM((devices, sum_rows, LANES), f32), pltpu.VMEM((2, width + LANES), f32)],
         [parts, w_in_other[0], w_out_other[0]],
     )
     gathered = lax.all_to_all(message, both, 0, 0, tiled=True)
@@ -438,7 +468,7 @@
             shape((slots, width), bf16),
             shape((3 * slots, own), f32),
         ),
-        [pltpu.VMEM((devices, row_count, LANES), f32)],
+        [pltpu.VMEM((devices, 2, width + LANES), f32)],
         [gathered, logits, comb_prob, tokens_near, tokens_other, cotangent_near, cotangent_other],
     )
     keys_parts = lax.all_to_all(message, both, 0, 0, tiled=True)

time: 53.4 us -> 53 us (level)
  no operation moved by 1% of the time
where the time goes in v9:
time: 53 us; the launch traced here: 52.7 us
  blocking collectives  33.6 us (63%)
  Pallas kernels  9.98 us (19%)
  waiting for transfers between devices  4.58 us (9%)
  starting transfers between devices  3.86 us (7%)
  between operations  0.68 us (1%)
    all_to_all x1, blocking collectives, local(): keys = lax.all_to_all(key_message, 'exp', 0, 0, tiled=True)  13.7 us
    all_to_all x1, blocking collectives, local(): keys_parts = lax.all_to_all(message, both, 0, 0, tiled=True)  10.3 us
    pallas_call x6, Pallas kernels, call(): pl.pallas_call(kernel, out_shape=out_shape, in_specs=[pl.BlockSpec(memory...  9.98 us
    all_to_all x1, blocking collectives, local(): parts = lax.all_to_all(message, both, 0, 0, tiled=True)  9.56 us
    all_to_all x1, waiting for transfers between devices, local(): gathered = lax.all_to_all(message, both, 0, 0, tiled=True)  3.41 us
    all_to_all x1, starting transfers between devices, local(): gathered = lax.all_to_all(message, both, 0, 0, tiled=True)  2.58 us
  transfers between devices with their start and end apart: 6, of which 3 were waited for; matrix products, arithmetic and copies ran while one was open for 0% of the time, Pallas kernels for 10%

profile of v9, /device:TPU:0, one launch (start us, length us, event | category | flops | bytes accessed | tf_op | source)
XLA Modules:
  0.0 52.7 jit_solution(9179612016183950362)
XLA Ops:
  0.6 0.5 collective-permute-start
  1.1 0.1 collective-permute-start.1
  1.2 1.1 %shard_map.92 = (bf16[8,16,128]{2,1,0:T(8,128)(2,1)S(1)}, bf16[128,1280]{1,0:T(8,128)(2,1)S(1)}, bf16[128,1280]{1,0:T(8,128)(2,1)S(1)}) custom-call(bf16[1,1280]{1,0:T(2,128)(2,1)} %bitcast.6, bf16[128,1280]{1,0:T(8,128)(2,1)} %tokens_in_ref.1, bf16[128,1280]{1,0:T(8,128)(2,1)} %cotangent_in_ref.1), custom_call_target="tpu_custom_call" | custom-call | tf_op jit(solution)/shard_map/pallas_call | solution.py:67
  2.3 13.7 %all_to_all.20.keys_ref = bf16[8,16,128]{2,1,0:T(8,128)(2,1)S(1)} all-to-all(bf16[8,16,128]{2,1,0:T(8,128)(2,1)S(1)} %get-tuple-element.33), channel_id=1, replica_groups=mesh['seq'=4,'exp'=8] {'exp'}, dimensions={0} | all-to-all | bytes 65536 | tf_op jit(solution)/shard_map/all_to_all | solution.py:416
  16.1 0.0 collective-permute-done.tokens_other_ref
  16.1 0.0 collective-permute-done.1.cotangent_other_ref
  16.1 0.0 collective-permute-start.2
  16.1 0.5 collective-permute-start.3
  16.6 0.6 %shard_map.93 = (bf16[32,16,128]{2,1,0:T(8,128)(2,1)S(1)}, f32[8,256]{1,0:T(8,128)S(1)}, f32[8,256]{1,0:T(8,128)S(1)}, bf16[8,1280]{1,0:T(8,128)(2,1)S(1)}) custom-call(bf16[8,16,128]{2,1,0:T(8,128)(2,1)S(1)} %all_to_all.20.keys_ref, bf16[128,1280]{1,0:T(8,128)(2,1)S(1)} %get-tuple-element.35.tokens_ref, ...), custom_call_target="tpu_custom_call" | custom-call | tf_op jit(solution)/shard_map/pallas_call | solution.py:67
  17.2 9.6 %all_to_all.21.parts_ref = bf16[32,16,128]{2,1,0:T(8,128)(2,1)S(1)} all-to-all(bf16[32,16,128]{2,1,0:T(8,128)(2,1)S(1)} %get-tuple-element.39), channel_id=1, replica_groups=mesh['seq'=4,'exp'=8] {'seq','exp'}, dimensions={0} | all-to-all | bytes 262144 | tf_op jit(solution)/shard_map/all_to_all | solution.py:436
  26.7 0.0 collective-permute-done.2
  26.7 0.1 collective-permute-done.3
  26.8 2.9 %shard_map.94 = (bf16[32,2,1408]{2,1,0:T(2,128)(2,1)}, bf16[1,1280]{1,0:T(2,128)(2,1)S(1)}, bf16[1,1280]{1,0:T(2,128)(2,1)S(1)}, bf16[2,1280]{1,0:T(2,128)(2,1)S(1)}) custom-call(bf16[32,16,128]{2,1,0:T(8,128)(2,1)S(1)} %all_to_all.21.parts_ref, bf16[1280,1280]{1,0:T(8,128)(2,1)S(1)} %bitcast.4, bf16[1280,1280]{1,0:T(8,128)(2,1)S(1)} %bitcast.5), custom_call_target="tpu_custom_call" | custom-call | tf_op jit(solution)/shard_map/pallas_call | solution.py:67
  29.8 2.6 %all-to-all-start.2 = ((bf16[32,2,1408]{2,1,0:T(2,128)(2,1)}), bf16[32,2,1408]{2,1,0:T(2,128)(2,1)S(1)}, u32[]{:S(2)}, u32[]{:S(2)}) async-start(bf16[32,2,1408]{2,1,0:T(2,128)(2,1)} %get-tuple-element.42), calls=%async_computation.2 | async-start | bytes 360448 | tf_op jit(solution)/shard_map/all_to_all | solution.py:449
  32.4 0.2 collective-permute-start.4
  32.5 1.1 %collective-permute-done.4.hidden_rows_ref = bf16[2,1280]{1,0:T(2,128)(2,1)S(1)} collective-permute-done((bf16[2,1280]{1,0:T(2,128)(2,1)S(1)}, bf16[2,1280]{1,0:T(2,128)(2,1)S(1)}, u32[]{:S(2)}, u32[]{:S(2)}) %collective-permute-start.4) | collective-permute-done | bytes 5152 | tf_op jit(solution)/shard_map/ppermute | solution.py:450
  33.6 3.4 %shard_map.95 = (bf16[1,1280,1280]{2,1,0:T(8,128)(2,1)}, bf16[1,1280,1280]{2,1,0:T(8,128)(2,1)}) custom-call(bf16[2,1280]{1,0:T(2,128)(2,1)S(1)} %collective-permute-done.4.hidden_rows_ref, bf16[1,1280]{1,0:T(2,128)(2,1)S(1)} %get-tuple-element.44.slot_in_ref, bf16[1,1280]{1,0:T(2,128)(2,1)S(1)} %get-tuple-element.45.slot_out_grad_ref), custom_call_target="tpu_custom_call" | custom-call | tf_op jit(solution)/shard_map/pallas_call | solution.py:67
  37.0 3.4 %all-to-all-done.2.parts_ref = bf16[32,2,1408]{2,1,0:T(2,128)(2,1)S(1)} async-done(((bf16[32,2,1408]{2,1,0:T(2,128)(2,1)}), bf16[32,2,1408]{2,1,0:T(2,128)(2,1)S(1)}, u32[]{:S(2)}, u32[]{:S(2)}) %all-to-all-start.2) | async-done | bytes 180256 | tf_op jit(solution)/shard_map/all_to_all | solution.py:449
  40.4 0.8 %shard_map.96 = (f32[32,1,640]{2,1,0:T(1,128)S(1)}, bf16[8,1280]{1,0:T(8,128)(2,1)S(1)}, bf16[8,1280]{1,0:T(8,128)(2,1)S(1)}, f32[24,128]{1,0:T(8,128)S(1)}) custom-call(bf16[32,2,1408]{2,1,0:T(2,128)(2,1)S(1)} %all-to-all-done.2.parts_ref, f32[8,256]{1,0:T(8,128)S(1)} %get-tuple-element.49.logits_ref, f32[8,256]{1,0:T(8,128)S(1)} %get-tuple-element.50.comb_ref, ...), custom_call_target="tpu_custom_call" | custom-call | tf_op jit(solution)/shard_map/pallas_call | solution.py:67
  41.2 10.3 %all_to_all.22.keys_parts_ref = f32[32,1,640]{2,1,0:T(1,128)S(1)} all-to-all(f32[32,1,640]{2,1,0:T(1,128)S(1)} %get-tuple-element.51), channel_id=1, replica_groups=mesh['seq'=4,'exp'=8] {'seq','exp'}, dimensions={0} | all-to-all | bytes 163840 | tf_op jit(solution)/shard_map/all_to_all | solution.py:474
  51.5 1.2 %shard_map.97 = (bf16[128,1280]{1,0:T(8,128)(2,1)}, bf16[128,1280]{1,0:T(8,128)(2,1)}, f32[1,1280]{1,0:T(1,128)}) custom-call(f32[32,1,640]{2,1,0:T(1,128)S(1)} %all_to_all.22.keys_parts_ref, f32[24,128]{1,0:T(8,128)S(1)} %get-tuple-element.52.factors_ref, bf16[8,1280]{1,0:T(8,128)(2,1)S(1)} %get-tuple-element.53.slot_out_ref, ...), custom_call_target="tpu_custom_call" | custom-call | tf_op jit(solution)/shard_map/pallas_call | solution.py:67
Async XLA Ops:
  0.6 15.4 %collective-permute-start = (bf16[128,1280]{1,0:T(8,128)(2,1)}, bf16[128,1280]{1,0:T(8,128)(2,1)S(1)}, u32[]{:S(2)}, u32[]{:S(2)}) collective-permute-start(bf16[128,1280]{1,0:T(8,128)(2,1)} %tokens_in_ref.1), channel_id=1, source_target_pairs={{0,8},{8,0},{16,24},{24,16},{1,9},{9,1},{17,25},{25,17},{2,10},{10... | collective-permute-start | bytes 983048 | tf_op jit(solution)/shard_map/ppermute | solution.py:414
  1.1 14.9 %collective-permute-start.1 = (bf16[128,1280]{1,0:T(8,128)(2,1)}, bf16[128,1280]{1,0:T(8,128)(2,1)S(1)}, u32[]{:S(2)}, u32[]{:S(2)}) collective-permute-start(bf16[128,1280]{1,0:T(8,128)(2,1)} %cotangent_in_ref.1), channel_id=1, source_target_pairs={{0,8},{8,0},{16,24},{24,16},{1,9},{9,1},{17,25},{25,17},{2,10},{10... | collective-permute-start | bytes 983048 | tf_op jit(solution)/shard_map/ppermute | solution.py:415
  16.1 10.6 %collective-permute-start.2 = (bf16[1,1280,1280]{2,1,0:T(8,128)(2,1)}, bf16[1,1280,1280]{2,1,0:T(8,128)(2,1)S(1)}, u32[]{:S(2)}, u32[]{:S(2)}) collective-permute-start(bf16[1,1280,1280]{2,1,0:T(8,128)(2,1)} %param.7), channel_id=1, source_target_pairs={{0,8},{8,0},{16,24},{24,16},{1,9},{9,1},{17,25},{25,17},{2,10},{10... | collective-permute-start | bytes 9830408 | tf_op jit(solution)/shard_map/ppermute | solution.py:418
  16.1 10.7 %collective-permute-start.3 = (bf16[1,1280,1280]{2,1,0:T(8,128)(2,1)}, bf16[1,1280,1280]{2,1,0:T(8,128)(2,1)S(1)}, u32[]{:S(2)}, u32[]{:S(2)}) collective-permute-start(bf16[1,1280,1280]{2,1,0:T(8,128)(2,1)} %param.8), channel_id=1, source_target_pairs={{0,8},{8,0},{16,24},{24,16},{1,9},{9,1},{17,25},{25,17},{2,10},{10... | collective-permute-start | bytes 9830408 | tf_op jit(solution)/shard_map/ppermute | solution.py:419
  29.8 10.6 %all-to-all-start.2 = ((bf16[32,2,1408]{2,1,0:T(2,128)(2,1)}), bf16[32,2,1408]{2,1,0:T(2,128)(2,1)S(1)}, u32[]{:S(2)}, u32[]{:S(2)}) async-start(bf16[32,2,1408]{2,1,0:T(2,128)(2,1)} %get-tuple-element.42), calls=%async_computation.2 | async-start | bytes 360448 | tf_op jit(solution)/shard_map/all_to_all | solution.py:449
  32.4 1.2 %collective-permute-start.4 = (bf16[2,1280]{1,0:T(2,128)(2,1)S(1)}, bf16[2,1280]{1,0:T(2,128)(2,1)S(1)}, u32[]{:S(2)}, u32[]{:S(2)}) collective-permute-start(bf16[2,1280]{1,0:T(2,128)(2,1)S(1)} %get-tuple-element.43), channel_id=1, source_target_pairs={{0,8},{8,0},{16,24},{24,16},{1,9},{9,1},{17,25},{25,17},{2,10},{10... | collective-permute-start | bytes 15368 | tf_op jit(solution)/shard_map/ppermute | solution.py:450

commit v10 on v9

--- a/solution.py
+++ b/solution.py
@@ -11,7 +11,7 @@
 cubic_coeff = 0.044715
 LANES = 128
 VECTOR_SHARE = 0.65
-SUM_SHARE = 0.45
+SUM_SHARE = 0.25
 
 
 def dot(left, right, left_dim, right_dim):
@@ -87,10 +87,9 @@
         copy.start()
     width = key_ref.shape[1]
     copies[0].wait()
-    rows_ref[...] = jnp.zeros_like(rows_ref)
     key = key_ref[...].astype(jnp.float32)
-    for j in range(width // LANES):
-        rows_ref[j : j + 1, :] = key[:, j * LANES : (j + 1) * LANES]
+    rows_ref[0:1, :] = key[:, : width // 2]
+    rows_ref[1:2, :] = key[:, width // 2 :]
     block = rows_ref[...].astype(jnp.bfloat16)
     for i in range(out_ref.shape[0]):
         out_ref[i] = block
@@ -109,9 +108,7 @@
     first = pl.multiple_of(lax.rem(lax.axis_index("seq"), 2) * half, LANES)
 
     keys_rows_ref[...] = keys_ref[...].astype(jnp.float32)
-    keys = jnp.concatenate(
-        [keys_rows_ref[:, j, :] for j in range(width // LANES)], axis=1
-    ).astype(jnp.bfloat16)
+    keys = jnp.concatenate([keys_rows_ref[:, 0, :], keys_rows_ref[:, 1, :]], axis=1).astype(jnp.bfloat16)
     keys_all_ref[...] = keys
     other_logits = dot(keys, tokens_other_ref[...], 1, 1)
     logits = jnp.concatenate([dot(keys, tokens_ref[...], 1, 1), other_logits], axis=1)
@@ -367,12 +364,6 @@
             [(layer_near_ref, layer_out_ref), (tokens_near_ref, tokens_grad_ref), (keys_near_ref, keys_grad_ref)]
         )
     ]
-    for side in range(2):
-        total = keys_parts_ref[side * slots : (side + 1) * slots, 0, :]
-        for first in range((side + 2) * slots, keys_parts_ref.shape[0], 2 * slots):
-            total = total + keys_parts_ref[first : first + slots, 0, :]
-        keys_near_ref[:, side * half : (side + 1) * half] = jnp.sum(total, axis=0, keepdims=True)
-    copies[2].start()
     combine = jnp.transpose(factors_ref[:slots, :]).astype(jnp.bfloat16)
     layer_near_ref[...] = dot(combine, slot_out_ref[...], 1, 0).astype(jnp.bfloat16)
     copies[0].start()
@@ -382,6 +373,12 @@
     ).astype(jnp.bfloat16)
     tokens_near_ref[...] = dot(others, rows, 1, 0).astype(jnp.bfloat16)
     copies[1].start()
+    for side in range(2):
+        total = keys_parts_ref[side * slots : (side + 1) * slots, 0, :]
+        for first in range((side + 2) * slots, keys_parts_ref.shape[0], 2 * slots):
+            total = total + keys_parts_ref[first : first + slots, 0, :]
+        keys_near_ref[:, side * half : (side + 1) * half] = jnp.sum(total, axis=0, keepdims=True)
+    copies[2].start()
     for copy in copies:
         copy.wait()
 
@@ -399,15 +396,14 @@
     f32, bf16 = jnp.float32, jnp.bfloat16
     shape = jax.ShapeDtypeStruct
 
-    key_rows = padded(width // LANES, 16)
     key_message, tokens_near, cotangent_near = call(
         keys_kernel,
         (
-            shape((exp_size, key_rows, LANES), bf16),
+            shape((exp_size, 2, half), bf16),
             shape(tokens.shape, bf16),
             shape(cotangent.shape, bf16),
         ),
-        [pltpu.VMEM((1, width), bf16), pltpu.VMEM((key_rows, LANES), f32), pltpu.SemaphoreType.DMA((3,))],
+        [pltpu.VMEM((1, width), bf16), pltpu.VMEM((2, half), f32), pltpu.SemaphoreType.DMA((3,))],
         [slot_keys.T, tokens, cotangent],
         far=3,
     )
@@ -428,7 +424,7 @@
             shape((slots, width), bf16),
         ),
         [
-            pltpu.VMEM((slots, key_rows, LANES), f32),
+            pltpu.VMEM((slots, 2, half), f32),
             pltpu.VMEM((slots, sum_rows, LANES), f32),
         ],
         [keys, tokens_near, tokens_other, cotangent_near, cotangent_other],

time: 53 us -> 52.9 us (level)
  no operation moved by 1% of the time
where the time goes in v10:
time: 52.9 us; the launch traced here: 52.5 us
  blocking collectives  33.5 us (63%)
  Pallas kernels  9.89 us (19%)
  waiting for transfers between devices  4.63 us (9%)
  starting transfers between devices  3.86 us (7%)
  between operations  0.68 us (1%)
    all_to_all x1, blocking collectives, local(): keys = lax.all_to_all(key_message, 'exp', 0, 0, tiled=True)  13.6 us
    all_to_all x1, blocking collectives, local(): keys_parts = lax.all_to_all(message, both, 0, 0, tiled=True)  10.3 us
    pallas_call x6, Pallas kernels, call(): pl.pallas_call(kernel, out_shape=out_shape, in_specs=[pl.BlockSpec(memory...  9.89 us
    all_to_all x1, blocking collectives, local(): parts = lax.all_to_all(message, both, 0, 0, tiled=True)  9.51 us
    all_to_all x1, waiting for transfers between devices, local(): gathered = lax.all_to_all(message, both, 0, 0, tiled=True)  3.41 us
    all_to_all x1, starting transfers between devices, local(): gathered = lax.all_to_all(message, both, 0, 0, tiled=True)  2.58 us
  transfers between devices with their start and end apart: 6, of which 3 were waited for; matrix products, arithmetic and copies ran while one was open for 0% of the time, Pallas kernels for 10%

profile of v10, /device:TPU:0, one launch (start us, length us, event | category | flops | bytes accessed | tf_op | source)
XLA Modules:
  0.0 52.5 jit_solution(15959165341808208421)
XLA Ops:
  0.6 0.5 collective-permute-start
  1.1 0.1 collective-permute-start.1
  1.2 1.1 %shard_map.92 = (bf16[8,2,640]{2,1,0:T(2,128)(2,1)S(1)}, bf16[128,1280]{1,0:T(8,128)(2,1)S(1)}, bf16[128,1280]{1,0:T(8,128)(2,1)S(1)}) custom-call(bf16[1,1280]{1,0:T(2,128)(2,1)} %bitcast.6, bf16[128,1280]{1,0:T(8,128)(2,1)} %tokens_in_ref.1, bf16[128,1280]{1,0:T(8,128)(2,1)} %cotangent_in_ref.1), custom_call_target="tpu_custom_call" | custom-call | tf_op jit(solution)/shard_map/pallas_call | solution.py:67
  2.3 13.6 %all_to_all.20.keys_ref = bf16[8,2,640]{2,1,0:T(2,128)(2,1)S(1)} all-to-all(bf16[8,2,640]{2,1,0:T(2,128)(2,1)S(1)} %get-tuple-element.33), channel_id=1, replica_groups=mesh['seq'=4,'exp'=8] {'exp'}, dimensions={0} | all-to-all | bytes 40960 | tf_op jit(solution)/shard_map/all_to_all | solution.py:412
  16.0 0.0 collective-permute-done.tokens_other_ref
  16.0 0.0 collective-permute-done.1.cotangent_other_ref
  16.0 0.0 collective-permute-start.2
  16.0 0.5 collective-permute-start.3
  16.5 0.6 %shard_map.93 = (bf16[32,16,128]{2,1,0:T(8,128)(2,1)S(1)}, f32[8,256]{1,0:T(8,128)S(1)}, f32[8,256]{1,0:T(8,128)S(1)}, bf16[8,1280]{1,0:T(8,128)(2,1)S(1)}) custom-call(bf16[8,2,640]{2,1,0:T(2,128)(2,1)S(1)} %all_to_all.20.keys_ref, bf16[128,1280]{1,0:T(8,128)(2,1)S(1)} %get-tuple-element.35.tokens_ref, ...), custom_call_target="tpu_custom_call" | custom-call | tf_op jit(solution)/shard_map/pallas_call | solution.py:67
  17.1 9.5 %all_to_all.21.parts_ref = bf16[32,16,128]{2,1,0:T(8,128)(2,1)S(1)} all-to-all(bf16[32,16,128]{2,1,0:T(8,128)(2,1)S(1)} %get-tuple-element.39), channel_id=1, replica_groups=mesh['seq'=4,'exp'=8] {'seq','exp'}, dimensions={0} | all-to-all | bytes 262144 | tf_op jit(solution)/shard_map/all_to_all | solution.py:432
  26.6 0.0 collective-permute-done.2
  26.6 0.2 collective-permute-done.3
  26.7 2.9 %shard_map.94 = (bf16[32,2,1408]{2,1,0:T(2,128)(2,1)}, bf16[1,1280]{1,0:T(2,128)(2,1)S(1)}, bf16[1,1280]{1,0:T(2,128)(2,1)S(1)}, bf16[2,1280]{1,0:T(2,128)(2,1)S(1)}) custom-call(bf16[32,16,128]{2,1,0:T(8,128)(2,1)S(1)} %all_to_all.21.parts_ref, bf16[1280,1280]{1,0:T(8,128)(2,1)S(1)} %bitcast.4, bf16[1280,1280]{1,0:T(8,128)(2,1)S(1)} %bitcast.5), custom_call_target="tpu_custom_call" | custom-call | tf_op jit(solution)/shard_map/pallas_call | solution.py:67
  29.6 2.6 %all-to-all-start.2 = ((bf16[32,2,1408]{2,1,0:T(2,128)(2,1)}), bf16[32,2,1408]{2,1,0:T(2,128)(2,1)S(1)}, u32[]{:S(2)}, u32[]{:S(2)}) async-start(bf16[32,2,1408]{2,1,0:T(2,128)(2,1)} %get-tuple-element.42), calls=%async_computation.2 | async-start | bytes 360448 | tf_op jit(solution)/shard_map/all_to_all | solution.py:445
  32.2 0.2 collective-permute-start.4
  32.4 1.1 %collective-permute-done.4.hidden_rows_ref = bf16[2,1280]{1,0:T(2,128)(2,1)S(1)} collective-permute-done((bf16[2,1280]{1,0:T(2,128)(2,1)S(1)}, bf16[2,1280]{1,0:T(2,128)(2,1)S(1)}, u32[]{:S(2)}, u32[]{:S(2)}) %collective-permute-start.4) | collective-permute-done | bytes 5152 | tf_op jit(solution)/shard_map/ppermute | solution.py:446
  33.4 3.4 %shard_map.95 = (bf16[1,1280,1280]{2,1,0:T(8,128)(2,1)}, bf16[1,1280,1280]{2,1,0:T(8,128)(2,1)}) custom-call(bf16[2,1280]{1,0:T(2,128)(2,1)S(1)} %collective-permute-done.4.hidden_rows_ref, bf16[1,1280]{1,0:T(2,128)(2,1)S(1)} %get-tuple-element.44.slot_in_ref, bf16[1,1280]{1,0:T(2,128)(2,1)S(1)} %get-tuple-element.45.slot_out_grad_ref), custom_call_target="tpu_custom_call" | custom-call | tf_op jit(solution)/shard_map/pallas_call | solution.py:67
  36.8 3.4 %all-to-all-done.2.parts_ref = bf16[32,2,1408]{2,1,0:T(2,128)(2,1)S(1)} async-done(((bf16[32,2,1408]{2,1,0:T(2,128)(2,1)}), bf16[32,2,1408]{2,1,0:T(2,128)(2,1)S(1)}, u32[]{:S(2)}, u32[]{:S(2)}) %all-to-all-start.2) | async-done | bytes 180256 | tf_op jit(solution)/shard_map/all_to_all | solution.py:445
  40.2 0.8 %shard_map.96 = (f32[32,1,640]{2,1,0:T(1,128)S(1)}, bf16[8,1280]{1,0:T(8,128)(2,1)S(1)}, bf16[8,1280]{1,0:T(8,128)(2,1)S(1)}, f32[24,128]{1,0:T(8,128)S(1)}) custom-call(bf16[32,2,1408]{2,1,0:T(2,128)(2,1)S(1)} %all-to-all-done.2.parts_ref, f32[8,256]{1,0:T(8,128)S(1)} %get-tuple-element.49.logits_ref, f32[8,256]{1,0:T(8,128)S(1)} %get-tuple-element.50.comb_ref, ...), custom_call_target="tpu_custom_call" | custom-call | tf_op jit(solution)/shard_map/pallas_call | solution.py:67
  41.0 10.3 %all_to_all.22.keys_parts_ref = f32[32,1,640]{2,1,0:T(1,128)S(1)} all-to-all(f32[32,1,640]{2,1,0:T(1,128)S(1)} %get-tuple-element.51), channel_id=1, replica_groups=mesh['seq'=4,'exp'=8] {'seq','exp'}, dimensions={0} | all-to-all | bytes 163840 | tf_op jit(solution)/shard_map/all_to_all | solution.py:470
  51.4 1.2 %shard_map.97 = (bf16[128,1280]{1,0:T(8,128)(2,1)}, bf16[128,1280]{1,0:T(8,128)(2,1)}, f32[1,1280]{1,0:T(1,128)}) custom-call(f32[32,1,640]{2,1,0:T(1,128)S(1)} %all_to_all.22.keys_parts_ref, f32[24,128]{1,0:T(8,128)S(1)} %get-tuple-element.52.factors_ref, bf16[8,1280]{1,0:T(8,128)(2,1)S(1)} %get-tuple-element.53.slot_out_ref, ...), custom_call_target="tpu_custom_call" | custom-call | tf_op jit(solution)/shard_map/pallas_call | solution.py:67
Async XLA Ops:
  0.6 15.4 %collective-permute-start = (bf16[128,1280]{1,0:T(8,128)(2,1)}, bf16[128,1280]{1,0:T(8,128)(2,1)S(1)}, u32[]{:S(2)}, u32[]{:S(2)}) collective-permute-start(bf16[128,1280]{1,0:T(8,128)(2,1)} %tokens_in_ref.1), channel_id=1, source_target_pairs={{0,8},{8,0},{16,24},{24,16},{1,9},{9,1},{17,25},{25,17},{2,10},{10... | collective-permute-start | bytes 983048 | tf_op jit(solution)/shard_map/ppermute | solution.py:410
  1.1 14.8 %collective-permute-start.1 = (bf16[128,1280]{1,0:T(8,128)(2,1)}, bf16[128,1280]{1,0:T(8,128)(2,1)S(1)}, u32[]{:S(2)}, u32[]{:S(2)}) collective-permute-start(bf16[128,1280]{1,0:T(8,128)(2,1)} %cotangent_in_ref.1), channel_id=1, source_target_pairs={{0,8},{8,0},{16,24},{24,16},{1,9},{9,1},{17,25},{25,17},{2,10},{10... | collective-permute-start | bytes 983048 | tf_op jit(solution)/shard_map/ppermute | solution.py:411
  16.0 10.6 %collective-permute-start.2 = (bf16[1,1280,1280]{2,1,0:T(8,128)(2,1)}, bf16[1,1280,1280]{2,1,0:T(8,128)(2,1)S(1)}, u32[]{:S(2)}, u32[]{:S(2)}) collective-permute-start(bf16[1,1280,1280]{2,1,0:T(8,128)(2,1)} %param.7), channel_id=1, source_target_pairs={{0,8},{8,0},{16,24},{24,16},{1,9},{9,1},{17,25},{25,17},{2,10},{10... | collective-permute-start | bytes 9830408 | tf_op jit(solution)/shard_map/ppermute | solution.py:414
  16.0 10.7 %collective-permute-start.3 = (bf16[1,1280,1280]{2,1,0:T(8,128)(2,1)}, bf16[1,1280,1280]{2,1,0:T(8,128)(2,1)S(1)}, u32[]{:S(2)}, u32[]{:S(2)}) collective-permute-start(bf16[1,1280,1280]{2,1,0:T(8,128)(2,1)} %param.8), channel_id=1, source_target_pairs={{0,8},{8,0},{16,24},{24,16},{1,9},{9,1},{17,25},{25,17},{2,10},{10... | collective-permute-start | bytes 9830408 | tf_op jit(solution)/shard_map/ppermute | solution.py:415
  29.6 10.6 %all-to-all-start.2 = ((bf16[32,2,1408]{2,1,0:T(2,128)(2,1)}), bf16[32,2,1408]{2,1,0:T(2,128)(2,1)S(1)}, u32[]{:S(2)}, u32[]{:S(2)}) async-start(bf16[32,2,1408]{2,1,0:T(2,128)(2,1)} %get-tuple-element.42), calls=%async_computation.2 | async-start | bytes 360448 | tf_op jit(solution)/shard_map/all_to_all | solution.py:445
  32.2 1.2 %collective-permute-start.4 = (bf16[2,1280]{1,0:T(2,128)(2,1)S(1)}, bf16[2,1280]{1,0:T(2,128)(2,1)S(1)}, u32[]{:S(2)}, u32[]{:S(2)}) collective-permute-start(bf16[2,1280]{1,0:T(2,128)(2,1)S(1)} %get-tuple-element.43), channel_id=1, source_target_pairs={{0,8},{8,0},{16,24},{24,16},{1,9},{9,1},{17,25},{25,17},{2,10},{10... | collective-permute-start | bytes 15368 | tf_op jit(solution)/shard_map/ppermute | solution.py:446

commit v11 on v10

--- a/solution.py
+++ b/solution.py
@@ -364,6 +364,12 @@
             [(layer_near_ref, layer_out_ref), (tokens_near_ref, tokens_grad_ref), (keys_near_ref, keys_grad_ref)]
         )
     ]
+    for side in range(2):
+        total = keys_parts_ref[side * slots : (side + 1) * slots, 0, :]
+        for first in range((side + 2) * slots, keys_parts_ref.shape[0], 2 * slots):
+            total = total + keys_parts_ref[first : first + slots, 0, :]
+        keys_near_ref[:, side * half : (side + 1) * half] = jnp.sum(total, axis=0, keepdims=True)
+    copies[2].start()
     combine = jnp.transpose(factors_ref[:slots, :]).astype(jnp.bfloat16)
     layer_near_ref[...] = dot(combine, slot_out_ref[...], 1, 0).astype(jnp.bfloat16)
     copies[0].start()
@@ -373,12 +379,6 @@
     ).astype(jnp.bfloat16)
     tokens_near_ref[...] = dot(others, rows, 1, 0).astype(jnp.bfloat16)
     copies[1].start()
-    for side in range(2):
-        total = keys_parts_ref[side * slots : (side + 1) * slots, 0, :]
-        for first in range((side + 2) * slots, keys_parts_ref.shape[0], 2 * slots):
-            total = total + keys_parts_ref[first : first + slots, 0, :]
-        keys_near_ref[:, side * half : (side + 1) * half] = jnp.sum(total, axis=0, keepdims=True)
-    copies[2].start()
     for copy in copies:
         copy.wait()
 

time: 52.9 us -> 52.9 us (level)
  no operation moved by 1% of the time
where the time goes in v11:
time: 52.9 us; the launch traced here: 52.6 us
  blocking collectives  33.5 us (63%)
  Pallas kernels  9.91 us (19%)
  waiting for transfers between devices  4.63 us (9%)
  starting transfers between devices  3.86 us (7%)
  between operations  0.68 us (1%)
    all_to_all x1, blocking collectives, local(): keys = lax.all_to_all(key_message, 'exp', 0, 0, tiled=True)  13.6 us
    all_to_all x1, blocking collectives, local(): keys_parts = lax.all_to_all(message, both, 0, 0, tiled=True)  10.3 us
    pallas_call x6, Pallas kernels, call(): pl.pallas_call(kernel, out_shape=out_shape, in_specs=[pl.BlockSpec(memory...  9.91 us
    all_to_all x1, blocking collectives, local(): parts = lax.all_to_all(message, both, 0, 0, tiled=True)  9.51 us
    all_to_all x1, waiting for transfers between devices, local(): gathered = lax.all_to_all(message, both, 0, 0, tiled=True)  3.41 us
    all_to_all x1, starting transfers between devices, local(): gathered = lax.all_to_all(message, both, 0, 0, tiled=True)  2.58 us
  transfers between devices with their start and end apart: 6, of which 3 were waited for; matrix products, arithmetic and copies ran while one was open for 0% of the time, Pallas kernels for 10%

profile of v11, /device:TPU:0, one launch (start us, length us, event | category | flops | bytes accessed | tf_op | source)
XLA Modules:
  0.0 52.6 jit_solution(11040635255687710607)
XLA Ops:
  0.6 0.5 collective-permute-start
  1.1 0.1 collective-permute-start.1
  1.2 1.1 %shard_map.92 = (bf16[8,2,640]{2,1,0:T(2,128)(2,1)S(1)}, bf16[128,1280]{1,0:T(8,128)(2,1)S(1)}, bf16[128,1280]{1,0:T(8,128)(2,1)S(1)}) custom-call(bf16[1,1280]{1,0:T(2,128)(2,1)} %bitcast.6, bf16[128,1280]{1,0:T(8,128)(2,1)} %tokens_in_ref.1, bf16[128,1280]{1,0:T(8,128)(2,1)} %cotangent_in_ref.1), custom_call_target="tpu_custom_call" | custom-call | tf_op jit(solution)/shard_map/pallas_call | solution.py:67
  2.3 13.6 %all_to_all.20.keys_ref = bf16[8,2,640]{2,1,0:T(2,128)(2,1)S(1)} all-to-all(bf16[8,2,640]{2,1,0:T(2,128)(2,1)S(1)} %get-tuple-element.33), channel_id=1, replica_groups=mesh['seq'=4,'exp'=8] {'exp'}, dimensions={0} | all-to-all | bytes 40960 | tf_op jit(solution)/shard_map/all_to_all | solution.py:412
  16.0 0.0 collective-permute-done.tokens_other_ref
  16.0 0.0 collective-permute-done.1.cotangent_other_ref
  16.0 0.0 collective-permute-start.2
  16.0 0.5 collective-permute-start.3
  16.5 0.6 %shard_map.93 = (bf16[32,16,128]{2,1,0:T(8,128)(2,1)S(1)}, f32[8,256]{1,0:T(8,128)S(1)}, f32[8,256]{1,0:T(8,128)S(1)}, bf16[8,1280]{1,0:T(8,128)(2,1)S(1)}) custom-call(bf16[8,2,640]{2,1,0:T(2,128)(2,1)S(1)} %all_to_all.20.keys_ref, bf16[128,1280]{1,0:T(8,128)(2,1)S(1)} %get-tuple-element.35.tokens_ref, ...), custom_call_target="tpu_custom_call" | custom-call | tf_op jit(solution)/shard_map/pallas_call | solution.py:67
  17.1 9.5 %all_to_all.21.parts_ref = bf16[32,16,128]{2,1,0:T(8,128)(2,1)S(1)} all-to-all(bf16[32,16,128]{2,1,0:T(8,128)(2,1)S(1)} %get-tuple-element.39), channel_id=1, replica_groups=mesh['seq'=4,'exp'=8] {'seq','exp'}, dimensions={0} | all-to-all | bytes 262144 | tf_op jit(solution)/shard_map/all_to_all | solution.py:432
  26.6 0.0 collective-permute-done.2
  26.6 0.2 collective-permute-done.3
  26.7 2.9 %shard_map.94 = (bf16[32,2,1408]{2,1,0:T(2,128)(2,1)}, bf16[1,1280]{1,0:T(2,128)(2,1)S(1)}, bf16[1,1280]{1,0:T(2,128)(2,1)S(1)}, bf16[2,1280]{1,0:T(2,128)(2,1)S(1)}) custom-call(bf16[32,16,128]{2,1,0:T(8,128)(2,1)S(1)} %all_to_all.21.parts_ref, bf16[1280,1280]{1,0:T(8,128)(2,1)S(1)} %bitcast.4, bf16[1280,1280]{1,0:T(8,128)(2,1)S(1)} %bitcast.5), custom_call_target="tpu_custom_call" | custom-call | tf_op jit(solution)/shard_map/pallas_call | solution.py:67
  29.6 2.6 %all-to-all-start.2 = ((bf16[32,2,1408]{2,1,0:T(2,128)(2,1)}), bf16[32,2,1408]{2,1,0:T(2,128)(2,1)S(1)}, u32[]{:S(2)}, u32[]{:S(2)}) async-start(bf16[32,2,1408]{2,1,0:T(2,128)(2,1)} %get-tuple-element.42), calls=%async_computation.2 | async-start | bytes 360448 | tf_op jit(solution)/shard_map/all_to_all | solution.py:445
  32.2 0.2 collective-permute-start.4
  32.4 1.1 %collective-permute-done.4.hidden_rows_ref = bf16[2,1280]{1,0:T(2,128)(2,1)S(1)} collective-permute-done((bf16[2,1280]{1,0:T(2,128)(2,1)S(1)}, bf16[2,1280]{1,0:T(2,128)(2,1)S(1)}, u32[]{:S(2)}, u32[]{:S(2)}) %collective-permute-start.4) | collective-permute-done | bytes 5152 | tf_op jit(solution)/shard_map/ppermute | solution.py:446
  33.4 3.4 %shard_map.95 = (bf16[1,1280,1280]{2,1,0:T(8,128)(2,1)}, bf16[1,1280,1280]{2,1,0:T(8,128)(2,1)}) custom-call(bf16[2,1280]{1,0:T(2,128)(2,1)S(1)} %collective-permute-done.4.hidden_rows_ref, bf16[1,1280]{1,0:T(2,128)(2,1)S(1)} %get-tuple-element.44.slot_in_ref, bf16[1,1280]{1,0:T(2,128)(2,1)S(1)} %get-tuple-element.45.slot_out_grad_ref), custom_call_target="tpu_custom_call" | custom-call | tf_op jit(solution)/shard_map/pallas_call | solution.py:67
  36.8 3.4 %all-to-all-done.2.parts_ref = bf16[32,2,1408]{2,1,0:T(2,128)(2,1)S(1)} async-done(((bf16[32,2,1408]{2,1,0:T(2,128)(2,1)}), bf16[32,2,1408]{2,1,0:T(2,128)(2,1)S(1)}, u32[]{:S(2)}, u32[]{:S(2)}) %all-to-all-start.2) | async-done | bytes 180256 | tf_op jit(solution)/shard_map/all_to_all | solution.py:445
  40.2 0.8 %shard_map.96 = (f32[32,1,640]{2,1,0:T(1,128)S(1)}, bf16[8,1280]{1,0:T(8,128)(2,1)S(1)}, bf16[8,1280]{1,0:T(8,128)(2,1)S(1)}, f32[24,128]{1,0:T(8,128)S(1)}) custom-call(bf16[32,2,1408]{2,1,0:T(2,128)(2,1)S(1)} %all-to-all-done.2.parts_ref, f32[8,256]{1,0:T(8,128)S(1)} %get-tuple-element.49.logits_ref, f32[8,256]{1,0:T(8,128)S(1)} %get-tuple-element.50.comb_ref, ...), custom_call_target="tpu_custom_call" | custom-call | tf_op jit(solution)/shard_map/pallas_call | solution.py:67
  41.0 10.3 %all_to_all.22.keys_parts_ref = f32[32,1,640]{2,1,0:T(1,128)S(1)} all-to-all(f32[32,1,640]{2,1,0:T(1,128)S(1)} %get-tuple-element.51), channel_id=1, replica_groups=mesh['seq'=4,'exp'=8] {'seq','exp'}, dimensions={0} | all-to-all | bytes 163840 | tf_op jit(solution)/shard_map/all_to_all | solution.py:470
  51.4 1.2 %shard_map.97 = (bf16[128,1280]{1,0:T(8,128)(2,1)}, bf16[128,1280]{1,0:T(8,128)(2,1)}, f32[1,1280]{1,0:T(1,128)}) custom-call(f32[32,1,640]{2,1,0:T(1,128)S(1)} %all_to_all.22.keys_parts_ref, f32[24,128]{1,0:T(8,128)S(1)} %get-tuple-element.52.factors_ref, bf16[8,1280]{1,0:T(8,128)(2,1)S(1)} %get-tuple-element.53.slot_out_ref, ...), custom_call_target="tpu_custom_call" | custom-call | tf_op jit(solution)/shard_map/pallas_call | solution.py:67
Async XLA Ops:
  0.6 15.4 %collective-permute-start = (bf16[128,1280]{1,0:T(8,128)(2,1)}, bf16[128,1280]{1,0:T(8,128)(2,1)S(1)}, u32[]{:S(2)}, u32[]{:S(2)}) collective-permute-start(bf16[128,1280]{1,0:T(8,128)(2,1)} %tokens_in_ref.1), channel_id=1, source_target_pairs={{0,8},{8,0},{16,24},{24,16},{1,9},{9,1},{17,25},{25,17},{2,10},{10... | collective-permute-start | bytes 983048 | tf_op jit(solution)/shard_map/ppermute | solution.py:410
  1.1 14.8 %collective-permute-start.1 = (bf16[128,1280]{1,0:T(8,128)(2,1)}, bf16[128,1280]{1,0:T(8,128)(2,1)S(1)}, u32[]{:S(2)}, u32[]{:S(2)}) collective-permute-start(bf16[128,1280]{1,0:T(8,128)(2,1)} %cotangent_in_ref.1), channel_id=1, source_target_pairs={{0,8},{8,0},{16,24},{24,16},{1,9},{9,1},{17,25},{25,17},{2,10},{10... | collective-permute-start | bytes 983048 | tf_op jit(solution)/shard_map/ppermute | solution.py:411
  16.0 10.6 %collective-permute-start.2 = (bf16[1,1280,1280]{2,1,0:T(8,128)(2,1)}, bf16[1,1280,1280]{2,1,0:T(8,128)(2,1)S(1)}, u32[]{:S(2)}, u32[]{:S(2)}) collective-permute-start(bf16[1,1280,1280]{2,1,0:T(8,128)(2,1)} %param.7), channel_id=1, source_target_pairs={{0,8},{8,0},{16,24},{24,16},{1,9},{9,1},{17,25},{25,17},{2,10},{10... | collective-permute-start | bytes 9830408 | tf_op jit(solution)/shard_map/ppermute | solution.py:414
  16.0 10.7 %collective-permute-start.3 = (bf16[1,1280,1280]{2,1,0:T(8,128)(2,1)}, bf16[1,1280,1280]{2,1,0:T(8,128)(2,1)S(1)}, u32[]{:S(2)}, u32[]{:S(2)}) collective-permute-start(bf16[1,1280,1280]{2,1,0:T(8,128)(2,1)} %param.8), channel_id=1, source_target_pairs={{0,8},{8,0},{16,24},{24,16},{1,9},{9,1},{17,25},{25,17},{2,10},{10... | collective-permute-start | bytes 9830408 | tf_op jit(solution)/shard_map/ppermute | solution.py:415
  29.6 10.6 %all-to-all-start.2 = ((bf16[32,2,1408]{2,1,0:T(2,128)(2,1)}), bf16[32,2,1408]{2,1,0:T(2,128)(2,1)S(1)}, u32[]{:S(2)}, u32[]{:S(2)}) async-start(bf16[32,2,1408]{2,1,0:T(2,128)(2,1)} %get-tuple-element.42), calls=%async_computation.2 | async-start | bytes 360448 | tf_op jit(solution)/shard_map/all_to_all | solution.py:445
  32.2 1.2 %collective-permute-start.4 = (bf16[2,1280]{1,0:T(2,128)(2,1)S(1)}, bf16[2,1280]{1,0:T(2,128)(2,1)S(1)}, u32[]{:S(2)}, u32[]{:S(2)}) collective-permute-start(bf16[2,1280]{1,0:T(2,128)(2,1)S(1)} %get-tuple-element.43), channel_id=1, source_target_pairs={{0,8},{8,0},{16,24},{24,16},{1,9},{9,1},{17,25},{25,17},{2,10},{10... | collective-permute-start | bytes 15368 | tf_op jit(solution)/shard_map/ppermute | solution.py:446
